TPU v7x, 512 devices: a whole 4x4x16 slice. The times are simulated.
512 devices in a mesh: expert: 128 (over z, x, core), group: 4 (over y).
Axes of the slice: x: 4, y: 4, z: 16, core: 2. Of those that a mesh axis runs over, the one named last changes fastest.
Arguments:
- layer_in: bfloat16 [4096, 4096], P(('expert', 'group')), may hold values from -3 to 3
- norm_gain: bfloat16 [4096], replicated, may hold values from 0.25 to 1.75
- route_ids: int32 [4096, 8], P('expert'), may hold values from 0 to 127, all different within a row; in each aligned block of 32 rows (0 to 31, 32 to 63, ...) at most 4 rows name the same one
- route_logits: float32 [4096, 8], P('expert'), may hold values from -6 to 6
- gate_proj: bfloat16 [128, 768, 4096], P('expert', 'group'), may hold values from -0.09375 to 0.09375
- up_proj: bfloat16 [128, 768, 4096], P('expert', 'group'), may hold values from -0.09375 to 0.09375
- down_proj: bfloat16 [128, 768, 4096], P('expert', 'group'), may hold values from -0.21875 to 0.21875
- low_feature: bfloat16 [4096, 4096], P(('expert', 'group')), may hold values from -6 to 6
- mid_feature: bfloat16 [4096, 4096], P(('expert', 'group')), may hold values from -6 to 6
- accepted_node: int32 [512], P('expert'), may hold values from 0 to 7
- join_weight: bfloat16 [3, 4096, 4096], P(None, 'expert', 'group'), may hold values from -0.0546875 to 0.0546875
Outputs:
- layer_out: bfloat16 [4096, 4096], P(('expert', 'group'))
- joined_rows: bfloat16 [512, 4096], P('expert', 'group')
Inputs may be any that keep to these rules, and one draw needn't show every extreme that they name: `route_ids`: each row names 8 different experts; in each aligned block of 32 rows (the rows of one index of expert) no expert is named by more than 4 rows, and some block reaches 4.
All inputs are finite; a program needn't handle non-finite values.
Results may differ from a plain program's by a relative error of at most 0.012.
Values may be sent and summed in bfloat16 or wider, within the bound.
No kernel may reach another device: no remote copies, remote signals or barrier semaphores. Data moves between devices by JAX's collectives and lax.ppermute only.
A program may use at most 64 MiB of HBM per device.

v0:
```python
import jax
import jax.numpy as jnp
from jax import lax
from jax.sharding import PartitionSpec as P

EPSILON = 1e-06


def rms_norm(values, norm_gain):
    widened = values.astype(jnp.float32)
    inverse_rms = lax.rsqrt(jnp.mean(widened * widened, axis=-1, keepdims=True) + EPSILON)
    return (widened * inverse_rms * norm_gain.astype(jnp.float32)).astype(jnp.bfloat16)


def route_weights(route_logits):
    exponent = jnp.exp(route_logits)
    return (exponent / jnp.sum(exponent, axis=-1, keepdims=True)).astype(jnp.bfloat16)


def slot_places(route_ids, experts, capacity):
    flat_ids = route_ids.reshape(-1)
    columns = jnp.arange(experts, dtype=jnp.int32)
    onehot = (flat_ids[:, None] == columns[None, :]).astype(jnp.int32)
    before = jnp.cumsum(onehot, axis=0) - onehot
    return flat_ids * capacity + jnp.sum(before * onehot, axis=1)


def pick_rows(features, nodes, tree_size):
    amount = nodes.shape[0]
    shaped = features.reshape(amount, tree_size, features.shape[-1])
    taken = jnp.take_along_axis(shaped, nodes[:, None, None], axis=1)
    return taken[:, 0]


def project_rows(rows, weight):
    return lax.dot_general(
        rows, weight, (((1,), (1,)), ((), ())), preferred_element_type=jnp.float32
    )


def on_device(
    layer_in,
    norm_gain,
    route_ids,
    route_logits,
    gate_proj,
    up_proj,
    down_proj,
    low_feature,
    mid_feature,
    accepted_node,
    join_weight,
):
    experts = lax.axis_size("expert")
    groups = lax.axis_size("group")
    rows_dev, model_width = layer_in.shape
    block_size, top_count = route_ids.shape
    capacity = min(2 * block_size * top_count // experts, block_size)
    trees_dev = accepted_node.shape[0] // groups
    tree_size = rows_dev // trees_dev
    group_index = lax.axis_index("group")
    own_nodes = lax.dynamic_slice_in_dim(accepted_node, group_index * trees_dev, trees_dev, 0)
    low_rows = pick_rows(low_feature, own_nodes, tree_size)
    mid_rows = pick_rows(mid_feature, own_nodes, tree_size)
    block_in, low_block, mid_block = (
        lax.all_gather(layer_in, "group", axis=0, tiled=True),
        lax.all_gather(low_rows, "group", axis=0, tiled=True),
        lax.all_gather(mid_rows, "group", axis=0, tiled=True),
    )
    normed = rms_norm(block_in, norm_gain)
    weights = route_weights(route_logits)
    places = slot_places(route_ids, experts, capacity)
    slot_ids = jnp.arange(experts * capacity, dtype=jnp.int32)
    matches = (
        (places[:, None] == slot_ids[None, :])
        .astype(jnp.float32)
        .reshape(block_size, top_count, experts * capacity)
    )
    dispatch_table = jnp.sum(matches, axis=1).astype(jnp.bfloat16)
    combine_table = jnp.sum(matches * weights.astype(jnp.float32)[:, :, None], axis=1).astype(
        jnp.bfloat16
    )
    outgoing = jnp.einsum("rs,rd->sd", dispatch_table, normed, preferred_element_type=jnp.float32)
    outgoing = outgoing.astype(jnp.bfloat16).reshape(experts, capacity, model_width)
    received = lax.all_to_all(outgoing, "expert", split_axis=0, concat_axis=0, tiled=True)
    amount = received.shape[1]
    flat_rows = received.reshape(experts * amount, model_width)
    gate_act = project_rows(flat_rows, gate_proj[0])
    up_act = project_rows(flat_rows, up_proj[0])
    hidden = (jax.nn.silu(gate_act) * up_act).astype(jnp.bfloat16)
    partial_value = jnp.dot(hidden, down_proj[0], preferred_element_type=jnp.float32).astype(
        jnp.bfloat16
    )
    partials = partial_value.reshape(experts, amount, model_width)
    returned = lax.all_to_all(partials, "expert", split_axis=0, concat_axis=0, tiled=True)
    moe_part = jnp.dot(
        combine_table,
        returned.reshape(experts * capacity, model_width),
        preferred_element_type=jnp.float32,
    )
    moe_all = lax.psum(moe_part.astype(jnp.bfloat16), "group").astype(jnp.float32)
    block_out = (block_in.astype(jnp.float32) + moe_all).astype(jnp.bfloat16)
    layer_out = lax.dynamic_slice_in_dim(block_out, group_index * rows_dev, rows_dev, 0)
    high_block = pick_rows(block_out, accepted_node, tree_size)
    features = jnp.stack([low_block, mid_block, high_block], axis=1)
    spread = lax.all_to_all(features, "expert", split_axis=2, concat_axis=0, tiled=True)
    summed = jnp.dot(spread[:, 0], join_weight[0], preferred_element_type=jnp.float32)
    summed = summed + jnp.dot(spread[:, 1], join_weight[1], preferred_element_type=jnp.float32)
    summed = summed + jnp.dot(spread[:, 2], join_weight[2], preferred_element_type=jnp.float32)
    joined_rows = lax.psum_scatter(summed, "expert", scatter_dimension=0, tiled=True).astype(
        jnp.bfloat16
    )
    return (layer_out, joined_rows)


def solution(mesh):
    placed = (
        P(("expert", "group"), None),
        P(),
        P("expert", None),
        P("expert", None),
        P("expert", "group", None),
        P("expert", "group", None),
        P("expert", "group", None),
        P(("expert", "group"), None),
        P(("expert", "group"), None),
        P("expert"),
        P(None, "expert", "group"),
    )
    return jax.shard_map(
        on_device,
        mesh=mesh,
        in_specs=placed,
        out_specs=(P(("expert", "group"), None), P("expert", "group")),
        check_vma=False,
    )
```

profile of v0, /device:TPU:1, one launch (start us, length us, event | category | flops | bytes accessed | tf_op | source)
XLA Modules:
  0.0 1103.0 jit_solution(13870927709493850247)
XLA Ops:
  7.2 0.9 copy.41
  8.1 0.1 eq.43
  8.1 0.1 eq.39
  8.2 10.9 all_gather.9
  19.2 0.7 convert_element_type.62
  19.9 0.2 fusion.13
  20.0 0.7 exponential_reduce_fusion
  20.8 0.7 fusion.41
  21.5 0.1 copy.46
  21.5 0.1 copy.44
  21.6 0.2 fusion.26
  22.0 0.2 fusion.30
  22.1 0.1 reduce_sum.48
  22.2 0.4 select_reduce_fusion
  22.6 3.3 convolution_convert_fusion.1
  25.9 7.2 reshape.121
  33.1 206.4 %all_to_all.28 = bf16[128,4,4096]{2,1,0:T(4,128)(2,1)} all-to-all(bf16[128,4,4096]{2,1,0:T(4,128)(2,1)} %reshape.121), channel_id=1, replica_groups=mesh['expert'=128,'group'=4] {'expert'}, dimensions={0} | all-to-all | bytes 8388608 | tf_op jit(solution)/shard_map/all_to_all | solution.py:85
  239.5 7.0 reshape.122
  246.6 4.5 fusion.3
  251.1 7.5 convolution_convert_fusion
  258.6 7.2 reshape.123
  265.8 13.7 %all-to-all-start.1 = ((bf16[128,4,4096]{2,1,0:T(4,128)(2,1)}), bf16[128,4,4096]{2,1,0:T(4,128)(2,1)}, u32[]{:S(2)}, u32[]{:S(2)}) async-start(bf16[128,4,4096]{2,1,0:T(4,128)(2,1)} %reshape.123), calls=%async_computation.1 | async-start | bytes 8388608 | tf_op jit(solution)/shard_map/all_to_all | solution.py:95
  279.6 0.6 dynamic_slice.7
  282.1 0.9 broadcast_select_fusion
  283.0 0.9 broadcast_select_fusion.1
  283.9 179.1 %all-to-all-done.1 = bf16[128,4,4096]{2,1,0:T(4,128)(2,1)} async-done(((bf16[128,4,4096]{2,1,0:T(4,128)(2,1)}), bf16[128,4,4096]{2,1,0:T(4,128)(2,1)}, u32[]{:S(2)}, u32[]{:S(2)}) %all-to-all-start.1) | async-done | bytes 4194336 | tf_op jit(solution)/shard_map/all_to_all | solution.py:95
  463.0 6.9 reshape.124
  469.9 3.7 convolution_convert_fusion.2
  473.7 9.3 all-gather.1
  483.0 9.2 all-gather
  492.3 1.3 dynamic-slice.7
  494.2 32.0 %all-reduce.4.cloned.1.call-done = bf16[32,4096]{1,0:T(8,128)(2,1)} async-done(((bf16[32,4096]{1,0:T(8,128)(2,1)}), bf16[32,4096]{1,0:T(8,128)(2,1)}) %all-reduce.4.cloned.1.call-update) | async-done | bytes 262160 | tf_op jit(solution)/shard_map/psum | solution.py:101
  526.2 1.0 fusion.16
  527.2 0.7 gather_fusion
  528.0 0.1 bitcast_select_fusion
  528.1 4.8 copy.49
  532.9 7.4 reshape.181
  540.3 18.7 %all-to-all-start.2 = ((bf16[128,2,192]{2,1,0:T(2,128)(2,1)}), bf16[128,2,192]{2,1,0:T(2,128)(2,1)S(1)}, u32[]{:S(2)}, u32[]{:S(2)}) async-start(bf16[128,2,192]{2,1,0:T(2,128)(2,1)} %reshape.181), calls=%async_computation.2 | async-start | bytes 262144 | tf_op jit(solution)/shard_map/all_to_all | solution.py:106
  559.0 0.6 constant_dynamic-slice_fusion
  559.7 15.4 %all-to-all-done.2 = bf16[128,2,192]{2,1,0:T(2,128)(2,1)S(1)} async-done(((bf16[128,2,192]{2,1,0:T(2,128)(2,1)}), bf16[128,2,192]{2,1,0:T(2,128)(2,1)S(1)}, u32[]{:S(2)}, u32[]{:S(2)}) %all-to-all-start.2) | async-done | bytes 98336 | tf_op jit(solution)/shard_map/all_to_all | solution.py:106
  575.1 6.3 reshape.182
  581.5 6.4 copy.55
  587.8 0.3 copy.51
  588.2 0.4 fusion.28
  588.6 0.4 fusion.27
  589.0 1.8 add_add_fusion
  590.7 504.8 %all-reduce.5 = bf16[512,1024]{1,0:T(8,128)(2,1)S(1)} all-reduce(f32[512,1024]{1,0:T(8,128)} %add_add_fusion), channel_id=4, replica_groups=mesh['expert'=128,'group'=4] {'expert'}, use_global_device_ids=true, to_apply=%region_8.10.clone | all-reduce | flops 524288 | bytes 3145728
  1095.5 0.6 dynamic-slice_convert_fusion
  (26 shorter events, 0.4 us)
Async XLA Ops:
  7.2 243.9 %copy-start = (bf16[1,192,4096]{2,1,0:T(8,128)(2,1)S(1)}, bf16[1,192,4096]{2,1,0:T(8,128)(2,1)}, u32[]{:S(2)}) copy-start(bf16[1,192,4096]{2,1,0:T(8,128)(2,1)} %param.19) | copy-start | bytes 4718596
  239.5 7.0 copy-start.2
  265.8 13.8 %copy-start.3 = (s32[4]{0:T(128)S(1)}, s32[4]{0:T(128)}, u32[]{:S(2)}) copy-start(s32[4]{0:T(128)} %param.22) | copy-start | bytes 52
  265.8 197.2 %all-to-all-start.1 = ((bf16[128,4,4096]{2,1,0:T(4,128)(2,1)}), bf16[128,4,4096]{2,1,0:T(4,128)(2,1)}, u32[]{:S(2)}, u32[]{:S(2)}) async-start(bf16[128,4,4096]{2,1,0:T(4,128)(2,1)} %reshape.123), calls=%async_computation.1 | async-start | bytes 8388608 | tf_op jit(solution)/shard_map/all_to_all | solution.py:95
  279.5 246.7 %all-reduce.4.cloned.1.call-start = ((), (), s32[]{:S(2)}) async-start(), calls=%async_computation.3 | async-start | bytes 524288 | tf_op jit(solution)/shard_map/psum | solution.py:101
  540.3 34.8 %all-to-all-start.2 = ((bf16[128,2,192]{2,1,0:T(2,128)(2,1)}), bf16[128,2,192]{2,1,0:T(2,128)(2,1)S(1)}, u32[]{:S(2)}, u32[]{:S(2)}) async-start(bf16[128,2,192]{2,1,0:T(2,128)(2,1)} %reshape.181), calls=%async_computation.2 | async-start | bytes 262144 | tf_op jit(solution)/shard_map/all_to_all | solution.py:106
  559.7 28.5 %copy-start.1 = (bf16[3,32,1024]{2,1,0:T(8,128)(2,1)S(1)}, bf16[3,32,1024]{2,1,0:T(8,128)(2,1)}, u32[]{:S(2)}) copy-start(bf16[3,32,1024]{2,1,0:T(8,128)(2,1)} %param.23) | copy-start | bytes 589828
Sparse Core Ops, SparseCore 0:
  473.8 52.3 all-reduce.3
where the time goes:
time: 1110 us; the launch traced here: 1100 us
  blocking collectives  741 us (67%)
  waiting for transfers between devices  227 us (20%)
  local copies, waits for them, and re-layouts  58.9 us (5%)
  starting transfers between devices  32.5 us (3%)
  matrix products  21.5 us (2%)
  between operations  16.8 us (2%)
    unnamed x1, blocking collectives  505 us
    all_to_all x1, blocking collectives, on_device(): lax.all_to_all(outgoing, 'expert', split_axis=0, concat_axis=0, tiled=True)  206 us
    all_to_all x1, waiting for transfers between devices, on_device(): lax.all_to_all(partials, 'expert', split_axis=0, concat_axis=0, tiled=True)  179 us
    psum x1, waiting for transfers between devices, on_device(): lax.psum(moe_part.astype(jnp.bfloat16), 'group').astype(jnp.float32)  32 us
  transfers between devices with their start and end apart: 3, of which 3 were waited for; matrix products, arithmetic and copies ran while one was open for 0% of the time, Pallas kernels for 0%

commit v1 on v0

v1 whole, which is shorter than its diff:
```python
import jax
import jax.numpy as jnp
from jax import lax
from jax.sharding import Mesh
from jax.sharding import PartitionSpec as P

EPSILON = 1e-06
Z_SIZE = 16
P_SIZE = 8
CAP = 4
EXPERT = ("z", "p")
F32 = jnp.float32
BF16 = jnp.bfloat16


def rms_norm(values, norm_gain):
    widened = values.astype(F32)
    inverse_rms = lax.rsqrt(jnp.mean(widened * widened, axis=-1, keepdims=True) + EPSILON)
    return (widened * inverse_rms * norm_gain.astype(F32)).astype(BF16)


def route_weights(route_logits):
    exponent = jnp.exp(route_logits)
    return (exponent / jnp.sum(exponent, axis=-1, keepdims=True)).astype(BF16)


def slot_places(route_ids, experts):
    flat_ids = route_ids.reshape(-1)
    amount = flat_ids.shape[0]
    onehot = flat_ids[:, None] == jnp.arange(experts, dtype=jnp.int32)[None, :]
    lower = jnp.arange(amount)[:, None] > jnp.arange(amount)[None, :]
    before = jnp.dot(lower.astype(BF16), onehot.astype(BF16), preferred_element_type=F32)
    rank = jnp.sum(jnp.where(onehot, before, 0.0), axis=1).astype(jnp.int32)
    return flat_ids * CAP + rank


def dot_t(rows, weight):
    return lax.dot_general(rows, weight, (((1,), (1,)), ((), ())), preferred_element_type=F32)


def shift_y(array, groups, shift):
    return lax.ppermute(array, "y", [(j, (j + shift) % groups) for j in range(groups)])


def on_device(
    layer_in,
    norm_gain,
    route_ids,
    route_logits,
    gate_proj,
    up_proj,
    down_proj,
    low_feature,
    mid_feature,
    accepted_node,
    join_weight,
):
    groups = lax.axis_size("y")
    experts = Z_SIZE * P_SIZE
    g = lax.axis_index("y")
    rows_dev, width = layer_in.shape
    block, top = route_ids.shape
    part = width // groups
    slots = experts * CAP
    trees = accepted_node.shape[0]

    join_all = lax.all_gather(join_weight, "z", axis=0, tiled=False)
    join_all = join_all.reshape(-1, join_weight.shape[-1])

    stacked = jnp.concatenate([gate_proj, up_proj, down_proj], axis=0)
    pieces = []
    for s in range(groups):
        to = (g + s) % groups
        piece = lax.dynamic_slice_in_dim(stacked, to * part, part, 2)
        pieces.append(shift_y(piece, groups, s) if s else piece)

    normed_own = rms_norm(layer_in, norm_gain)
    both = jnp.stack([normed_own, layer_in], axis=0).reshape(2, rows_dev, groups, part)
    both = lax.all_to_all(both.transpose(2, 0, 1, 3), "y", 0, 0, tiled=True)
    normed = both[:, 0].reshape(block, part)
    block_in = both[:, 1].reshape(block, part)

    weights = route_weights(route_logits)
    places = slot_places(route_ids, experts)
    slot_ids = jnp.arange(slots, dtype=jnp.int32)
    matches = (places[:, None] == slot_ids[None, :]).reshape(block, top, slots)
    dispatch = jnp.any(matches, axis=1).astype(BF16)
    combine = jnp.sum(
        jnp.where(matches, weights.astype(F32)[:, :, None], 0.0), axis=1
    ).astype(BF16)

    outgoing = lax.dot_general(
        dispatch, normed, (((0,), (0,)), ((), ())), preferred_element_type=F32
    ).astype(BF16)
    received = lax.all_to_all(outgoing.reshape(experts, CAP, part), EXPERT, 0, 0, tiled=True)
    rows = received.reshape(slots, part)

    acts = None
    for s in range(groups):
        gate_up = pieces[s][:2].reshape(-1, part)
        product = dot_t(rows, gate_up)
        if s:
            product = shift_y(product.astype(BF16), groups, groups - s).astype(F32)
        acts = product if acts is None else acts + product
    units = acts.shape[1] // 2
    hidden = (jax.nn.silu(acts[:, :units]) * acts[:, units:]).astype(BF16)
    hidden_all = lax.all_gather(hidden, "y", axis=0, tiled=False)

    expert_out = None
    for s in range(groups):
        taken = lax.dynamic_index_in_dim(hidden_all, (g + groups - s) % groups, 0, keepdims=False)
        product = jnp.dot(taken, pieces[s][2], preferred_element_type=F32)
        expert_out = product if expert_out is None else expert_out + product
    expert_out = expert_out.astype(BF16).reshape(experts, CAP, part)
    returned = lax.all_to_all(expert_out, EXPERT, 0, 0, tiled=True)
    moe = jnp.dot(combine, returned.reshape(slots, part), preferred_element_type=F32)
    block_out = (block_in.astype(F32) + moe).astype(BF16)

    own_rows = lax.all_to_all(block_out.reshape(groups, rows_dev, part), "y", 0, 0, tiled=True)
    layer_out = own_rows.transpose(1, 0, 2).reshape(rows_dev, width)

    tree = rows_dev
    high = jnp.take_along_axis(
        block_out.reshape(trees, tree, part), accepted_node[:, None, None], axis=1
    )[:, 0]
    own_node = lax.dynamic_slice_in_dim(accepted_node, g, 1, 0)[0]
    low = lax.dynamic_index_in_dim(low_feature, own_node, 0, keepdims=False)
    mid = lax.dynamic_index_in_dim(mid_feature, own_node, 0, keepdims=False)
    z_part = Z_SIZE // groups
    feat = width // experts
    high = high.reshape(trees, z_part, P_SIZE, feat).transpose(2, 0, 1, 3).reshape(P_SIZE, -1)
    low = low.reshape(Z_SIZE, P_SIZE, feat).transpose(1, 0, 2).reshape(P_SIZE, -1)
    mid = mid.reshape(Z_SIZE, P_SIZE, feat).transpose(1, 0, 2).reshape(P_SIZE, -1)
    payload = jnp.stack([low, mid, high], axis=1)
    payload = jnp.broadcast_to(payload[:, None], (P_SIZE, groups) + payload.shape[1:])
    payload = payload.reshape((P_SIZE * groups,) + payload.shape[2:])
    spread = lax.all_to_all(payload, ("p", "y"), 0, 0, tiled=True)
    low_rows = spread[:, 0].reshape(P_SIZE * trees, Z_SIZE, feat)
    mid_rows = spread[:, 1].reshape(P_SIZE * trees, Z_SIZE, feat)
    high_rows = spread[:, 2].reshape(P_SIZE, groups, trees, z_part, feat)
    high_rows = high_rows.transpose(0, 2, 1, 3, 4).reshape(P_SIZE * trees, Z_SIZE, feat)
    features = jnp.stack([low_rows, mid_rows, high_rows], axis=2).reshape(P_SIZE * trees, -1)
    summed = jnp.dot(features, join_all, preferred_element_type=F32)
    summed = lax.all_to_all(summed.reshape(P_SIZE, trees, -1), "p", 0, 0, tiled=True)
    joined_rows = jnp.sum(summed, axis=0).astype(BF16)
    return (layer_out, joined_rows)


def solution(mesh):
    split = Mesh(mesh.devices.reshape(Z_SIZE, P_SIZE, -1), ("z", "p", "y"))
    every = ("z", "p", "y")
    placed = (
        P(every, None),
        P(),
        P(EXPERT, None),
        P(EXPERT, None),
        P(EXPERT, "y", None),
        P(EXPERT, "y", None),
        P(EXPERT, "y", None),
        P(every, None),
        P(every, None),
        P(EXPERT),
        P(None, EXPERT, "y"),
    )
    return jax.shard_map(
        on_device,
        mesh=split,
        in_specs=placed,
        out_specs=(P(every, None), P(EXPERT, "y")),
        check_vma=False,
    )
```

time: 1110 us -> 279 us (0.25)
  blocking collectives: 741 us -> 26.7 us
  waiting for transfers between devices: 227 us -> 120 us
  starting transfers between devices: 32.5 us -> 71.6 us
  local copies, waits for them, and re-layouts: 58.9 us -> 23.6 us
    unnamed x1 -> x0, blocking collectives: 505 us -> none
    all_to_all x1, blocking collectives: 206 us -> 15.7 us  [on_device(): spread = lax.all_to_all(payload, ('p', 'y'), 0, 0, tiled=True)]
    all_to_all x2 -> x5, waiting for transfers between devices: 195 us -> 56.2 us  [the longest x1 47.5 us: on_device(): returned = lax.all_to_all(expert_out, EXPERT, 0, 0, tiled=True)]
    ppermute x0 -> x6, waiting for transfers between devices: none -> 63.6 us  [shift_y(): lax.ppermute(array, 'y', [(j, (j + shift) % groups) for j in range(groups)])]
    psum x1 -> x0, waiting for transfers between devices: 32 us -> none  [on_device(): lax.psum(moe_part.astype(jnp.bfloat16), 'group').astype(jnp.float32)]
    reshape x4 -> x6, local copies, waits for them, and re-layouts: 28.3 us -> 3.11 us  [the longest x1 1.21 us: on_device(): expert_out = expert_out.astype(BF16).reshape(experts, CAP, part)]
    all_to_all x2 -> x5, starting transfers between devices: 32.5 us -> 53.4 us  [the longest x1 21 us: on_device(): lax.all_to_all(outgoing.reshape(experts, CAP, part), EXPERT, 0, 0, tiled=...]
    all_gather x3 -> x1, blocking collectives: 29.4 us -> 10.9 us  [on_device(): hidden_all = lax.all_gather(hidden, 'y', axis=0, tiled=False)]
  transfers between devices with their start and end apart: 3 -> 12, of which waited for: 3 -> 8; matrix products, arithmetic and copies ran while one was open for 0% -> 12% of each run, Pallas kernels for 0% -> 0%
where the time goes in v1:
time: 279 us; the launch traced here: 277 us
  waiting for transfers between devices  120 us (43%)
  starting transfers between devices  71.6 us (26%)
  blocking collectives  26.7 us (10%)
  local copies, waits for them, and re-layouts  23.6 us (8%)
  between operations  16.6 us (6%)
  matrix products  13.5 us (5%)
  other arithmetic  5.79 us (2%)
    ppermute x6, waiting for transfers between devices, shift_y(): lax.ppermute(array, 'y', [(j, (j + shift) % groups) for j in range(groups)])  63.6 us
    all_to_all x1, waiting for transfers between devices, on_device(): returned = lax.all_to_all(expert_out, EXPERT, 0, 0, tiled=True)  47.5 us
    all_to_all x1, starting transfers between devices, on_device(): lax.all_to_all(outgoing.reshape(experts, CAP, part), EXPERT, 0, 0, tiled=...  21 us
    all_to_all x1, starting transfers between devices, on_device(): returned = lax.all_to_all(expert_out, EXPERT, 0, 0, tiled=True)  19.7 us
    ppermute x6, starting transfers between devices, shift_y(): lax.ppermute(array, 'y', [(j, (j + shift) % groups) for j in range(groups)])  18.1 us
    all_to_all x1, blocking collectives, on_device(): spread = lax.all_to_all(payload, ('p', 'y'), 0, 0, tiled=True)  15.7 us
    all_gather x1, blocking collectives, on_device(): hidden_all = lax.all_gather(hidden, 'y', axis=0, tiled=False)  10.9 us
  transfers between devices with their start and end apart: 12, of which 8 were waited for; matrix products, arithmetic and copies ran while one was open for 12% of the time, Pallas kernels for 0%

profile of v1, /device:TPU:1, one launch (start us, length us, event | category | flops | bytes accessed | tf_op | source)
XLA Modules:
  0.0 277.4 jit_solution(1809382176542385105)
XLA Ops:
  7.2 0.7 convert_element_type.71
  7.9 1.0 fusion.9
  8.9 0.9 fusion.11
  9.8 1.5 maximum_bitcast_fusion
  11.3 5.0 %all-to-all-start = ((bf16[4,2,8,1024]{3,2,1,0:T(8,128)(2,1)}), bf16[4,2,8,1024]{3,2,1,0:T(8,128)(2,1)S(1)}, u32[]{:S(2)}, u32[]{:S(2)}) async-start(bf16[4,2,8,1024]{3,2,1,0:T(8,128)(2,1)} %maximum_bitcast_fusion), calls=%async_computation | async-start | bytes 262144 | tf_op jit(solution)/shard_map/all_to_all | solution.py:79
  16.3 0.8 copy.66
  17.7 3.4 %all-to-all-done = bf16[4,2,8,1024]{3,2,1,0:T(8,128)(2,1)S(1)} async-done(((bf16[4,2,8,1024]{3,2,1,0:T(8,128)(2,1)}), bf16[4,2,8,1024]{3,2,1,0:T(8,128)(2,1)S(1)}, u32[]{:S(2)}, u32[]{:S(2)}) %all-to-all-start) | async-done | bytes 131104 | tf_op jit(solution)/shard_map/all_to_all | solution.py:79
  21.6 1.2 reshape.112
  22.8 21.0 %all-to-all-start.1 = ((bf16[128,4,1024]{2,1,0:T(4,128)(2,1)}), bf16[128,4,1024]{2,1,0:T(4,128)(2,1)S(1)}, u32[]{:S(2)}, u32[]{:S(2)}) async-start(bf16[128,4,1024]{2,1,0:T(4,128)(2,1)} %reshape.112), calls=%async_computation.1 | async-start | bytes 2097152 | tf_op jit(solution)/shard_map/all_to_all | solution.py:95
  44.1 1.2 copy-done.2
  45.5 1.3 copy-done.3
  46.9 2.2 constant_dynamic-slice_fusion.7
  49.1 1.0 copy-done
  50.1 2.2 collective-permute-start
  52.3 3.7 %collective-permute-start.2 = (bf16[3,192,1024]{2,1,0:T(8,128)(2,1)}, bf16[3,192,1024]{2,1,0:T(8,128)(2,1)S(1)}, u32[]{:S(2)}, u32[]{:S(2)}) collective-permute-start(bf16[3,192,1024]{2,1,0:T(8,128)(2,1)} %get-tuple-element.7), channel_id=1, source_target_pairs={{0,2},{1,3},{2,0},{3,1},{4,6},{5,7},{6,4},{7,5},{8,10},{9,11},{10,... | collective-permute-start | bytes 3538952 | tf_op jit(solution)/shard_map/ppermute | solution.py:42
  56.0 2.5 collective-permute-start.4
  58.6 22.1 %collective-permute-done = bf16[3,192,1024]{2,1,0:T(8,128)(2,1)} collective-permute-done((bf16[3,192,1024]{2,1,0:T(8,128)(2,1)}, bf16[3,192,1024]{2,1,0:T(8,128)(2,1)}, u32[]{:S(2)}, u32[]{:S(2)}) %collective-permute-start) | collective-permute-done | bytes 1179680 | tf_op jit(solution)/shard_map/ppermute | solution.py:42
  80.7 2.1 slice.64
  82.8 21.9 %collective-permute-done.2 = bf16[3,192,1024]{2,1,0:T(8,128)(2,1)S(1)} collective-permute-done((bf16[3,192,1024]{2,1,0:T(8,128)(2,1)}, bf16[3,192,1024]{2,1,0:T(8,128)(2,1)S(1)}, u32[]{:S(2)}, u32[]{:S(2)}) %collective-permute-start.2) | collective-permute-done | bytes 1179680 | tf_op jit(solution)/shard_map/ppermute | solution.py:42
  104.7 3.4 %collective-permute-done.4 = bf16[3,192,1024]{2,1,0:T(8,128)(2,1)} collective-permute-done((bf16[3,192,1024]{2,1,0:T(8,128)(2,1)}, bf16[3,192,1024]{2,1,0:T(8,128)(2,1)}, u32[]{:S(2)}, u32[]{:S(2)}) %collective-permute-start.4) | collective-permute-done | bytes 1179680 | tf_op jit(solution)/shard_map/ppermute | solution.py:42
  108.2 2.1 slice.66
  110.6 1.9 convolution_convert_fusion.3
  112.4 5.3 %collective-permute-start.1 = (bf16[512,384]{0,1:T(8,128)(2,1)S(1)}, bf16[512,384]{0,1:T(8,128)(2,1)S(1)}, u32[]{:S(2)}, u32[]{:S(2)}) collective-permute-start(bf16[512,384]{0,1:T(8,128)(2,1)S(1)} %convolution_convert_fusion.3), channel_id=1, source_target_pairs={{0,3},{1,0},{2,1},{3,2},{4,7},{5,4},{6,5},{7,6},{8,11},{9,8},{10,9... | collective-permute-start | bytes 1179656 | tf_op jit(solution)/shard_map/ppermute | solution.py:42
  117.8 0.6 convolution_convert_fusion.2
  118.4 1.9 collective-permute-start.3
  120.3 0.6 convolution_convert_fusion.1
  120.9 2.5 collective-permute-start.5
  123.4 1.2 constant_dynamic-slice_fusion
  125.2 8.8 %collective-permute-done.1 = bf16[512,384]{0,1:T(8,128)(2,1)S(1)} collective-permute-done((bf16[512,384]{0,1:T(8,128)(2,1)S(1)}, bf16[512,384]{0,1:T(8,128)(2,1)S(1)}, u32[]{:S(2)}, u32[]{:S(2)}) %collective-permute-start.1) | collective-permute-done | bytes 393248 | tf_op jit(solution)/shard_map/ppermute | solution.py:42
  134.0 7.3 %collective-permute-done.5 = bf16[512,384]{0,1:T(8,128)(2,1)S(1)} collective-permute-done((bf16[512,384]{0,1:T(8,128)(2,1)S(1)}, bf16[512,384]{0,1:T(8,128)(2,1)S(1)}, u32[]{:S(2)}, u32[]{:S(2)}) %collective-permute-start.5) | collective-permute-done | bytes 393248 | tf_op jit(solution)/shard_map/ppermute | solution.py:42
  141.7 10.9 %all-gather = bf16[2048,192]{0,1:T(8,128)(2,1)S(1)} all-gather(bf16[512,192]{0,1:T(8,128)(2,1)S(1)} %fusion.8), channel_id=2, replica_groups=mesh['z'=16,'p'=8,'y'=4] {'y'}, dimensions={0}, use_global_device_ids=true | all-gather | bytes 983040 | tf_op jit(solution)/shard_map/all_gather | solution.py:107
  153.2 1.6 constant_dynamic-slice_fusion.1
  154.8 1.6 fusion.6
  156.4 1.5 fusion.7
  158.4 1.5 add_convert_fusion
  159.9 1.2 reshape.118
  161.1 19.7 %all-to-all-start.2 = ((bf16[128,4,1024]{2,1,0:T(4,128)(2,1)}), bf16[128,4,1024]{2,1,0:T(4,128)(2,1)S(1)}, u32[]{:S(2)}, u32[]{:S(2)}) async-start(bf16[128,4,1024]{2,1,0:T(4,128)(2,1)} %reshape.118), calls=%async_computation.2 | async-start | bytes 2097152 | tf_op jit(solution)/shard_map/all_to_all | solution.py:115
  183.4 1.0 dynamic-slice_reduce_fusion
  185.1 47.5 %all-to-all-done.2 = bf16[128,4,1024]{2,1,0:T(4,128)(2,1)S(1)} async-done(((bf16[128,4,1024]{2,1,0:T(4,128)(2,1)}), bf16[128,4,1024]{2,1,0:T(4,128)(2,1)S(1)}, u32[]{:S(2)}, u32[]{:S(2)}) %all-to-all-start.2) | async-done | bytes 1048608 | tf_op jit(solution)/shard_map/all_to_all | solution.py:115
  232.9 0.9 fusion.2
  233.8 1.4 gather_fusion
  235.7 15.7 %all_to_all.30 = bf16[32,3,512]{2,1,0:T(4,128)(2,1)S(1)} all-to-all(bf16[32,3,512]{2,1,0:T(4,128)(2,1)S(1)} %bitcast.85), channel_id=1, replica_groups=mesh['z'=16,'p'=8,'y'=4] {'p','y'}, dimensions={0} | all-to-all | bytes 196608 | tf_op jit(solution)/shard_map/all_to_all | solution.py:137
  251.4 3.3 %all-to-all-start.3 = ((bf16[4,8,1024]{2,1,0:T(8,128)(2,1)}), bf16[4,8,1024]{2,1,0:T(8,128)(2,1)S(1)}, u32[]{:S(2)}, u32[]{:S(2)}) async-start(bf16[4,8,1024]{2,1,0:T(8,128)(2,1)} %fusion.2), calls=%async_computation.3 | async-start | bytes 131072 | tf_op jit(solution)/shard_map/all_to_all | solution.py:119
  256.4 3.1 %fusion.19 = f32[8,4,1024]{2,1,0:T(4,128)} fusion(bf16[8,4,1536]{2,1,0:T(4,128)(2,1)S(1)} %dot_general.49, bf16[1536,1024,1]{1,0,2:T(8,128)(2,1)} %bitcast.79), kind=kOutput, calls=%fused_computation.73 | convolution fusion | flops 100663296 | bytes 3375104 | tf_op jit(solution)/shard_map/dot_general | solution.py:143
  259.6 4.4 %all-to-all-start.5 = ((f32[8,4,1024]{2,1,0:T(4,128)}), f32[8,4,1024]{2,1,0:T(4,128)S(1)}, u32[]{:S(2)}, u32[]{:S(2)}) async-start(f32[8,4,1024]{2,1,0:T(4,128)} %fusion.19), calls=%async_computation.5 | async-start | bytes 262144 | tf_op jit(solution)/shard_map/all_to_all | solution.py:144
  264.0 5.3 %all-to-all-done.5 = f32[8,4,1024]{2,1,0:T(4,128)S(1)} async-done(((f32[8,4,1024]{2,1,0:T(4,128)}), f32[8,4,1024]{2,1,0:T(4,128)S(1)}, u32[]{:S(2)}, u32[]{:S(2)}) %all-to-all-start.5) | async-done | bytes 131104 | tf_op jit(solution)/shard_map/all_to_all | solution.py:144
  269.3 0.6 reduce_sum.49
  269.9 0.6 copy.107
  (71 shorter events, 7.6 us)
Async XLA Ops:
  11.3 9.8 %all-to-all-start = ((bf16[4,2,8,1024]{3,2,1,0:T(8,128)(2,1)}), bf16[4,2,8,1024]{3,2,1,0:T(8,128)(2,1)S(1)}, u32[]{:S(2)}, u32[]{:S(2)}) async-start(bf16[4,2,8,1024]{3,2,1,0:T(8,128)(2,1)} %maximum_bitcast_fusion), calls=%async_computation | async-start | bytes 262144 | tf_op jit(solution)/shard_map/all_to_all | solution.py:79
  21.6 22.3 %copy-start.1 = (bf16[1,192,4096]{2,1,0:T(8,128)(2,1)S(1)}, bf16[1,192,4096]{2,1,0:T(8,128)(2,1)}, u32[]{:S(2)}) copy-start(bf16[1,192,4096]{2,1,0:T(8,128)(2,1)} %param.15) | copy-start | bytes 4718596
  22.8 87.4 %all-to-all-start.1 = ((bf16[128,4,1024]{2,1,0:T(4,128)(2,1)}), bf16[128,4,1024]{2,1,0:T(4,128)(2,1)S(1)}, u32[]{:S(2)}, u32[]{:S(2)}) async-start(bf16[128,4,1024]{2,1,0:T(4,128)(2,1)} %reshape.112), calls=%async_computation.1 | async-start | bytes 2097152 | tf_op jit(solution)/shard_map/all_to_all | solution.py:95
  43.8 212.6 %all-gather.4.cloned.1.call-start = ((), (), s32[]{:S(2)}) async-start(), calls=%async_computation.6 | async-start | bytes 3342336 | tf_op jit(solution)/shard_map/all_gather | solution.py:67
  43.9 1.4 copy-start.2
  45.3 1.4 copy-start.3
  46.9 3.2 %copy-start = (bf16[3,192,4096]{2,1,0:T(8,128)(2,1)}, bf16[3,192,4096]{2,1,0:T(8,128)(2,1)S(1)}, u32[]{:S(2)}) copy-start(bf16[3,192,4096]{2,1,0:T(8,128)(2,1)S(1)} %constant_dynamic-update-slice_fusion) | copy-start | bytes 14155780
  50.1 30.6 %collective-permute-start = (bf16[3,192,1024]{2,1,0:T(8,128)(2,1)}, bf16[3,192,1024]{2,1,0:T(8,128)(2,1)}, u32[]{:S(2)}, u32[]{:S(2)}) collective-permute-start(bf16[3,192,1024]{2,1,0:T(8,128)(2,1)} %get-tuple-element.5), channel_id=1, source_target_pairs={{0,1},{1,2},{2,3},{3,0},{4,5},{5,6},{6,7},{7,4},{8,9},{9,10},{10,1... | collective-permute-start | bytes 3538952 | tf_op jit(solution)/shard_map/ppermute | solution.py:42
  52.3 52.4 %collective-permute-start.2 = (bf16[3,192,1024]{2,1,0:T(8,128)(2,1)}, bf16[3,192,1024]{2,1,0:T(8,128)(2,1)S(1)}, u32[]{:S(2)}, u32[]{:S(2)}) collective-permute-start(bf16[3,192,1024]{2,1,0:T(8,128)(2,1)} %get-tuple-element.7), channel_id=1, source_target_pairs={{0,2},{1,3},{2,0},{3,1},{4,6},{5,7},{6,4},{7,5},{8,10},{9,11},{10,... | collective-permute-start | bytes 3538952 | tf_op jit(solution)/shard_map/ppermute | solution.py:42
  56.0 52.2 %collective-permute-start.4 = (bf16[3,192,1024]{2,1,0:T(8,128)(2,1)}, bf16[3,192,1024]{2,1,0:T(8,128)(2,1)}, u32[]{:S(2)}, u32[]{:S(2)}) collective-permute-start(bf16[3,192,1024]{2,1,0:T(8,128)(2,1)} %get-tuple-element.6), channel_id=1, source_target_pairs={{0,3},{1,0},{2,1},{3,2},{4,7},{5,4},{6,5},{7,6},{8,11},{9,8},{10,9... | collective-permute-start | bytes 3538952 | tf_op jit(solution)/shard_map/ppermute | solution.py:42
  104.7 5.8 %copy-start.4 = (bf16[3,192,1024]{2,1,0:T(8,128)(2,1)}, bf16[3,192,1024]{2,1,0:T(8,128)(2,1)S(1)}, u32[]{:S(2)}) copy-start(bf16[3,192,1024]{2,1,0:T(8,128)(2,1)S(1)} %collective-permute-done.2) | copy-start | bytes 3538948
  110.5 7.2 %slice-start = ((bf16[3,192,1024]{2,1,0:T(8,128)(2,1)}), bf16[2,192,1024]{2,1,0:T(8,128)(2,1)S(1)}, s32[]{:S(2)}) async-start(bf16[3,192,1024]{2,1,0:T(8,128)(2,1)} %copy-done.4), calls=%async_computation.7 | async-start | bytes 1572864 | tf_op jit(solution)/shard_map/slice | solution.py:100
  110.6 9.8 %copy-start.6 = (bf16[2,192,1024]{2,1,0:T(8,128)(2,1)S(1)}, bf16[2,192,1024]{2,1,0:T(8,128)(2,1)}, u32[]{:S(2)}) copy-start(bf16[2,192,1024]{2,1,0:T(8,128)(2,1)} %slice.66) | copy-start | bytes 2359300
  112.4 21.6 %collective-permute-start.1 = (bf16[512,384]{0,1:T(8,128)(2,1)S(1)}, bf16[512,384]{0,1:T(8,128)(2,1)S(1)}, u32[]{:S(2)}, u32[]{:S(2)}) collective-permute-start(bf16[512,384]{0,1:T(8,128)(2,1)S(1)} %convolution_convert_fusion.3), channel_id=1, source_target_pairs={{0,3},{1,0},{2,1},{3,2},{4,7},{5,4},{6,5},{7,6},{8,11},{9,8},{10,9... | collective-permute-start | bytes 1179656 | tf_op jit(solution)/shard_map/ppermute | solution.py:42
  118.4 15.6 %collective-permute-start.3 = (bf16[512,384]{0,1:T(8,128)(2,1)S(1)}, bf16[512,384]{0,1:T(8,128)(2,1)S(1)}, u32[]{:S(2)}, u32[]{:S(2)}) collective-permute-start(bf16[512,384]{0,1:T(8,128)(2,1)S(1)} %convolution_convert_fusion.2), channel_id=1, source_target_pairs={{0,2},{1,3},{2,0},{3,1},{4,6},{5,7},{6,4},{7,5},{8,10},{9,11},{10,... | collective-permute-start | bytes 1179656 | tf_op jit(solution)/shard_map/ppermute | solution.py:42
  120.9 20.4 %collective-permute-start.5 = (bf16[512,384]{0,1:T(8,128)(2,1)S(1)}, bf16[512,384]{0,1:T(8,128)(2,1)S(1)}, u32[]{:S(2)}, u32[]{:S(2)}) collective-permute-start(bf16[512,384]{0,1:T(8,128)(2,1)S(1)} %convolution_convert_fusion.1), channel_id=1, source_target_pairs={{0,1},{1,2},{2,3},{3,0},{4,5},{5,6},{6,7},{7,4},{8,9},{9,10},{10,1... | collective-permute-start | bytes 1179656 | tf_op jit(solution)/shard_map/ppermute | solution.py:42
  154.8 3.1 %copy-start.5 = (bf16[3,192,1024]{2,1,0:T(8,128)(2,1)S(1)}, bf16[3,192,1024]{2,1,0:T(8,128)(2,1)}, u32[]{:S(2)}) copy-start(bf16[3,192,1024]{2,1,0:T(8,128)(2,1)} %copy-done.4) | copy-start | bytes 3538948
  159.9 20.9 %copy-start.7 = (f32[32,8]{0,1:T(8,128)S(1)}, f32[32,8]{0,1:T(8,128)}, u32[]{:S(2)}) copy-start(f32[32,8]{0,1:T(8,128)} %param.14) | copy-start | bytes 3076
  159.9 21.0 %copy-start.8 = (s32[4]{0:T(128)S(1)}, s32[4]{0:T(128)}, u32[]{:S(2)}) copy-start(s32[4]{0:T(128)} %param.20) | copy-start | bytes 52
  161.1 71.5 %all-to-all-start.2 = ((bf16[128,4,1024]{2,1,0:T(4,128)(2,1)}), bf16[128,4,1024]{2,1,0:T(4,128)(2,1)S(1)}, u32[]{:S(2)}, u32[]{:S(2)}) async-start(bf16[128,4,1024]{2,1,0:T(4,128)(2,1)} %reshape.118), calls=%async_computation.2 | async-start | bytes 2097152 | tf_op jit(solution)/shard_map/all_to_all | solution.py:115
  251.4 8.2 %all-to-all-start.3 = ((bf16[4,8,1024]{2,1,0:T(8,128)(2,1)}), bf16[4,8,1024]{2,1,0:T(8,128)(2,1)S(1)}, u32[]{:S(2)}, u32[]{:S(2)}) async-start(bf16[4,8,1024]{2,1,0:T(8,128)(2,1)} %fusion.2), calls=%async_computation.3 | async-start | bytes 131072 | tf_op jit(solution)/shard_map/all_to_all | solution.py:119
  259.6 9.7 %all-to-all-start.5 = ((f32[8,4,1024]{2,1,0:T(4,128)}), f32[8,4,1024]{2,1,0:T(4,128)S(1)}, u32[]{:S(2)}, u32[]{:S(2)}) async-start(f32[8,4,1024]{2,1,0:T(4,128)} %fusion.19), calls=%async_computation.5 | async-start | bytes 262144 | tf_op jit(solution)/shard_map/all_to_all | solution.py:144
Sparse Core Ops, SparseCore 0:
  58.7 80.5 all-gather.3

commit v2 on v1

v2 whole, which is shorter than its diff:
```python
import functools

import jax
import jax.numpy as jnp
from jax import lax
from jax.experimental import pallas as pl
from jax.experimental.pallas import tpu as pltpu
from jax.sharding import Mesh
from jax.sharding import PartitionSpec as P

EPSILON = 1e-06
Z_SIZE = 16
P_SIZE = 8
CAP = 4
EXPERT = ("z", "p")
F32 = jnp.float32
BF16 = jnp.bfloat16
PARAMS = pltpu.CompilerParams(vmem_limit_bytes=40 * 1024 * 1024)
VMEM = pl.BlockSpec(memory_space=pltpu.VMEM)
SMEM = pl.BlockSpec(memory_space=pltpu.SMEM)


def cost(flops, moved):
    return pl.CostEstimate(flops=flops, bytes_accessed=moved, transcendentals=0)


def norm_kernel(layer_ref, gain_ref, out_ref):
    groups, _, _, part = out_ref.shape
    widened = layer_ref[...].astype(F32)
    inverse = lax.rsqrt(jnp.mean(widened * widened, axis=-1, keepdims=True) + EPSILON)
    normed = (widened * inverse * gain_ref[...].astype(F32)).astype(BF16)
    for j in range(groups):
        out_ref[j, 0] = normed[:, j * part : (j + 1) * part]
        out_ref[j, 1] = layer_ref[:, j * part : (j + 1) * part]


def normed_and_raw(layer_in, norm_gain, groups):
    rows, width = layer_in.shape
    return pl.pallas_call(
        norm_kernel,
        out_shape=jax.ShapeDtypeStruct((groups, 2, rows, width // groups), BF16),
        in_specs=[VMEM] * 2,
        out_specs=VMEM,
        compiler_params=PARAMS,
        cost_estimate=cost(rows * width * 6, rows * width * 6),
        name="norm_pack",
    )(layer_in, norm_gain.reshape(1, width))


def slice_kernel(groups, g_ref, gate_ref, up_ref, down_ref, *refs):
    outs, sems = refs[:-1], refs[-1]
    units = gate_ref.shape[1]
    part = gate_ref.shape[2] // groups
    copies = []
    for s in range(1, groups):
        lane = pl.multiple_of(lax.rem(g_ref[0] + s, groups) * part, part)
        for k, source in enumerate((gate_ref, up_ref, down_ref)):
            copies.append(
                pltpu.make_async_copy(
                    source.at[0, :, pl.ds(lane, part)],
                    outs[s - 1].at[pl.ds(k * units, units), :],
                    sems.at[s - 1, k],
                )
            )
    for copy in copies:
        copy.start()
    for copy in copies:
        copy.wait()


def weight_pieces(g, gate, up, down, groups):
    _, units, width = gate.shape
    any_space = pl.BlockSpec(memory_space=pl.ANY)
    shape = jax.ShapeDtypeStruct((3 * units, width // groups), BF16)
    return pl.pallas_call(
        functools.partial(slice_kernel, groups),
        out_shape=[shape] * (groups - 1),
        in_specs=[SMEM] + [any_space] * 3,
        out_specs=[any_space] * (groups - 1),
        scratch_shapes=[pltpu.SemaphoreType.DMA((groups - 1, 3))],
        compiler_params=PARAMS,
        cost_estimate=cost(0, 6 * units * width * 2),
        name="weight_slices",
    )(g, gate, up, down)


def dot_nt(a, b):
    return lax.dot_general(a, b, (((1,), (1,)), ((), ())), preferred_element_type=F32)


def dot_tn(a, b):
    return lax.dot_general(a, b, (((0,), (0,)), ((), ())), preferred_element_type=F32)


def gate_up_kernel(groups, g_ref, rows_ref, gate_ref, up_ref, *refs):
    pieces, out_ref = refs[:-1], refs[-1]
    units = gate_ref.shape[1]
    rows = rows_ref[...]
    g = g_ref[0]
    out_ref[g, :units] = dot_nt(gate_ref[0], rows).astype(BF16)
    out_ref[g, units:] = dot_nt(up_ref[0], rows).astype(BF16)
    for s in range(1, groups):
        home = lax.rem(g + groups - s, groups)
        out_ref[home] = dot_nt(pieces[s - 1][...], rows).astype(BF16)


def gate_up(g, rows, gate, up, pieces, groups):
    slots, part = rows.shape
    units = gate.shape[1]
    own = pl.BlockSpec((1, units, part), lambda i, g_ref: (0, 0, g_ref[0]))
    return pl.pallas_call(
        functools.partial(gate_up_kernel, groups),
        out_shape=jax.ShapeDtypeStruct((groups, 2 * units, slots), BF16),
        grid_spec=pltpu.PrefetchScalarGridSpec(
            num_scalar_prefetch=1,
            grid=(1,),
            in_specs=[pl.BlockSpec((slots, part), lambda i, g_ref: (0, 0)), own, own]
            + [pl.BlockSpec((2 * units, part), lambda i, g_ref: (0, 0))] * (groups - 1),
            out_specs=pl.BlockSpec((groups, 2 * units, slots), lambda i, g_ref: (0, 0, 0)),
        ),
        compiler_params=PARAMS,
        cost_estimate=cost(2 * slots * part * 2 * units * groups, 6 << 20),
        name="gate_up",
    )(g, rows, gate, up, *pieces)


def silu_kernel(acts_ref, out_ref):
    units = out_ref.shape[0]
    gate = jnp.sum(acts_ref[:, :units].astype(F32), axis=0)
    up = jnp.sum(acts_ref[:, units:].astype(F32), axis=0)
    out_ref[...] = (gate / (1.0 + jnp.exp(-gate)) * up).astype(BF16)


def silu(acts):
    _, double, slots = acts.shape
    return pl.pallas_call(
        silu_kernel,
        out_shape=jax.ShapeDtypeStruct((double // 2, slots), BF16),
        in_specs=[VMEM],
        out_specs=VMEM,
        compiler_params=PARAMS,
        cost_estimate=cost(8 * double * slots, 2 << 20),
        name="silu_sum",
    )(acts)


def down_kernel(groups, g_ref, hidden_ref, own_ref, *refs):
    pieces, out_ref = refs[:-1], refs[-1]
    units = own_ref.shape[1]
    part = out_ref.shape[1]
    g = g_ref[0]
    chunk = part // 4
    held = [
        hidden_ref[pl.ds(pl.multiple_of(lax.rem(g + groups - s, groups) * units, units), units), :]
        for s in range(groups)
    ]
    for n in range(4):
        columns = slice(n * chunk, (n + 1) * chunk)
        total = dot_tn(held[0], own_ref[0, :, columns])
        for s in range(1, groups):
            total += dot_tn(held[s], pieces[s - 1][:, columns])
        out_ref[:, columns] = total.astype(BF16)


def down(g, hidden, own, pieces, groups):
    inner, slots = hidden.shape
    units = own.shape[1]
    part = own.shape[2] // groups
    return pl.pallas_call(
        functools.partial(down_kernel, groups),
        out_shape=jax.ShapeDtypeStruct((slots, part), BF16),
        grid_spec=pltpu.PrefetchScalarGridSpec(
            num_scalar_prefetch=1,
            grid=(1,),
            in_specs=[
                pl.BlockSpec((inner, slots), lambda i, g_ref: (0, 0)),
                pl.BlockSpec((1, units, part), lambda i, g_ref: (0, 0, g_ref[0])),
            ]
            + [pl.BlockSpec((units, part), lambda i, g_ref: (2, 0))] * (groups - 1),
            out_specs=pl.BlockSpec((slots, part), lambda i, g_ref: (0, 0)),
        ),
        compiler_params=PARAMS,
        cost_estimate=cost(2 * slots * inner * part, 4 << 20),
        name="down",
    )(g, hidden, own, *pieces)


def combine_kernel(node_ref, table_ref, returned_ref, block_ref, out_ref, high_ref):
    trees = high_ref.shape[0]
    tree = out_ref.shape[0] // trees
    moe = jnp.dot(table_ref[...], returned_ref[...], preferred_element_type=F32)
    result = (block_ref[...].astype(F32) + moe).astype(BF16)
    out_ref[...] = result
    widened = result.astype(F32)
    place = lax.broadcasted_iota(jnp.int32, (tree, out_ref.shape[1]), 0)
    for t in range(trees):
        rows = widened[t * tree : (t + 1) * tree]
        kept = jnp.sum(jnp.where(place == node_ref[t], rows, 0.0), axis=0, keepdims=True)
        high_ref[t : t + 1, :] = kept


def combine(nodes, table, returned, block_in):
    block, part = block_in.shape
    return pl.pallas_call(
        combine_kernel,
        out_shape=[
            jax.ShapeDtypeStruct((block, part), BF16),
            jax.ShapeDtypeStruct((nodes.shape[0], part), F32),
        ],
        in_specs=[SMEM] + [VMEM] * 3,
        out_specs=[VMEM] * 2,
        compiler_params=PARAMS,
        cost_estimate=cost(2 * block * returned.shape[0] * part, 2 << 20),
        name="combine",
    )(nodes, table, returned, block_in)


def early_kernel(rows_ref, weight_ref, out_ref):
    out_ref[...] = jnp.dot(
        rows_ref[...], weight_ref[...].reshape(-1, out_ref.shape[1]), preferred_element_type=F32
    )


def early_join(rows, weight):
    z_size, _, feat, width = weight.shape
    return pl.pallas_call(
        early_kernel,
        out_shape=jax.ShapeDtypeStruct((rows.shape[0], width), F32),
        grid=(1,),
        in_specs=[
            pl.BlockSpec(rows.shape, lambda i: (0, 0)),
            pl.BlockSpec((z_size, 2, feat, width), lambda i: (0, 0, 0, 0)),
        ],
        out_specs=pl.BlockSpec((rows.shape[0], width), lambda i: (0, 0)),
        compiler_params=PARAMS,
        cost_estimate=cost(2 * rows.shape[0] * rows.shape[1] * width, 2 << 20),
        name="join_early",
    )(rows, weight)


def late_kernel(rows_ref, weight_ref, early_ref, out_ref):
    out_ref[...] = early_ref[...] + jnp.dot(
        rows_ref[...], weight_ref[...].reshape(-1, out_ref.shape[1]), preferred_element_type=F32
    )


def late_join(rows, weight, early):
    z_size, _, feat, width = weight.shape
    return pl.pallas_call(
        late_kernel,
        out_shape=jax.ShapeDtypeStruct((rows.shape[0], width), F32),
        grid=(1,),
        in_specs=[
            pl.BlockSpec(rows.shape, lambda i: (0, 0)),
            pl.BlockSpec((z_size, 1, feat, width), lambda i: (0, 2, 0, 0)),
            pl.BlockSpec(early.shape, lambda i: (0, 0)),
        ],
        out_specs=pl.BlockSpec((rows.shape[0], width), lambda i: (0, 0)),
        compiler_params=PARAMS,
        cost_estimate=cost(2 * rows.shape[0] * rows.shape[1] * width, 1 << 20),
        name="join_late",
    )(rows, weight, early)


def route_weights(route_logits):
    exponent = jnp.exp(route_logits)
    return (exponent / jnp.sum(exponent, axis=-1, keepdims=True)).astype(BF16)


def slot_places(route_ids, experts):
    flat_ids = route_ids.reshape(-1)
    amount = flat_ids.shape[0]
    onehot = flat_ids[:, None] == jnp.arange(experts, dtype=jnp.int32)[None, :]
    lower = jnp.arange(amount)[:, None] > jnp.arange(amount)[None, :]
    before = jnp.dot(lower.astype(BF16), onehot.astype(BF16), preferred_element_type=F32)
    rank = jnp.sum(jnp.where(onehot, before, 0.0), axis=1).astype(jnp.int32)
    return flat_ids * CAP + rank


def on_device(
    layer_in,
    norm_gain,
    route_ids,
    route_logits,
    gate_proj,
    up_proj,
    down_proj,
    low_feature,
    mid_feature,
    accepted_node,
    join_weight,
):
    groups = lax.axis_size("y")
    experts = Z_SIZE * P_SIZE
    g = lax.axis_index("y").astype(jnp.int32)
    g_one = g.reshape(1)
    rows_dev, width = layer_in.shape
    block, top = route_ids.shape
    part = width // groups
    slots = experts * CAP
    trees = accepted_node.shape[0]

    join_all = lax.all_gather(join_weight, "z", axis=0, tiled=False)

    both = normed_and_raw(layer_in, norm_gain, groups)
    both = lax.all_to_all(both, "y", 0, 0, tiled=True)
    normed = both[:, 0].reshape(block, part)
    block_in = both[:, 1].reshape(block, part)

    weights = route_weights(route_logits)
    places = slot_places(route_ids, experts)
    slot_ids = jnp.arange(slots, dtype=jnp.int32)
    matches = (places[:, None] == slot_ids[None, :]).reshape(block, top, slots)
    dispatch = jnp.any(matches, axis=1).astype(BF16)
    outgoing = dot_tn(dispatch, normed).astype(BF16).reshape(experts, CAP, part)

    cut = weight_pieces(g_one, gate_proj, up_proj, down_proj, groups)
    outgoing, *cut = lax.optimization_barrier((outgoing, *cut))
    pieces = [
        lax.ppermute(piece, "y", [(j, (j + s + 1) % groups) for j in range(groups)])
        for s, piece in enumerate(cut)
    ]
    received = lax.all_to_all(outgoing, EXPERT, 0, 0, tiled=True)
    rows = received.reshape(slots, part)

    combine_table = jnp.sum(
        jnp.where(matches, weights.astype(F32)[:, :, None], 0.0), axis=1
    ).astype(BF16)

    acts = gate_up(g_one, rows, gate_proj, up_proj, pieces, groups)
    acts = lax.all_to_all(acts, "y", 0, 0, tiled=True)
    hidden = silu(acts)
    hidden_all = lax.all_gather(hidden, "y", axis=0, tiled=True)
    expert_out = down(g_one, hidden_all, down_proj, pieces, groups)
    returned = lax.all_to_all(expert_out.reshape(experts, CAP, part), EXPERT, 0, 0, tiled=True)

    own_node = lax.dynamic_slice_in_dim(accepted_node, g, 1, 0)[0]
    feat = width // experts
    low = lax.dynamic_index_in_dim(low_feature, own_node, 0, keepdims=False)
    mid = lax.dynamic_index_in_dim(mid_feature, own_node, 0, keepdims=False)
    known = jnp.stack([low.reshape(Z_SIZE, P_SIZE, feat), mid.reshape(Z_SIZE, P_SIZE, feat)], 0)
    known = known.transpose(2, 1, 0, 3).reshape(P_SIZE, 1, 1, -1)
    known = jnp.broadcast_to(known, (P_SIZE, groups, 1, known.shape[-1]))
    known = known.reshape(P_SIZE * groups, 1, -1)
    known, _ = lax.optimization_barrier((known, hidden))
    known = lax.all_to_all(known, ("p", "y"), 0, 0, tiled=True)
    early = early_join(known.reshape(P_SIZE * trees, -1), join_all)
    returned, early = lax.optimization_barrier((returned, early))

    block_out, high = combine(
        accepted_node, combine_table, returned.reshape(slots, part), block_in
    )

    z_part = Z_SIZE // groups
    high = high.astype(BF16).reshape(trees, z_part, P_SIZE, feat).transpose(2, 0, 1, 3)
    high = jnp.broadcast_to(
        high.reshape(P_SIZE, 1, trees, z_part * feat), (P_SIZE, groups, trees, z_part * feat)
    )
    high = lax.all_to_all(
        high.reshape(P_SIZE * groups, trees, z_part * feat), ("p", "y"), 0, 0, tiled=True
    )
    high = high.reshape(P_SIZE, groups, trees, z_part * feat).transpose(0, 2, 1, 3)
    summed = late_join(high.reshape(P_SIZE * trees, -1), join_all, early)
    summed = lax.all_to_all(summed.reshape(P_SIZE, trees, -1), "p", 0, 0, tiled=True)
    joined_rows = jnp.sum(summed, axis=0).astype(BF16)

    own_rows = lax.all_to_all(block_out.reshape(groups, rows_dev, part), "y", 0, 0, tiled=True)
    layer_out = own_rows.transpose(1, 0, 2).reshape(rows_dev, width)
    return (layer_out, joined_rows)


def solution(mesh):
    split = Mesh(mesh.devices.reshape(Z_SIZE, P_SIZE, -1), ("z", "p", "y"))
    every = ("z", "p", "y")
    placed = (
        P(every, None),
        P(),
        P(EXPERT, None),
        P(EXPERT, None),
        P(EXPERT, "y", None),
        P(EXPERT, "y", None),
        P(EXPERT, "y", None),
        P(every, None),
        P(every, None),
        P(EXPERT),
        P(None, EXPERT, "y"),
    )
    return jax.shard_map(
        on_device,
        mesh=split,
        in_specs=placed,
        out_specs=(P(every, None), P(EXPERT, "y")),
        check_vma=False,
    )
```

time: 279 us -> 281 us (level)
  matrix products: 13.5 us -> 0.72 us
  Pallas kernels: 0 us -> 9.95 us
  starting transfers between devices: 71.6 us -> 78.1 us
  waiting for transfers between devices: 120 us -> 115 us
  local copies, waits for them, and re-layouts: 23.6 us -> 27.7 us
  other arithmetic: 5.79 us -> 2.58 us
    ppermute x6 -> x3, waiting for transfers between devices: 63.6 us -> 1.13 us  [on_device(): lax.ppermute(piece, 'y', [(j, (j + s + 1) % groups) for j in range(groups)])]
    all_to_all x3 -> x5, waiting for transfers between devices: 50.9 us -> 105 us  [the longest x1 48.6 us: on_device(): lax.all_to_all(expert_out.reshape(experts, CAP, part), EXPERT, 0, 0, tile...]
    all_to_all x3 -> x5, starting transfers between devices: 45.7 us -> 58.8 us  [the longest x1 20.4 us: on_device(): received = lax.all_to_all(outgoing, EXPERT, 0, 0, tiled=True)]
    dot_general x11 -> x1, matrix products: 13.2 us -> 0.48 us  [dot_tn(): lax.dot_general(a, b, (((0,), (0,)), ((), ())), preferred_element_type=F32)]
    unnamed x23 -> x40, local copies, waits for them, and re-layouts: 5.21 us -> 15.9 us
    pallas_call x0 -> x8, Pallas kernels: none -> 9.95 us  [the longest x1 3.72 us: gate_up(): pl.pallas_call(functools.partial(gate_up_kernel, groups), out_shape=jax.S...]
    ppermute x6 -> x3, starting transfers between devices: 18.1 us -> 11.2 us  [on_device(): lax.ppermute(piece, 'y', [(j, (j + s + 1) % groups) for j in range(groups)])]
    slice x6 -> x0, local copies, waits for them, and re-layouts: 5.8 us -> none  [the longest x5 5.39 us: on_device(): gate_up = pieces[s][:2].reshape(-1, part)]
  transfers between devices with their start and end apart: 12 -> 11, of which waited for: 8 -> 6; matrix products, arithmetic and copies ran while one was open for 12% -> 4% of each run, Pallas kernels for 0% -> 3%
where the time goes in v2:
time: 281 us; the launch traced here: 280 us
  waiting for transfers between devices  115 us (41%)
  starting transfers between devices  78.1 us (28%)
  blocking collectives  29.3 us (10%)
  local copies, waits for them, and re-layouts  27.7 us (10%)
  between operations  16.3 us (6%)
  Pallas kernels  9.95 us (4%)
    all_to_all x1, waiting for transfers between devices, on_device(): lax.all_to_all(expert_out.reshape(experts, CAP, part), EXPERT, 0, 0, tile...  48.6 us
    all_to_all x1, waiting for transfers between devices, on_device(): received = lax.all_to_all(outgoing, EXPERT, 0, 0, tiled=True)  44 us
    all_to_all x1, starting transfers between devices, on_device(): received = lax.all_to_all(outgoing, EXPERT, 0, 0, tiled=True)  20.4 us
    all_to_all x1, starting transfers between devices, on_device(): lax.all_to_all(expert_out.reshape(experts, CAP, part), EXPERT, 0, 0, tile...  17.3 us
    all_to_all x1, blocking collectives, on_device(): lax.all_to_all(high.reshape(P_SIZE * groups, trees, z_part * feat), ('p',...  17 us
    unnamed x40, local copies, waits for them, and re-layouts  15.9 us
    all_to_all x1, waiting for transfers between devices, on_device(): acts = lax.all_to_all(acts, 'y', 0, 0, tiled=True)  12.8 us
    all_gather x1, blocking collectives, on_device(): hidden_all = lax.all_gather(hidden, 'y', axis=0, tiled=True)  12.3 us
  transfers between devices with their start and end apart: 11, of which 6 were waited for; matrix products, arithmetic and copies ran while one was open for 4% of the time, Pallas kernels for 3%

profile of v2, /device:TPU:1, one launch (start us, length us, event | category | flops | bytes accessed | tf_op | source)
XLA Modules:
  0.0 280.0 jit_solution(3113536945039841270)
XLA Ops:
  7.2 0.7 reshape.82.gain_ref
  7.9 0.8 copy-done.11
  8.7 0.8 norm_pack.1
  9.5 5.0 %all-to-all-start = ((bf16[4,2,8,1024]{3,2,1,0:T(8,128)(2,1)}), bf16[4,2,8,1024]{3,2,1,0:T(8,128)(2,1)S(1)}, u32[]{:S(2)}, u32[]{:S(2)}) async-start(bf16[4,2,8,1024]{3,2,1,0:T(8,128)(2,1)} %norm_pack.1), calls=%async_computation | async-start | bytes 262144 | tf_op jit(solution)/shard_map/all_to_all | solution.py:306
  14.5 0.8 copy.43
  15.7 1.4 copy-done.2
  17.1 1.4 copy-done.4
  18.5 1.4 copy-done.6
  20.4 1.0 copy-done.13
  21.4 1.1 copy-done.14
  22.5 1.0 copy-done.15
  24.3 1.2 reshape.83
  25.5 20.4 %all-to-all-start.1 = ((bf16[128,4,1024]{2,1,0:T(4,128)(2,1)}), bf16[128,4,1024]{2,1,0:T(4,128)(2,1)}, u32[]{:S(2)}, u32[]{:S(2)}) async-start(bf16[128,4,1024]{2,1,0:T(4,128)(2,1)} %reshape.83), calls=%async_computation.1 | async-start | bytes 2097152 | tf_op jit(solution)/shard_map/all_to_all | solution.py:323
  46.0 3.8 %collective-permute-start = (bf16[576,1024]{1,0:T(8,128)(2,1)}, bf16[576,1024]{1,0:T(8,128)(2,1)}, u32[]{:S(2)}, u32[]{:S(2)}) collective-permute-start(bf16[576,1024]{1,0:T(8,128)(2,1)} %copy-done.15), channel_id=1, source_target_pairs={{0,1},{1,2},{2,3},{3,0},{4,5},{5,6},{6,7},{7,4},{8,9},{9,10},{10,1... | collective-permute-start | bytes 3538952 | tf_op jit(solution)/shard_map/ppermute | solution.py:320
  49.8 4.3 %collective-permute-start.1 = (bf16[576,1024]{1,0:T(8,128)(2,1)}, bf16[576,1024]{1,0:T(8,128)(2,1)}, u32[]{:S(2)}, u32[]{:S(2)}) collective-permute-start(bf16[576,1024]{1,0:T(8,128)(2,1)} %copy-done.14), channel_id=1, source_target_pairs={{0,2},{1,3},{2,0},{3,1},{4,6},{5,7},{6,4},{7,5},{8,10},{9,11},{10,... | collective-permute-start | bytes 3538952 | tf_op jit(solution)/shard_map/ppermute | solution.py:320
  54.1 3.1 %collective-permute-start.2 = (bf16[576,1024]{1,0:T(8,128)(2,1)}, bf16[576,1024]{1,0:T(8,128)(2,1)}, u32[]{:S(2)}, u32[]{:S(2)}) collective-permute-start(bf16[576,1024]{1,0:T(8,128)(2,1)} %copy-done.13), channel_id=1, source_target_pairs={{0,3},{1,0},{2,1},{3,2},{4,7},{5,4},{6,5},{7,6},{8,11},{9,8},{10,9... | collective-permute-start | bytes 3538952 | tf_op jit(solution)/shard_map/ppermute | solution.py:320
  57.2 44.0 %all-to-all-done.1 = bf16[128,4,1024]{2,1,0:T(4,128)(2,1)} async-done(((bf16[128,4,1024]{2,1,0:T(4,128)(2,1)}), bf16[128,4,1024]{2,1,0:T(4,128)(2,1)}, u32[]{:S(2)}, u32[]{:S(2)}) %all-to-all-start.1) | async-done | bytes 1048608 | tf_op jit(solution)/shard_map/all_to_all | solution.py:323
  101.2 2.1 reshape.84.rows_ref
  103.4 1.1 collective-permute-done.2.refs_2_
  104.5 1.2 copy-done.9
  105.7 3.7 %gate_up.1 = bf16[4,384,512]{2,1,0:T(8,128)(2,1)S(1)} custom-call(s32[1]{0:T(128)} %bitcast.g_ref, bf16[512,1024]{1,0:T(8,128)(2,1)S(1)} %copy-done.9, bf16[1,192,4096]{2,1,0:T(8,128)(2,1)S(1)} %copy-done.3, bf16[1,192,4096]{2,1,0:T(8,128)(2,1)S(1)} %copy-done.5, bf16[576,1024]{1,0:T(8,128)(2,1)} %collective-permute-done.refs_0_, ...), custom_call_target="tpu_custom_call" | custom-call | flops 1610612736 | bytes 6291456 | tf_op jit(solution)/shard_map/gate_up/pallas_call | solution.py:111
  109.5 1.2 copy-done.8
  110.7 4.8 %all-to-all-start.2 = ((bf16[4,384,512]{2,1,0:T(8,128)(2,1)}), bf16[4,384,512]{2,1,0:T(8,128)(2,1)S(1)}, u32[]{:S(2)}, u32[]{:S(2)}) async-start(bf16[4,384,512]{2,1,0:T(8,128)(2,1)} %copy-done.8), calls=%async_computation.2 | async-start | bytes 3145728 | tf_op jit(solution)/shard_map/all_to_all | solution.py:331
  115.5 0.6 dynamic_slice.10
  118.0 1.0 dynamic-slice_reduce_fusion
  119.5 0.6 broadcast_in_dim.44
  120.1 12.8 %all-to-all-done.2.acts_ref = bf16[4,384,512]{2,1,0:T(8,128)(2,1)S(1)} async-done(((bf16[4,384,512]{2,1,0:T(8,128)(2,1)}), bf16[4,384,512]{2,1,0:T(8,128)(2,1)S(1)}, u32[]{:S(2)}, u32[]{:S(2)}) %all-to-all-start.2) | async-done | bytes 1572896 | tf_op jit(solution)/shard_map/all_to_all | solution.py:331
  133.2 0.5 broadcast.16
  133.7 1.4 reduce.4
  135.2 0.7 reshape.98
  135.8 11.2 %all-to-all-start.4 = ((bf16[32,2,512]{2,1,0:T(2,128)(2,1)}), bf16[32,2,512]{2,1,0:T(2,128)(2,1)S(1)}, u32[]{:S(2)}, u32[]{:S(2)}) async-start(bf16[32,2,512]{2,1,0:T(2,128)(2,1)} %reshape.98), calls=%async_computation.4 | async-start | bytes 131072 | tf_op jit(solution)/shard_map/all_to_all | solution.py:346
  147.0 12.3 %all_gather.9.hidden_ref = bf16[768,512]{1,0:T(8,128)(2,1)S(1)} all-gather(bf16[192,512]{1,0:T(8,128)(2,1)S(1)} %silu_sum.1), channel_id=1, replica_groups=mesh['z'=16,'p'=8,'y'=4] {'y'}, dimensions={0}, use_global_device_ids=true | all-gather | bytes 983040 | tf_op jit(solution)/shard_map/all_gather | solution.py:333
  159.4 2.5 down.1
  161.9 1.2 reshape.85
  163.1 17.3 %all-to-all-start.3 = ((bf16[128,4,1024]{2,1,0:T(4,128)(2,1)}), bf16[128,4,1024]{2,1,0:T(4,128)(2,1)}, u32[]{:S(2)}, u32[]{:S(2)}) async-start(bf16[128,4,1024]{2,1,0:T(4,128)(2,1)} %reshape.85), calls=%async_computation.3 | async-start | bytes 2097152 | tf_op jit(solution)/shard_map/all_to_all | solution.py:335
  181.0 1.9 copy-done
  183.3 48.6 %all-to-all-done.3 = bf16[128,4,1024]{2,1,0:T(4,128)(2,1)} async-done(((bf16[128,4,1024]{2,1,0:T(4,128)(2,1)}), bf16[128,4,1024]{2,1,0:T(4,128)(2,1)}, u32[]{:S(2)}, u32[]{:S(2)}) %all-to-all-start.3) | async-done | bytes 1048608 | tf_op jit(solution)/shard_map/all_to_all | solution.py:335
  232.0 2.1 reshape.87.returned_ref
  234.1 1.2 copy-done.10
  235.3 1.5 combine.1
  237.0 17.0 %all_to_all.40 = bf16[32,4,128]{2,1,0:T(4,128)(2,1)S(1)} all-to-all(bf16[32,4,128]{2,1,0:T(4,128)(2,1)S(1)} %bitcast.38), channel_id=1, replica_groups=mesh['z'=16,'p'=8,'y'=4] {'p','y'}, dimensions={0} | all-to-all | bytes 65536 | tf_op jit(solution)/shard_map/all_to_all | solution.py:359
  254.1 3.3 %all-to-all-start.5 = ((bf16[4,8,1024]{2,1,0:T(8,128)(2,1)}), bf16[4,8,1024]{2,1,0:T(8,128)(2,1)S(1)}, u32[]{:S(2)}, u32[]{:S(2)}) async-start(bf16[4,8,1024]{2,1,0:T(8,128)(2,1)} %bitcast.6), calls=%async_computation.5 | async-start | bytes 131072 | tf_op jit(solution)/shard_map/all_to_all | solution.py:367
  257.7 0.7 reshape.94
  258.4 3.4 %all-to-all-done.5 = bf16[4,8,1024]{2,1,0:T(8,128)(2,1)S(1)} async-done(((bf16[4,8,1024]{2,1,0:T(8,128)(2,1)}), bf16[4,8,1024]{2,1,0:T(8,128)(2,1)S(1)}, u32[]{:S(2)}, u32[]{:S(2)}) %all-to-all-start.5) | async-done | bytes 65568 | tf_op jit(solution)/shard_map/all_to_all | solution.py:367
  261.8 4.8 %all-to-all-start.7 = ((f32[8,4,1024]{2,1,0:T(4,128)}), f32[8,4,1024]{2,1,0:T(4,128)S(1)}, u32[]{:S(2)}, u32[]{:S(2)}) async-start(f32[8,4,1024]{2,1,0:T(4,128)} %reshape.94), calls=%async_computation.7 | async-start | bytes 262144 | tf_op jit(solution)/shard_map/all_to_all | solution.py:364
  266.6 5.3 %all-to-all-done.7 = f32[8,4,1024]{2,1,0:T(4,128)S(1)} async-done(((f32[8,4,1024]{2,1,0:T(4,128)}), f32[8,4,1024]{2,1,0:T(4,128)S(1)}, u32[]{:S(2)}, u32[]{:S(2)}) %all-to-all-start.7) | async-done | bytes 131104 | tf_op jit(solution)/shard_map/all_to_all | solution.py:364
  271.9 0.6 reduce_sum.39
  272.5 0.6 copy.62
  (63 shorter events, 3.8 us)
Async XLA Ops:
  7.9 0.8 copy-start.11
  9.5 14.3 %all-to-all-start = ((bf16[4,2,8,1024]{3,2,1,0:T(8,128)(2,1)}), bf16[4,2,8,1024]{3,2,1,0:T(8,128)(2,1)S(1)}, u32[]{:S(2)}, u32[]{:S(2)}) async-start(bf16[4,2,8,1024]{3,2,1,0:T(8,128)(2,1)} %norm_pack.1), calls=%async_computation | async-start | bytes 262144 | tf_op jit(solution)/shard_map/all_to_all | solution.py:306
  15.7 1.4 copy-start.2
  17.1 1.4 copy-start.4
  18.5 1.4 copy-start.6
  20.4 1.0 copy-start.13
  21.4 1.1 copy-start.14
  22.5 1.0 copy-start.15
  25.5 79.0 %copy-start.5 = (bf16[1,192,4096]{2,1,0:T(8,128)(2,1)S(1)}, bf16[1,192,4096]{2,1,0:T(8,128)(2,1)}, u32[]{:S(2)}) copy-start(bf16[1,192,4096]{2,1,0:T(8,128)(2,1)} %up_ref.3) | copy-start | bytes 4718596
  25.5 75.7 %all-to-all-start.1 = ((bf16[128,4,1024]{2,1,0:T(4,128)(2,1)}), bf16[128,4,1024]{2,1,0:T(4,128)(2,1)}, u32[]{:S(2)}, u32[]{:S(2)}) async-start(bf16[128,4,1024]{2,1,0:T(4,128)(2,1)} %reshape.83), calls=%async_computation.1 | async-start | bytes 2097152 | tf_op jit(solution)/shard_map/all_to_all | solution.py:323
  45.9 58.6 %copy-start.3 = (bf16[1,192,4096]{2,1,0:T(8,128)(2,1)S(1)}, bf16[1,192,4096]{2,1,0:T(8,128)(2,1)}, u32[]{:S(2)}) copy-start(bf16[1,192,4096]{2,1,0:T(8,128)(2,1)} %gate_ref.3) | copy-start | bytes 4718596
  45.9 135.0 %all-gather.3.cloned.1.call-start = ((), (), s32[]{:S(2)}) async-start(), calls=%async_computation.8 | async-start | bytes 3342336 | tf_op jit(solution)/shard_map/all_gather | solution.py:303
  46.0 57.4 %collective-permute-start = (bf16[576,1024]{1,0:T(8,128)(2,1)}, bf16[576,1024]{1,0:T(8,128)(2,1)}, u32[]{:S(2)}, u32[]{:S(2)}) collective-permute-start(bf16[576,1024]{1,0:T(8,128)(2,1)} %copy-done.15), channel_id=1, source_target_pairs={{0,1},{1,2},{2,3},{3,0},{4,5},{5,6},{6,7},{7,4},{8,9},{9,10},{10,1... | collective-permute-start | bytes 3538952 | tf_op jit(solution)/shard_map/ppermute | solution.py:320
  49.8 53.6 %collective-permute-start.1 = (bf16[576,1024]{1,0:T(8,128)(2,1)}, bf16[576,1024]{1,0:T(8,128)(2,1)}, u32[]{:S(2)}, u32[]{:S(2)}) collective-permute-start(bf16[576,1024]{1,0:T(8,128)(2,1)} %copy-done.14), channel_id=1, source_target_pairs={{0,2},{1,3},{2,0},{3,1},{4,6},{5,7},{6,4},{7,5},{8,10},{9,11},{10,... | collective-permute-start | bytes 3538952 | tf_op jit(solution)/shard_map/ppermute | solution.py:320
  54.1 50.4 %collective-permute-start.2 = (bf16[576,1024]{1,0:T(8,128)(2,1)}, bf16[576,1024]{1,0:T(8,128)(2,1)}, u32[]{:S(2)}, u32[]{:S(2)}) collective-permute-start(bf16[576,1024]{1,0:T(8,128)(2,1)} %copy-done.13), channel_id=1, source_target_pairs={{0,3},{1,0},{2,1},{3,2},{4,7},{5,4},{6,5},{7,6},{8,11},{9,8},{10,9... | collective-permute-start | bytes 3538952 | tf_op jit(solution)/shard_map/ppermute | solution.py:320
  104.5 1.2 copy-start.9
  109.4 1.2 copy-start.8
  110.7 4.8 %copy-start.12 = (s32[4]{0:T(128)S(1)}, s32[4]{0:T(128)}, u32[]{:S(2)}) copy-start(s32[4]{0:T(128)} %node_ref.1) | copy-start | bytes 52
  110.7 22.3 %all-to-all-start.2 = ((bf16[4,384,512]{2,1,0:T(8,128)(2,1)}), bf16[4,384,512]{2,1,0:T(8,128)(2,1)S(1)}, u32[]{:S(2)}, u32[]{:S(2)}) async-start(bf16[4,384,512]{2,1,0:T(8,128)(2,1)} %copy-done.8), calls=%async_computation.2 | async-start | bytes 3145728 | tf_op jit(solution)/shard_map/all_to_all | solution.py:331
  120.1 39.3 %copy-start.7 = (bf16[1,192,4096]{2,1,0:T(8,128)(2,1)S(1)}, bf16[1,192,4096]{2,1,0:T(8,128)(2,1)}, u32[]{:S(2)}) copy-start(bf16[1,192,4096]{2,1,0:T(8,128)(2,1)} %own_ref.1) | copy-start | bytes 4718596
  135.8 27.3 %all-to-all-start.4 = ((bf16[32,2,512]{2,1,0:T(2,128)(2,1)}), bf16[32,2,512]{2,1,0:T(2,128)(2,1)S(1)}, u32[]{:S(2)}, u32[]{:S(2)}) async-start(bf16[32,2,512]{2,1,0:T(2,128)(2,1)} %reshape.98), calls=%async_computation.4 | async-start | bytes 131072 | tf_op jit(solution)/shard_map/all_to_all | solution.py:346
  163.1 17.3 %copy-start.16 = (f32[32,8]{0,1:T(8,128)S(1)}, f32[32,8]{0,1:T(8,128)}, u32[]{:S(2)}) copy-start(f32[32,8]{0,1:T(8,128)} %param.14) | copy-start | bytes 3076
  163.1 68.8 %all-to-all-start.3 = ((bf16[128,4,1024]{2,1,0:T(4,128)(2,1)}), bf16[128,4,1024]{2,1,0:T(4,128)(2,1)}, u32[]{:S(2)}, u32[]{:S(2)}) async-start(bf16[128,4,1024]{2,1,0:T(4,128)(2,1)} %reshape.85), calls=%async_computation.3 | async-start | bytes 2097152 | tf_op jit(solution)/shard_map/all_to_all | solution.py:335
  181.0 1.9 copy-start
  183.3 74.1 %copy-start.1 = (bf16[48,32,1024]{2,1,0:T(8,128)(2,1)S(1)}, bf16[48,32,1024]{2,1,0:T(8,128)(2,1)}, u32[]{:S(2)}) copy-start(bf16[48,32,1024]{2,1,0:T(8,128)(2,1)} %all-gather.3.cloned.1.call-done) | copy-start | bytes 9437188
  234.1 1.2 copy-start.10
  254.1 7.7 %all-to-all-start.5 = ((bf16[4,8,1024]{2,1,0:T(8,128)(2,1)}), bf16[4,8,1024]{2,1,0:T(8,128)(2,1)S(1)}, u32[]{:S(2)}, u32[]{:S(2)}) async-start(bf16[4,8,1024]{2,1,0:T(8,128)(2,1)} %bitcast.6), calls=%async_computation.5 | async-start | bytes 131072 | tf_op jit(solution)/shard_map/all_to_all | solution.py:367
  261.8 10.1 %all-to-all-start.7 = ((f32[8,4,1024]{2,1,0:T(4,128)}), f32[8,4,1024]{2,1,0:T(4,128)S(1)}, u32[]{:S(2)}, u32[]{:S(2)}) async-start(f32[8,4,1024]{2,1,0:T(4,128)} %reshape.94), calls=%async_computation.7 | async-start | bytes 262144 | tf_op jit(solution)/shard_map/all_to_all | solution.py:364
Sparse Core Ops, SparseCore 0:
  57.3 82.4 all-gather.2

commit v3 on v2

v3 whole, which is shorter than its diff:
```python
import functools

import jax
import jax.numpy as jnp
from jax import lax
from jax.experimental import pallas as pl
from jax.experimental.pallas import tpu as pltpu
from jax.sharding import Mesh
from jax.sharding import PartitionSpec as P

EPSILON = 1e-06
Z_SIZE = 16
P_SIZE = 8
CAP = 4
EXPERT = ("z", "p")
F32 = jnp.float32
BF16 = jnp.bfloat16
PARAMS = pltpu.CompilerParams(vmem_limit_bytes=40 * 1024 * 1024)
VMEM = pl.BlockSpec(memory_space=pltpu.VMEM)
SMEM = pl.BlockSpec(memory_space=pltpu.SMEM)


def cost(flops, moved):
    return pl.CostEstimate(flops=flops, bytes_accessed=moved, transcendentals=0)


def norm_kernel(layer_ref, gain_ref, out_ref):
    groups, _, _, part = out_ref.shape
    widened = layer_ref[...].astype(F32)
    inverse = lax.rsqrt(jnp.mean(widened * widened, axis=-1, keepdims=True) + EPSILON)
    normed = (widened * inverse * gain_ref[...].astype(F32)).astype(BF16)
    for j in range(groups):
        out_ref[j, 0] = normed[:, j * part : (j + 1) * part]
        out_ref[j, 1] = layer_ref[:, j * part : (j + 1) * part]


def normed_and_raw(layer_in, norm_gain, groups):
    rows, width = layer_in.shape
    return pl.pallas_call(
        norm_kernel,
        out_shape=jax.ShapeDtypeStruct((groups, 2, rows, width // groups), BF16),
        in_specs=[VMEM] * 2,
        out_specs=VMEM,
        compiler_params=PARAMS,
        cost_estimate=cost(rows * width * 6, rows * width * 6),
        name="norm_pack",
    )(layer_in, norm_gain.reshape(1, width))


def slice_kernel(groups, g_ref, gate_ref, up_ref, down_ref, *refs):
    outs, sems = refs[:-1], refs[-1]
    units = gate_ref.shape[1]
    part = gate_ref.shape[2] // groups
    copies = []
    for s in range(groups):
        lane = pl.multiple_of(lax.rem(g_ref[0] + s, groups) * part, part)
        for k, source in enumerate((gate_ref, up_ref, down_ref)):
            copies.append(
                pltpu.make_async_copy(
                    source.at[0, :, pl.ds(lane, part)],
                    outs[s].at[pl.ds(k * units, units), :],
                    sems.at[s, k],
                )
            )
    for copy in copies:
        copy.start()
    for copy in copies:
        copy.wait()


def weight_pieces(g, gate, up, down, groups):
    _, units, width = gate.shape
    any_space = pl.BlockSpec(memory_space=pltpu.HBM)
    shape = jax.ShapeDtypeStruct((3 * units, width // groups), BF16)
    return pl.pallas_call(
        functools.partial(slice_kernel, groups),
        out_shape=[shape] * groups,
        in_specs=[SMEM] + [any_space] * 3,
        out_specs=[any_space] * groups,
        scratch_shapes=[pltpu.SemaphoreType.DMA((groups, 3))],
        compiler_params=pltpu.CompilerParams(vmem_limit_bytes=60 * 1024 * 1024),
        cost_estimate=cost(0, 6 * units * width * 2),
        name="weight_slices",
    )(g, gate, up, down)


def dot_nt(a, b):
    return lax.dot_general(a, b, (((1,), (1,)), ((), ())), preferred_element_type=F32)


def dot_tn(a, b):
    return lax.dot_general(a, b, (((0,), (0,)), ((), ())), preferred_element_type=F32)


def gate_up_kernel(groups, g_ref, rows_ref, *refs):
    pieces, out_ref = refs[:-1], refs[-1]
    rows = rows_ref[...].reshape(-1, rows_ref.shape[2])
    for s in range(groups):
        home = lax.rem(g_ref[0] + groups - s, groups)
        out_ref[home] = dot_nt(pieces[s][...], rows).astype(BF16)


def gate_up(g, rows, pieces):
    experts, cap, part = rows.shape
    slots = experts * cap
    groups = len(pieces)
    double = pieces[0].shape[0] * 2 // 3
    return pl.pallas_call(
        functools.partial(gate_up_kernel, groups),
        out_shape=jax.ShapeDtypeStruct((groups, double, slots), BF16),
        grid_spec=pltpu.PrefetchScalarGridSpec(
            num_scalar_prefetch=1,
            grid=(1,),
            in_specs=[pl.BlockSpec(rows.shape, lambda i, g_ref: (0, 0, 0))]
            + [pl.BlockSpec((double, part), lambda i, g_ref: (0, 0))] * groups,
            out_specs=pl.BlockSpec((groups, double, slots), lambda i, g_ref: (0, 0, 0)),
        ),
        compiler_params=PARAMS,
        cost_estimate=cost(2 * slots * part * double * groups, 6 << 20),
        name="gate_up",
    )(g, rows, *pieces)


def silu_kernel(acts_ref, out_ref):
    units = out_ref.shape[0]
    gate = jnp.sum(acts_ref[:, :units].astype(F32), axis=0)
    up = jnp.sum(acts_ref[:, units:].astype(F32), axis=0)
    out_ref[...] = (gate / (1.0 + jnp.exp(-gate)) * up).astype(BF16)


def silu(acts):
    _, double, slots = acts.shape
    return pl.pallas_call(
        silu_kernel,
        out_shape=jax.ShapeDtypeStruct((double // 2, slots), BF16),
        in_specs=[VMEM],
        out_specs=VMEM,
        compiler_params=PARAMS,
        cost_estimate=cost(8 * double * slots, 2 << 20),
        name="silu_sum",
    )(acts)


def down_kernel(groups, g_ref, hidden_ref, *refs):
    pieces, out_ref = refs[:-1], refs[-1]
    units, part = pieces[0].shape
    experts, cap, _ = out_ref.shape
    g = g_ref[0]
    chunk = part // 4
    held = [
        hidden_ref[pl.ds(pl.multiple_of(lax.rem(g + groups - s, groups) * units, units), units), :]
        for s in range(groups)
    ]
    for n in range(4):
        columns = slice(n * chunk, (n + 1) * chunk)
        total = dot_tn(held[0], pieces[0][:, columns])
        for s in range(1, groups):
            total += dot_tn(held[s], pieces[s][:, columns])
        out_ref[:, :, columns] = total.astype(BF16).reshape(experts, cap, chunk)


def down(g, hidden, pieces):
    inner, slots = hidden.shape
    groups = len(pieces)
    units, part = inner // groups, pieces[0].shape[1]
    out = (slots // CAP, CAP, part)
    return pl.pallas_call(
        functools.partial(down_kernel, groups),
        out_shape=jax.ShapeDtypeStruct(out, BF16),
        grid_spec=pltpu.PrefetchScalarGridSpec(
            num_scalar_prefetch=1,
            grid=(1,),
            in_specs=[pl.BlockSpec((inner, slots), lambda i, g_ref: (0, 0))]
            + [pl.BlockSpec((units, part), lambda i, g_ref: (2, 0))] * groups,
            out_specs=pl.BlockSpec(out, lambda i, g_ref: (0, 0, 0)),
        ),
        compiler_params=PARAMS,
        cost_estimate=cost(2 * slots * inner * part, 4 << 20),
        name="down",
    )(g, hidden, *pieces)


def combine_kernel(node_ref, table_ref, returned_ref, block_ref, known_ref, out_ref):
    dests, trees, _ = out_ref.shape
    block, part = block_ref.shape
    peers = part // 128
    groups = dests // peers
    tree = block // trees
    zs = known_ref.shape[2] // 2 // 32
    returned = returned_ref[...].reshape(-1, part)
    moe = jnp.dot(table_ref[...], returned, preferred_element_type=F32)
    result = (block_ref[...].astype(F32) + moe).astype(BF16).astype(F32)
    place = lax.broadcasted_iota(jnp.int32, (tree, part), 0)
    chosen = []
    for t in range(trees):
        rows = result[t * tree : (t + 1) * tree]
        chosen.append(jnp.sum(jnp.where(place == node_ref[t], rows, 0.0), axis=0, keepdims=True))
    chosen = jnp.concatenate(chosen, axis=0)
    for p in range(peers):
        parts = [chosen[:, z * peers * 32 + p * 32 : z * peers * 32 + p * 32 + 32] for z in range(zs)]
        high = jnp.concatenate(parts, axis=1).astype(BF16)
        lanes = slice(p * 128, p * 128 + 128)
        for j in range(groups):
            d = p * groups + j
            out_ref[d, :, 0:256] = known_ref[p]
            out_ref[d, :, 256:384] = high
            rows = result[j * tree : (j + 1) * tree, lanes]
            out_ref[d, :, 384:512] = rows[:trees].astype(BF16)
            out_ref[d, :, 512:640] = rows[trees:].astype(BF16)


def combine(nodes, table, returned, block_in, known, dests):
    block, part = block_in.shape
    trees = nodes.shape[0]
    return pl.pallas_call(
        combine_kernel,
        out_shape=jax.ShapeDtypeStruct((dests, trees, 640), BF16),
        in_specs=[SMEM] + [VMEM] * 4,
        out_specs=VMEM,
        compiler_params=PARAMS,
        cost_estimate=cost(2 * block * table.shape[1] * part, 2 << 20),
        name="combine",
    )(nodes, table, returned, block_in, known)


def join_kernel(rows_ref, tiles_ref, weight_ref, out_ref):
    amount, trees, step = tiles_ref.shape
    peers = out_ref.shape[0]
    line = 128
    quarter = weight_ref.shape[0] // trees
    high = jnp.concatenate(
        [rows_ref[:, t * step + 2 * line : t * step + 3 * line] for t in range(trees)], axis=0
    )
    row = lax.broadcasted_iota(jnp.int32, (amount, amount * trees), 0)
    column = lax.broadcasted_iota(jnp.int32, (amount, amount * trees), 1)
    place = lax.rem(column, amount)
    same = (lax.div(column, amount) == lax.rem(row, trees)) & (
        lax.div(place, trees) == lax.div(row, trees)
    )
    total = None
    for q in range(trees):
        chosen = jnp.where(same & (lax.rem(place, trees) == q), 1.0, 0.0).astype(BF16)
        parts = [
            rows_ref[:, q * step : q * step + line],
            rows_ref[:, q * step + line : q * step + 2 * line],
            jnp.dot(chosen, high, preferred_element_type=F32).astype(BF16),
        ]
        for k, values in enumerate(parts):
            weight = weight_ref[q * quarter : (q + 1) * quarter, k].reshape(line, -1)
            product = jnp.dot(values, weight, preferred_element_type=F32)
            total = product if total is None else total + product
    half = total.shape[1] // 2
    for p in range(peers):
        rows = slice(p * trees, (p + 1) * trees)
        pair = jnp.concatenate([total[rows, :half], total[rows, half:]], axis=0)
        out_ref[p, 0 : 2 * trees] = pair.astype(BF16)
        for j in range(trees):
            for h in range(2):
                lanes = slice((3 + h) * line, (4 + h) * line)
                out_ref[p, (2 + h) * trees : (3 + h) * trees, j * line : (j + 1) * line] = (
                    tiles_ref[p * trees + j, :, lanes]
                )


def join(tiles, weight):
    amount, trees, step = tiles.shape
    peers = amount // trees
    width = weight.shape[-1]
    return pl.pallas_call(
        join_kernel,
        out_shape=jax.ShapeDtypeStruct((peers, 4 * trees, width // 2), BF16),
        in_specs=[VMEM] * 3,
        out_specs=VMEM,
        compiler_params=PARAMS,
        cost_estimate=cost(2 * amount * weight.size, 4 << 20),
        name="join",
    )(tiles.reshape(amount, trees * step), tiles, weight)


def finish_kernel(back_ref, layer_ref, joined_ref):
    peers, rows, half = back_ref.shape
    trees = rows // 4
    summed = jnp.sum(back_ref[:, 0 : 2 * trees].astype(F32), axis=0)
    joined_ref[:, :half] = summed[:trees].astype(BF16)
    joined_ref[:, half:] = summed[trees:].astype(BF16)
    for p in range(peers):
        for j in range(trees):
            lane = j * 2 * half + p * 128
            layer_ref[:, lane : lane + 128] = back_ref[
                p, 2 * trees : 4 * trees, j * 128 : (j + 1) * 128
            ]


def finish(back, layer_shape, joined_shape):
    return pl.pallas_call(
        finish_kernel,
        out_shape=[
            jax.ShapeDtypeStruct(layer_shape, BF16),
            jax.ShapeDtypeStruct(joined_shape, BF16),
        ],
        in_specs=[VMEM],
        out_specs=[VMEM] * 2,
        compiler_params=PARAMS,
        cost_estimate=cost(back.size, back.size * 4),
        name="finish",
    )(back)


def route_weights(route_logits):
    exponent = jnp.exp(route_logits)
    return (exponent / jnp.sum(exponent, axis=-1, keepdims=True)).astype(BF16)


def slot_places(route_ids, experts):
    flat_ids = route_ids.reshape(-1)
    amount = flat_ids.shape[0]
    onehot = flat_ids[:, None] == jnp.arange(experts, dtype=jnp.int32)[None, :]
    lower = jnp.arange(amount)[:, None] > jnp.arange(amount)[None, :]
    before = jnp.dot(lower.astype(BF16), onehot.astype(BF16), preferred_element_type=F32)
    rank = jnp.sum(jnp.where(onehot, before, 0.0), axis=1).astype(jnp.int32)
    return flat_ids * CAP + rank


def on_device(
    layer_in,
    norm_gain,
    route_ids,
    route_logits,
    gate_proj,
    up_proj,
    down_proj,
    low_feature,
    mid_feature,
    accepted_node,
    join_weight,
):
    groups = lax.axis_size("y")
    experts = Z_SIZE * P_SIZE
    g = lax.axis_index("y").astype(jnp.int32)
    g_one = g.reshape(1)
    rows_dev, width = layer_in.shape
    block, top = route_ids.shape
    part = width // groups
    slots = experts * CAP
    trees = accepted_node.shape[0]

    join_all = lax.all_gather(join_weight, "z", axis=0, tiled=False)

    both = normed_and_raw(layer_in, norm_gain, groups)
    both = lax.all_to_all(both, "y", 0, 0, tiled=True)
    normed = both[:, 0].reshape(block, part)
    block_in = both[:, 1].reshape(block, part)

    weights = route_weights(route_logits)
    places = slot_places(route_ids, experts)
    slot_ids = jnp.arange(slots, dtype=jnp.int32)
    matches = (places[:, None] == slot_ids[None, :]).reshape(block, top, slots)
    dispatch = jnp.any(matches, axis=1).astype(BF16)
    outgoing = dot_tn(dispatch, normed).astype(BF16).reshape(experts, CAP, part)

    cut = weight_pieces(g_one, gate_proj, up_proj, down_proj, groups)
    outgoing, *cut = lax.optimization_barrier((outgoing, *cut))
    pieces = [
        lax.ppermute(piece, "y", [(j, (j + s) % groups) for j in range(groups)]) if s else piece
        for s, piece in enumerate(cut)
    ]
    received = lax.all_to_all(outgoing, EXPERT, 0, 0, tiled=True)

    combine_table = jnp.sum(
        jnp.where(matches, weights.astype(F32)[:, :, None], 0.0), axis=1
    ).astype(BF16)

    acts = gate_up(g_one, received, pieces)
    acts = lax.all_to_all(acts, "y", 0, 0, tiled=True)
    hidden = silu(acts)
    hidden_all = lax.all_gather(hidden, "y", axis=0, tiled=True)
    expert_out = down(g_one, hidden_all, pieces)
    returned = lax.all_to_all(expert_out, EXPERT, 0, 0, tiled=True)

    own_node = lax.dynamic_slice_in_dim(accepted_node, g, 1, 0)[0]
    feat = width // experts
    z_part = Z_SIZE // groups

    def known(feature):
        row = lax.dynamic_index_in_dim(feature, own_node, 0, keepdims=False)
        row = row.reshape(groups, z_part, P_SIZE, feat).transpose(2, 0, 1, 3)
        return row.reshape(P_SIZE, groups, z_part * feat)

    early = jnp.concatenate([known(low_feature), known(mid_feature)], axis=-1)
    early, combine_table, block_in, returned = lax.optimization_barrier(
        (early, combine_table, block_in, returned)
    )
    sent = combine(accepted_node, combine_table, returned, block_in, early, P_SIZE * groups)
    spread = lax.all_to_all(sent, ("p", "y"), 0, 0, tiled=True)

    back = lax.all_to_all(join(spread, join_all), "p", 0, 0, tiled=True)
    return tuple(finish(back, (rows_dev, width), (trees, part)))


def solution(mesh):
    split = Mesh(mesh.devices.reshape(Z_SIZE, P_SIZE, -1), ("z", "p", "y"))
    every = ("z", "p", "y")
    placed = (
        P(every, None),
        P(),
        P(EXPERT, None),
        P(EXPERT, None),
        P(EXPERT, "y", None),
        P(EXPERT, "y", None),
        P(EXPERT, "y", None),
        P(every, None),
        P(every, None),
        P(EXPERT),
        P(None, EXPERT, "y"),
    )
    return jax.shard_map(
        on_device,
        mesh=split,
        in_specs=placed,
        out_specs=(P(every, None), P(EXPERT, "y")),
        check_vma=False,
    )
```

time: 281 us -> 392 us (1.40)
  Pallas kernels: 9.95 us -> 153 us
  blocking collectives: 29.3 us -> 60.5 us
  starting transfers between devices: 78.1 us -> 56.4 us
  waiting for transfers between devices: 115 us -> 94.8 us
  local copies, waits for them, and re-layouts: 27.7 us -> 8.76 us
    pallas_call x1, Pallas kernels: 0.43 us -> 144 us  [weight_pieces(): pl.pallas_call(functools.partial(slice_kernel, groups), out_shape=[shape]...]
    ppermute x3, waiting for transfers between devices: 1.13 us -> 47.3 us  [on_device(): lax.ppermute(piece, 'y', [(j, (j + s) % groups) for j in range(groups)])]
    all_to_all x1, waiting for transfers between devices: 44 us -> 0.01 us  [on_device(): received = lax.all_to_all(outgoing, EXPERT, 0, 0, tiled=True)]
    all_to_all x1 -> x3, blocking collectives: 17 us -> 48 us  [the longest x1 23.6 us: on_device(): acts = lax.all_to_all(acts, 'y', 0, 0, tiled=True)]
    all_to_all x5 -> x1, waiting for transfers between devices: 70.2 us -> 47.5 us  [on_device(): returned = lax.all_to_all(expert_out, EXPERT, 0, 0, tiled=True)]
    all_to_all x5 -> x1, starting transfers between devices: 41.5 us -> 19.8 us  [on_device(): returned = lax.all_to_all(expert_out, EXPERT, 0, 0, tiled=True)]
    unnamed x40 -> x18, local copies, waits for them, and re-layouts: 15.9 us -> 4.64 us
    reshape x6 -> x4, local copies, waits for them, and re-layouts: 6.35 us -> 0.35 us  [the longest x2 0.18 us: known(): return row.reshape(P_SIZE, groups, z_part * feat)]
  transfers between devices with their start and end apart: 11 -> 7, of which waited for: 6 -> 4; matrix products, arithmetic and copies ran while one was open for 4% -> 1% of each run, Pallas kernels for 3% -> 39%
where the time goes in v3:
time: 392 us; the launch traced here: 391 us
  Pallas kernels  153 us (39%)
  waiting for transfers between devices  94.8 us (24%)
  blocking collectives  60.5 us (15%)
  starting transfers between devices  56.4 us (14%)
  between operations  16.2 us (4%)
  local copies, waits for them, and re-layouts  8.76 us (2%)
    pallas_call x1, Pallas kernels, weight_pieces(): pl.pallas_call(functools.partial(slice_kernel, groups), out_shape=[shape]...  144 us
    all_to_all x1, waiting for transfers between devices, on_device(): returned = lax.all_to_all(expert_out, EXPERT, 0, 0, tiled=True)  47.5 us
    ppermute x3, waiting for transfers between devices, on_device(): lax.ppermute(piece, 'y', [(j, (j + s) % groups) for j in range(groups)])  47.3 us
    all_to_all x1, blocking collectives, on_device(): acts = lax.all_to_all(acts, 'y', 0, 0, tiled=True)  23.6 us
    all_to_all x1, starting transfers between devices, on_device(): received = lax.all_to_all(outgoing, EXPERT, 0, 0, tiled=True)  20.4 us
    all_to_all x1, starting transfers between devices, on_device(): returned = lax.all_to_all(expert_out, EXPERT, 0, 0, tiled=True)  19.8 us
    all_to_all x1, blocking collectives, on_device(): spread = lax.all_to_all(sent, ('p', 'y'), 0, 0, tiled=True)  16.3 us
    all_gather x1, blocking collectives, on_device(): hidden_all = lax.all_gather(hidden, 'y', axis=0, tiled=True)  12.4 us
  transfers between devices with their start and end apart: 7, of which 4 were waited for; matrix products, arithmetic and copies ran while one was open for 1% of the time, Pallas kernels for 39%

profile of v3, /device:TPU:1, one launch (start us, length us, event | category | flops | bytes accessed | tf_op | source)
XLA Modules:
  0.0 391.0 jit_solution(16049502443309954926)
XLA Ops:
  7.2 0.7 reshape.57.gain_ref
  7.9 0.0 copy-start.3
  7.9 0.8 copy-done.3
  8.7 0.8 norm_pack.1
  9.5 5.0 %all-to-all-start = ((bf16[4,2,8,1024]{3,2,1,0:T(8,128)(2,1)}), bf16[4,2,8,1024]{3,2,1,0:T(8,128)(2,1)S(1)}, u32[]{:S(2)}, u32[]{:S(2)}) async-start(bf16[4,2,8,1024]{3,2,1,0:T(8,128)(2,1)} %norm_pack.1), calls=%async_computation | async-start | bytes 262144 | tf_op jit(solution)/shard_map/all_to_all | solution.py:350
  14.5 0.8 copy.27
  15.3 0.1 eq.29
  15.4 0.2 fusion
  15.6 0.1 convert_element_type.26
  15.7 144.2 %weight_slices.1 = (bf16[576,1024]{1,0:T(8,128)(2,1)}, bf16[576,1024]{1,0:T(8,128)(2,1)}, bf16[576,1024]{1,0:T(8,128)(2,1)}, bf16[576,1024]{1,0:T(8,128)(2,1)}) custom-call(s32[1]{0:T(128)} %bitcast.4.g_ref, bf16[1,192,4096]{2,1,0:T(8,128)(2,1)} %gate_ref.1, bf16[1,192,4096]{2,1,0:T(8,128)(2,1)} %up_ref.1, bf16[1,192,4096]{2,1,0:T(8,128)(2,1)} %down_ref.1), custom_call_target="tpu_custom_call" | custom-call | bytes 9437184 | tf_op jit(solution)/shard_map/weight_slices/pallas_call | solution.py:75
  159.9 0.2 fusion.1
  160.1 0.0 all-to-all-done
  160.1 0.5 convolution_convert_fusion
  160.6 0.1 copy-done.5
  160.8 1.2 reshape.59
  162.0 20.4 %all-to-all-start.1 = ((bf16[128,4,1024]{2,1,0:T(4,128)(2,1)}), bf16[128,4,1024]{2,1,0:T(4,128)(2,1)}, u32[]{:S(2)}, u32[]{:S(2)}) async-start(bf16[128,4,1024]{2,1,0:T(4,128)(2,1)} %reshape.59), calls=%async_computation.1 | async-start | bytes 2097152 | tf_op jit(solution)/shard_map/all_to_all | solution.py:367
  182.4 0.0 all-gather.3.cloned.1.call-start
  182.5 3.7 collective-permute-start
  186.1 4.3 %collective-permute-start.1 = (bf16[576,1024]{1,0:T(8,128)(2,1)}, bf16[576,1024]{1,0:T(8,128)(2,1)S(1)}, u32[]{:S(2)}, u32[]{:S(2)}) collective-permute-start(bf16[576,1024]{1,0:T(8,128)(2,1)} %get-tuple-element.22), channel_id=1, source_target_pairs={{0,2},{1,3},{2,0},{3,1},{4,6},{5,7},{6,4},{7,5},{8,10},{9,11},{10,... | collective-permute-start | bytes 3538952 | tf_op jit(solution)/shard_map/ppermute | solution.py:364
  190.4 3.1 collective-permute-start.2
  193.5 0.0 all-gather.3.cloned.1.call-update
  193.6 19.4 %collective-permute-done.refs_1_ = bf16[576,1024]{1,0:T(8,128)(2,1)S(1)} collective-permute-done((bf16[576,1024]{1,0:T(8,128)(2,1)}, bf16[576,1024]{1,0:T(8,128)(2,1)S(1)}, u32[]{:S(2)}, u32[]{:S(2)}) %collective-permute-start) | collective-permute-done | bytes 1179680 | tf_op jit(solution)/shard_map/ppermute | solution.py:364
  213.0 26.1 %collective-permute-done.1.refs_2_ = bf16[576,1024]{1,0:T(8,128)(2,1)S(1)} collective-permute-done((bf16[576,1024]{1,0:T(8,128)(2,1)}, bf16[576,1024]{1,0:T(8,128)(2,1)S(1)}, u32[]{:S(2)}, u32[]{:S(2)}) %collective-permute-start.1) | collective-permute-done | bytes 1179680 | tf_op jit(solution)/shard_map/ppermute | solution.py:364
  239.1 1.7 collective-permute-done.2.refs_3_
  240.8 0.0 all-to-all-done.1.rows_ref
  240.8 3.3 gate_up.1
  244.1 23.6 %all_to_all.30.acts_ref = bf16[4,384,512]{2,1,0:T(8,128)(2,1)S(1)} all-to-all(bf16[4,384,512]{2,1,0:T(8,128)(2,1)S(1)} %gate_up.1), channel_id=1, replica_groups=mesh['z'=16,'p'=8,'y'=4] {'y'}, dimensions={0} | all-to-all | bytes 3145728 | tf_op jit(solution)/shard_map/all_to_all | solution.py:374
  267.7 0.3 silu_sum.1
  268.0 12.4 %all_gather.9.hidden_ref = bf16[768,512]{1,0:T(8,128)(2,1)S(1)} all-gather(bf16[192,512]{1,0:T(8,128)(2,1)S(1)} %silu_sum.1), channel_id=1, replica_groups=mesh['z'=16,'p'=8,'y'=4] {'y'}, dimensions={0}, use_global_device_ids=true | all-gather | bytes 983040 | tf_op jit(solution)/shard_map/all_gather | solution.py:376
  280.5 2.3 down.1
  282.8 1.0 copy-done.1
  283.7 19.8 %all-to-all-start.3 = ((bf16[128,4,1024]{2,1,0:T(4,128)(2,1)}), bf16[128,4,1024]{2,1,0:T(4,128)(2,1)S(1)}, u32[]{:S(2)}, u32[]{:S(2)}) async-start(bf16[128,4,1024]{2,1,0:T(4,128)(2,1)} %copy-done.1), calls=%async_computation.3 | async-start | bytes 2097152 | tf_op jit(solution)/shard_map/all_to_all | solution.py:378
  303.6 0.6 dynamic_slice.10
  306.1 1.0 dynamic-slice_reduce_fusion
  307.1 0.1 reshape.55
  307.2 0.1 reshape.56
  307.3 0.1 reshape.53
  307.4 0.1 reshape.54
  307.5 0.1 copy.29
  307.6 0.2 select_reduce_fusion.table_ref
  307.9 47.5 %all-to-all-done.3.returned_ref = bf16[128,4,1024]{2,1,0:T(4,128)(2,1)S(1)} async-done(((bf16[128,4,1024]{2,1,0:T(4,128)(2,1)}), bf16[128,4,1024]{2,1,0:T(4,128)(2,1)S(1)}, u32[]{:S(2)}, u32[]{:S(2)}) %all-to-all-start.3) | async-done | bytes 1048608 | tf_op jit(solution)/shard_map/all_to_all | solution.py:378
  355.4 0.9 combine.1
  356.4 16.3 %all_to_all.31.tiles_ref = bf16[32,4,640]{2,1,0:T(4,128)(2,1)S(1)} all-to-all(bf16[32,4,640]{2,1,0:T(4,128)(2,1)S(1)} %combine.1), channel_id=1, replica_groups=mesh['z'=16,'p'=8,'y'=4] {'p','y'}, dimensions={0} | all-to-all | bytes 327680 | tf_op jit(solution)/shard_map/all_to_all | solution.py:394
  372.6 0.0 all-gather.3.cloned.1.call-done
  372.7 1.9 copy-done.2
  374.6 0.8 join.1
  375.4 8.2 %all_to_all.32.back_ref = bf16[8,16,512]{2,1,0:T(8,128)(2,1)S(1)} all-to-all(bf16[8,16,512]{2,1,0:T(8,128)(2,1)S(1)} %join.1), channel_id=1, replica_groups=mesh['z'=16,'p'=8,'y'=4] {'p'}, dimensions={0} | all-to-all | bytes 262144 | tf_op jit(solution)/shard_map/all_to_all | solution.py:396
  383.5 0.6 finish.1
  (20 shorter events, 0.1 us)
Async XLA Ops:
  7.9 0.8 copy-start.3
  9.5 150.6 %all-to-all-start = ((bf16[4,2,8,1024]{3,2,1,0:T(8,128)(2,1)}), bf16[4,2,8,1024]{3,2,1,0:T(8,128)(2,1)S(1)}, u32[]{:S(2)}, u32[]{:S(2)}) async-start(bf16[4,2,8,1024]{3,2,1,0:T(8,128)(2,1)} %norm_pack.1), calls=%async_computation | async-start | bytes 262144 | tf_op jit(solution)/shard_map/all_to_all | solution.py:350
  160.1 0.6 copy-start.5
  162.0 78.9 %copy-start = (bf16[576,1024]{1,0:T(8,128)(2,1)S(1)}, bf16[576,1024]{1,0:T(8,128)(2,1)}, u32[]{:S(2)}) copy-start(bf16[576,1024]{1,0:T(8,128)(2,1)} %get-tuple-element.20.refs_0_) | copy-start | bytes 3538948
  162.0 78.9 %all-to-all-start.1 = ((bf16[128,4,1024]{2,1,0:T(4,128)(2,1)}), bf16[128,4,1024]{2,1,0:T(4,128)(2,1)}, u32[]{:S(2)}, u32[]{:S(2)}) async-start(bf16[128,4,1024]{2,1,0:T(4,128)(2,1)} %reshape.59), calls=%async_computation.1 | async-start | bytes 2097152 | tf_op jit(solution)/shard_map/all_to_all | solution.py:367
  182.4 190.2 %all-gather.3.cloned.1.call-start = ((), (), s32[]{:S(2)}) async-start(), calls=%async_computation.6 | async-start | bytes 3342336 | tf_op jit(solution)/shard_map/all_gather | solution.py:347
  182.5 30.5 %collective-permute-start = (bf16[576,1024]{1,0:T(8,128)(2,1)}, bf16[576,1024]{1,0:T(8,128)(2,1)S(1)}, u32[]{:S(2)}, u32[]{:S(2)}) collective-permute-start(bf16[576,1024]{1,0:T(8,128)(2,1)} %get-tuple-element.21), channel_id=1, source_target_pairs={{0,1},{1,2},{2,3},{3,0},{4,5},{5,6},{6,7},{7,4},{8,9},{9,10},{10,1... | collective-permute-start | bytes 3538952 | tf_op jit(solution)/shard_map/ppermute | solution.py:364
  186.1 53.0 %collective-permute-start.1 = (bf16[576,1024]{1,0:T(8,128)(2,1)}, bf16[576,1024]{1,0:T(8,128)(2,1)S(1)}, u32[]{:S(2)}, u32[]{:S(2)}) collective-permute-start(bf16[576,1024]{1,0:T(8,128)(2,1)} %get-tuple-element.22), channel_id=1, source_target_pairs={{0,2},{1,3},{2,0},{3,1},{4,6},{5,7},{6,4},{7,5},{8,10},{9,11},{10,... | collective-permute-start | bytes 3538952 | tf_op jit(solution)/shard_map/ppermute | solution.py:364
  190.4 50.4 %collective-permute-start.2 = (bf16[576,1024]{1,0:T(8,128)(2,1)}, bf16[576,1024]{1,0:T(8,128)(2,1)}, u32[]{:S(2)}, u32[]{:S(2)}) collective-permute-start(bf16[576,1024]{1,0:T(8,128)(2,1)} %get-tuple-element.23), channel_id=1, source_target_pairs={{0,3},{1,0},{2,1},{3,2},{4,7},{5,4},{6,5},{7,6},{8,11},{9,8},{10,9... | collective-permute-start | bytes 3538952 | tf_op jit(solution)/shard_map/ppermute | solution.py:364
  282.7 1.0 copy-start.1
  283.7 19.8 %copy-start.4 = (s32[4]{0:T(128)S(1)}, s32[4]{0:T(128)}, u32[]{:S(2)}) copy-start(s32[4]{0:T(128)} %node_ref.1) | copy-start | bytes 52
  283.7 23.8 %copy-start.7 = (f32[32,8]{0,1:T(8,128)S(1)}, f32[32,8]{0,1:T(8,128)}, u32[]{:S(2)}) copy-start(f32[32,8]{0,1:T(8,128)} %param.14) | copy-start | bytes 3076
  283.7 24.1 %copy-start.6 = (bf16[4,2,8,1024]{3,2,1,0:T(8,128)(2,1)S(1)}, bf16[4,2,8,1024]{3,2,1,0:T(8,128)(2,1)}, u32[]{:S(2)}) copy-start(bf16[4,2,8,1024]{3,2,1,0:T(8,128)(2,1)} %copy-done.5) | copy-start | bytes 393220
  283.7 71.7 %all-to-all-start.3 = ((bf16[128,4,1024]{2,1,0:T(4,128)(2,1)}), bf16[128,4,1024]{2,1,0:T(4,128)(2,1)S(1)}, u32[]{:S(2)}, u32[]{:S(2)}) async-start(bf16[128,4,1024]{2,1,0:T(4,128)(2,1)} %copy-done.1), calls=%async_computation.3 | async-start | bytes 2097152 | tf_op jit(solution)/shard_map/all_to_all | solution.py:378
  372.7 1.9 copy-start.2
Sparse Core Ops, SparseCore 0:
  193.7 82.6 all-gather.2

commit v4 on v3

--- a/solution.py
+++ b/solution.py
@@ -20,6 +20,10 @@
 SMEM = pl.BlockSpec(memory_space=pltpu.SMEM)
 
 
+def shift_y(array, groups, shift):
+    return lax.ppermute(array, "y", [(j, (j + shift) % groups) for j in range(groups)])
+
+
 def cost(flops, moved):
     return pl.CostEstimate(flops=flops, bytes_accessed=moved, transcendentals=0)
 
@@ -28,7 +32,8 @@
     groups, _, _, part = out_ref.shape
     widened = layer_ref[...].astype(F32)
     inverse = lax.rsqrt(jnp.mean(widened * widened, axis=-1, keepdims=True) + EPSILON)
-    normed = (widened * inverse * gain_ref[...].astype(F32)).astype(BF16)
+    gain = gain_ref[...].reshape(1, -1).astype(F32)
+    normed = (widened * inverse * gain).astype(BF16)
     for j in range(groups):
         out_ref[j, 0] = normed[:, j * part : (j + 1) * part]
         out_ref[j, 1] = layer_ref[:, j * part : (j + 1) * part]
@@ -44,22 +49,23 @@
         compiler_params=PARAMS,
         cost_estimate=cost(rows * width * 6, rows * width * 6),
         name="norm_pack",
-    )(layer_in, norm_gain.reshape(1, width))
-
-
-def slice_kernel(groups, g_ref, gate_ref, up_ref, down_ref, *refs):
-    outs, sems = refs[:-1], refs[-1]
-    units = gate_ref.shape[1]
-    part = gate_ref.shape[2] // groups
+    )(layer_in, norm_gain)
+
+
+def slice_kernel(shifts, groups, g_ref, *refs):
+    count = len(refs) - 1 - len(shifts)
+    sources, outs, sems = refs[:count], refs[count:-1], refs[-1]
+    _, units, width = sources[0].shape
+    part = width // groups
     copies = []
-    for s in range(groups):
+    for i, s in enumerate(shifts):
         lane = pl.multiple_of(lax.rem(g_ref[0] + s, groups) * part, part)
-        for k, source in enumerate((gate_ref, up_ref, down_ref)):
+        for k, source in enumerate(sources):
             copies.append(
                 pltpu.make_async_copy(
                     source.at[0, :, pl.ds(lane, part)],
-                    outs[s].at[pl.ds(k * units, units), :],
-                    sems.at[s, k],
+                    outs[i].at[pl.ds(k * units, units), :],
+                    sems.at[i, k],
                 )
             )
     for copy in copies:
@@ -68,20 +74,42 @@
         copy.wait()
 
 
-def weight_pieces(g, gate, up, down, groups):
-    _, units, width = gate.shape
-    any_space = pl.BlockSpec(memory_space=pltpu.HBM)
-    shape = jax.ShapeDtypeStruct((3 * units, width // groups), BF16)
-    return pl.pallas_call(
-        functools.partial(slice_kernel, groups),
-        out_shape=[shape] * groups,
-        in_specs=[SMEM] + [any_space] * 3,
-        out_specs=[any_space] * groups,
-        scratch_shapes=[pltpu.SemaphoreType.DMA((groups, 3))],
+def weight_slices(g, sources, shifts, groups, name):
+    _, units, width = sources[0].shape
+    count = len(sources)
+    shape = jax.ShapeDtypeStruct((count * units, width // groups), BF16)
+    moved = 2 * len(shifts) * count * units * width // groups * 2
+    return pl.pallas_call(
+        functools.partial(slice_kernel, shifts, groups),
+        out_shape=[shape] * len(shifts),
+        in_specs=[SMEM] + [pl.BlockSpec(memory_space=pltpu.HBM)] * count,
+        out_specs=[VMEM] * len(shifts),
+        scratch_shapes=[pltpu.SemaphoreType.DMA((len(shifts), count))],
         compiler_params=pltpu.CompilerParams(vmem_limit_bytes=60 * 1024 * 1024),
-        cost_estimate=cost(0, 6 * units * width * 2),
-        name="weight_slices",
-    )(g, gate, up, down)
+        cost_estimate=cost(0, moved),
+        name=name,
+    )(g, *sources)
+
+
+def dispatch_kernel(table_ref, both_ref, out_ref):
+    part = both_ref.shape[3]
+    normed = both_ref[:, 0].reshape(-1, part)
+    rows = dot_tn(table_ref[...], normed).astype(BF16)
+    out_ref[...] = rows.reshape(out_ref.shape)
+
+
+def dispatch_rows(table, both):
+    part = both.shape[3]
+    slots = table.shape[1]
+    return pl.pallas_call(
+        dispatch_kernel,
+        out_shape=jax.ShapeDtypeStruct((slots // CAP, CAP, part), BF16),
+        in_specs=[VMEM] * 2,
+        out_specs=VMEM,
+        compiler_params=PARAMS,
+        cost_estimate=cost(2 * table.size * part, 2 * slots * part),
+        name="dispatch",
+    )(table, both)
 
 
 def dot_nt(a, b):
@@ -104,7 +132,7 @@
     experts, cap, part = rows.shape
     slots = experts * cap
     groups = len(pieces)
-    double = pieces[0].shape[0] * 2 // 3
+    double = pieces[0].shape[0]
     return pl.pallas_call(
         functools.partial(gate_up_kernel, groups),
         out_shape=jax.ShapeDtypeStruct((groups, double, slots), BF16),
@@ -171,7 +199,7 @@
             num_scalar_prefetch=1,
             grid=(1,),
             in_specs=[pl.BlockSpec((inner, slots), lambda i, g_ref: (0, 0))]
-            + [pl.BlockSpec((units, part), lambda i, g_ref: (2, 0))] * groups,
+            + [pl.BlockSpec((units, part), lambda i, g_ref: (0, 0))] * groups,
             out_specs=pl.BlockSpec(out, lambda i, g_ref: (0, 0, 0)),
         ),
         compiler_params=PARAMS,
@@ -348,7 +376,6 @@
 
     both = normed_and_raw(layer_in, norm_gain, groups)
     both = lax.all_to_all(both, "y", 0, 0, tiled=True)
-    normed = both[:, 0].reshape(block, part)
     block_in = both[:, 1].reshape(block, part)
 
     weights = route_weights(route_logits)
@@ -356,25 +383,29 @@
     slot_ids = jnp.arange(slots, dtype=jnp.int32)
     matches = (places[:, None] == slot_ids[None, :]).reshape(block, top, slots)
     dispatch = jnp.any(matches, axis=1).astype(BF16)
-    outgoing = dot_tn(dispatch, normed).astype(BF16).reshape(experts, CAP, part)
-
-    cut = weight_pieces(g_one, gate_proj, up_proj, down_proj, groups)
+    outgoing = dispatch_rows(dispatch, both)
+
+    others = tuple(range(1, groups))
+    both_in = [gate_proj, up_proj]
+    cut = weight_slices(g_one, both_in, others, groups, "gate_up_slices")
     outgoing, *cut = lax.optimization_barrier((outgoing, *cut))
-    pieces = [
-        lax.ppermute(piece, "y", [(j, (j + s) % groups) for j in range(groups)]) if s else piece
-        for s, piece in enumerate(cut)
-    ]
+    gate_up_pieces = [shift_y(piece, groups, s) for s, piece in zip(others, cut)]
+    cut = weight_slices(g_one, [down_proj], others, groups, "down_slices")
+    down_pieces = [shift_y(piece, groups, s) for s, piece in zip(others, cut)]
+    gate_up_pieces = [*weight_slices(g_one, both_in, (0,), groups, "gate_up_own"), *gate_up_pieces]
+    down_pieces = [*weight_slices(g_one, [down_proj], (0,), groups, "down_own"), *down_pieces]
     received = lax.all_to_all(outgoing, EXPERT, 0, 0, tiled=True)
 
     combine_table = jnp.sum(
         jnp.where(matches, weights.astype(F32)[:, :, None], 0.0), axis=1
     ).astype(BF16)
 
-    acts = gate_up(g_one, received, pieces)
+    acts = gate_up(g_one, received, gate_up_pieces)
+    acts, *down_pieces = lax.optimization_barrier((acts, *down_pieces))
     acts = lax.all_to_all(acts, "y", 0, 0, tiled=True)
     hidden = silu(acts)
     hidden_all = lax.all_gather(hidden, "y", axis=0, tiled=True)
-    expert_out = down(g_one, hidden_all, pieces)
+    expert_out = down(g_one, hidden_all, down_pieces)
     returned = lax.all_to_all(expert_out, EXPERT, 0, 0, tiled=True)
 
     own_node = lax.dynamic_slice_in_dim(accepted_node, g, 1, 0)[0]
@@ -387,8 +418,8 @@
         return row.reshape(P_SIZE, groups, z_part * feat)
 
     early = jnp.concatenate([known(low_feature), known(mid_feature)], axis=-1)
-    early, combine_table, block_in, returned = lax.optimization_barrier(
-        (early, combine_table, block_in, returned)
+    early, combine_table, block_in, join_all, returned = lax.optimization_barrier(
+        (early, combine_table, block_in, join_all, returned)
     )
     sent = combine(accepted_node, combine_table, returned, block_in, early, P_SIZE * groups)
     spread = lax.all_to_all(sent, ("p", "y"), 0, 0, tiled=True)

time: 392 us -> 247 us (0.63)
  Pallas kernels: 153 us -> 19.7 us
  waiting for transfers between devices: 94.8 us -> 77.2 us
  starting transfers between devices: 56.4 us -> 63.5 us
    pallas_call x1 -> x5, Pallas kernels: 144 us -> 10.8 us  [the longest x4 9.34 us: weight_slices(): pl.pallas_call(functools.partial(slice_kernel, shifts, groups), out_shape...]
    ppermute x3 -> x6, waiting for transfers between devices: 47.3 us -> 19.9 us  [shift_y(): lax.ppermute(array, 'y', [(j, (j + shift) % groups) for j in range(groups)])]
    all_to_all x1, waiting for transfers between devices: 0.01 us -> 9.53 us  [on_device(): received = lax.all_to_all(outgoing, EXPERT, 0, 0, tiled=True)]
    ppermute x3 -> x6, starting transfers between devices: 11 us -> 17 us  [shift_y(): lax.ppermute(array, 'y', [(j, (j + shift) % groups) for j in range(groups)])]
  transfers between devices with their start and end apart: 7 -> 10, of which waited for: 4 -> 7; matrix products, arithmetic and copies ran while one was open for 1% -> 2% of each run, Pallas kernels for 39% -> 6%
where the time goes in v4:
time: 247 us; the launch traced here: 246 us
  waiting for transfers between devices  77.2 us (31%)
  starting transfers between devices  63.5 us (26%)
  blocking collectives  59.9 us (24%)
  Pallas kernels  19.7 us (8%)
  between operations  16.2 us (7%)
  local copies, waits for them, and re-layouts  8.42 us (3%)
    all_to_all x1, waiting for transfers between devices, on_device(): returned = lax.all_to_all(expert_out, EXPERT, 0, 0, tiled=True)  47.5 us
    all_to_all x1, blocking collectives, on_device(): acts = lax.all_to_all(acts, 'y', 0, 0, tiled=True)  24.2 us
    all_to_all x1, starting transfers between devices, on_device(): received = lax.all_to_all(outgoing, EXPERT, 0, 0, tiled=True)  21 us
    all_to_all x1, starting transfers between devices, on_device(): returned = lax.all_to_all(expert_out, EXPERT, 0, 0, tiled=True)  20.4 us
    ppermute x6, waiting for transfers between devices, shift_y(): lax.ppermute(array, 'y', [(j, (j + shift) % groups) for j in range(groups)])  19.9 us
    ppermute x6, starting transfers between devices, shift_y(): lax.ppermute(array, 'y', [(j, (j + shift) % groups) for j in range(groups)])  17 us
    all_to_all x1, blocking collectives, on_device(): spread = lax.all_to_all(sent, ('p', 'y'), 0, 0, tiled=True)  15.9 us
    all_gather x1, blocking collectives, on_device(): hidden_all = lax.all_gather(hidden, 'y', axis=0, tiled=True)  11.6 us
  transfers between devices with their start and end apart: 10, of which 7 were waited for; matrix products, arithmetic and copies ran while one was open for 2% of the time, Pallas kernels for 6%

profile of v4, /device:TPU:1, one launch (start us, length us, event | category | flops | bytes accessed | tf_op | source)
XLA Modules:
  0.0 245.7 jit_solution(14700518480236597085)
XLA Ops:
  7.2 0.8 copy-done.3
  8.0 0.7 copy-done.4
  8.7 0.8 norm_pack.1
  9.5 5.0 %all-to-all-start = ((bf16[4,2,8,1024]{3,2,1,0:T(8,128)(2,1)}), bf16[4,2,8,1024]{3,2,1,0:T(8,128)(2,1)S(1)}, u32[]{:S(2)}, u32[]{:S(2)}) async-start(bf16[4,2,8,1024]{3,2,1,0:T(8,128)(2,1)} %norm_pack.1), calls=%async_computation | async-start | bytes 262144 | tf_op jit(solution)/shard_map/all_to_all | solution.py:378
  14.5 0.8 copy.27
  15.3 0.1 eq.29
  15.3 0.2 fusion
  15.7 0.2 fusion.1
  15.9 3.1 %gate_up_slices.1 = (bf16[384,1024]{1,0:T(8,128)(2,1)}, bf16[384,1024]{1,0:T(8,128)(2,1)}, bf16[384,1024]{1,0:T(8,128)(2,1)}) custom-call(s32[1]{0:T(128)} %bitcast.5.g_ref, bf16[1,192,4096]{2,1,0:T(8,128)(2,1)} %refs_0_.5, bf16[1,192,4096]{2,1,0:T(8,128)(2,1)} %refs_1_.3), custom_call_target="tpu_custom_call" | custom-call | bytes 4718592 | tf_op jit(solution)/shard_map/gate_up_slices/pallas_call | solution.py:82
  19.1 0.3 all-to-all-done.both_ref
  19.3 1.4 dispatch.1
  20.8 21.0 %all-to-all-start.1 = ((bf16[128,4,1024]{2,1,0:T(4,128)(2,1)}), bf16[128,4,1024]{2,1,0:T(4,128)(2,1)S(1)}, u32[]{:S(2)}, u32[]{:S(2)}) async-start(bf16[128,4,1024]{2,1,0:T(4,128)(2,1)} %dispatch.1), calls=%async_computation.1 | async-start | bytes 2097152 | tf_op jit(solution)/shard_map/all_to_all | solution.py:397
  41.8 2.2 collective-permute-start
  44.1 4.3 %collective-permute-start.1 = (bf16[384,1024]{1,0:T(8,128)(2,1)}, bf16[384,1024]{1,0:T(8,128)(2,1)}, u32[]{:S(2)}, u32[]{:S(2)}) collective-permute-start(bf16[384,1024]{1,0:T(8,128)(2,1)} %get-tuple-element.27), channel_id=1, source_target_pairs={{0,2},{1,3},{2,0},{3,1},{4,6},{5,7},{6,4},{7,5},{8,10},{9,11},{10,... | collective-permute-start | bytes 2359304 | tf_op jit(solution)/shard_map/ppermute | solution.py:24
  48.4 3.1 %collective-permute-start.2 = (bf16[384,1024]{1,0:T(8,128)(2,1)}, bf16[384,1024]{1,0:T(8,128)(2,1)}, u32[]{:S(2)}, u32[]{:S(2)}) collective-permute-start(bf16[384,1024]{1,0:T(8,128)(2,1)} %get-tuple-element.28), channel_id=1, source_target_pairs={{0,3},{1,0},{2,1},{3,2},{4,7},{5,4},{6,5},{7,6},{8,11},{9,8},{10,9... | collective-permute-start | bytes 2359304 | tf_op jit(solution)/shard_map/ppermute | solution.py:24
  51.5 2.3 down_slices.1
  53.8 2.2 collective-permute-start.3
  56.0 2.8 %collective-permute-start.4 = (bf16[192,1024]{1,0:T(8,128)(2,1)}, bf16[192,1024]{1,0:T(8,128)(2,1)S(1)}, u32[]{:S(2)}, u32[]{:S(2)}) collective-permute-start(bf16[192,1024]{1,0:T(8,128)(2,1)} %get-tuple-element.30), channel_id=1, source_target_pairs={{0,2},{1,3},{2,0},{3,1},{4,6},{5,7},{6,4},{7,5},{8,10},{9,11},{10,... | collective-permute-start | bytes 1179656 | tf_op jit(solution)/shard_map/ppermute | solution.py:24
  58.8 4.5 %collective-permute-done.refs_1_ = bf16[384,1024]{1,0:T(8,128)(2,1)S(1)} collective-permute-done((bf16[384,1024]{1,0:T(8,128)(2,1)}, bf16[384,1024]{1,0:T(8,128)(2,1)S(1)}, u32[]{:S(2)}, u32[]{:S(2)}) %collective-permute-start) | collective-permute-done | bytes 786464 | tf_op jit(solution)/shard_map/ppermute | solution.py:24
  63.3 0.9 copy-done.6
  64.2 2.3 collective-permute-start.5
  66.6 2.1 gate_up_own.1.refs_0_
  68.7 1.8 down_own.1.refs_0_
  70.5 9.9 %collective-permute-done.1.refs_2_ = bf16[384,1024]{1,0:T(8,128)(2,1)} collective-permute-done((bf16[384,1024]{1,0:T(8,128)(2,1)}, bf16[384,1024]{1,0:T(8,128)(2,1)}, u32[]{:S(2)}, u32[]{:S(2)}) %collective-permute-start.1) | collective-permute-done | bytes 786464 | tf_op jit(solution)/shard_map/ppermute | solution.py:24
  80.4 3.7 %collective-permute-done.2.refs_3_ = bf16[384,1024]{1,0:T(8,128)(2,1)} collective-permute-done((bf16[384,1024]{1,0:T(8,128)(2,1)}, bf16[384,1024]{1,0:T(8,128)(2,1)}, u32[]{:S(2)}, u32[]{:S(2)}) %collective-permute-start.2) | collective-permute-done | bytes 786464 | tf_op jit(solution)/shard_map/ppermute | solution.py:24
  84.1 9.5 %all-to-all-done.1.rows_ref = bf16[128,4,1024]{2,1,0:T(4,128)(2,1)S(1)} async-done(((bf16[128,4,1024]{2,1,0:T(4,128)(2,1)}), bf16[128,4,1024]{2,1,0:T(4,128)(2,1)S(1)}, u32[]{:S(2)}, u32[]{:S(2)}) %all-to-all-start.1) | async-done | bytes 1048608 | tf_op jit(solution)/shard_map/all_to_all | solution.py:397
  93.6 1.1 copy-done.7
  94.8 3.2 %gate_up.1 = bf16[4,384,512]{2,1,0:T(8,128)(2,1)S(1)} custom-call(s32[1]{0:T(128)} %bitcast.5.g_ref, bf16[128,4,1024]{2,1,0:T(4,128)(2,1)S(1)} %all-to-all-done.1.rows_ref, bf16[384,1024]{1,0:T(8,128)(2,1)S(1)} %copy-done.2, bf16[384,1024]{1,0:T(8,128)(2,1)S(1)} %copy-done.7, bf16[384,1024]{1,0:T(8,128)(2,1)} %collective-permute-done.1.refs_2_, ...), custom_call_target="tpu_custom_call" | custom-call | flops 1610612736 | bytes 6291456 | tf_op jit(solution)/shard_map/gate_up/pallas_call | solution.py:136
  98.0 1.8 collective-permute-done.5.refs_3_
  99.8 24.2 %all_to_all.30.acts_ref = bf16[4,384,512]{2,1,0:T(8,128)(2,1)S(1)} all-to-all(bf16[4,384,512]{2,1,0:T(8,128)(2,1)S(1)} %gate_up.1), channel_id=1, replica_groups=mesh['z'=16,'p'=8,'y'=4] {'y'}, dimensions={0} | all-to-all | bytes 3145728 | tf_op jit(solution)/shard_map/all_to_all | solution.py:405
  124.0 0.3 silu_sum.1
  124.3 11.6 %all_gather.11.hidden_ref = bf16[768,512]{1,0:T(8,128)(2,1)S(1)} all-gather(bf16[192,512]{1,0:T(8,128)(2,1)S(1)} %silu_sum.1), channel_id=1, replica_groups=mesh['z'=16,'p'=8,'y'=4] {'y'}, dimensions={0}, use_global_device_ids=true | all-gather | bytes 983040 | tf_op jit(solution)/shard_map/all_gather | solution.py:407
  135.9 2.3 down.1
  138.2 20.4 %all-to-all-start.3 = ((bf16[128,4,1024]{2,1,0:T(4,128)(2,1)}), bf16[128,4,1024]{2,1,0:T(4,128)(2,1)S(1)}, u32[]{:S(2)}, u32[]{:S(2)}) async-start(bf16[128,4,1024]{2,1,0:T(4,128)(2,1)} %down.1), calls=%async_computation.3 | async-start | bytes 2097152 | tf_op jit(solution)/shard_map/all_to_all | solution.py:409
  158.7 0.6 dynamic_slice.10
  161.2 1.0 dynamic-slice_reduce_fusion
  162.2 0.1 reshape.47
  162.3 0.1 reshape.48
  162.4 0.1 reshape.49
  162.5 0.1 reshape.50
  162.7 0.2 select_reduce_fusion.table_ref
  163.0 47.5 %all-to-all-done.3.returned_ref = bf16[128,4,1024]{2,1,0:T(4,128)(2,1)S(1)} async-done(((bf16[128,4,1024]{2,1,0:T(4,128)(2,1)}), bf16[128,4,1024]{2,1,0:T(4,128)(2,1)S(1)}, u32[]{:S(2)}, u32[]{:S(2)}) %all-to-all-start.3) | async-done | bytes 1048608 | tf_op jit(solution)/shard_map/all_to_all | solution.py:409
  210.5 0.9 combine.1
  211.4 15.9 %all_to_all.31.tiles_ref = bf16[32,4,640]{2,1,0:T(4,128)(2,1)S(1)} all-to-all(bf16[32,4,640]{2,1,0:T(4,128)(2,1)S(1)} %combine.1), channel_id=1, replica_groups=mesh['z'=16,'p'=8,'y'=4] {'p','y'}, dimensions={0} | all-to-all | bytes 327680 | tf_op jit(solution)/shard_map/all_to_all | solution.py:425
  227.4 1.9 copy-done
  229.3 0.8 join.1
  230.1 8.2 %all_to_all.32.back_ref = bf16[8,16,512]{2,1,0:T(8,128)(2,1)S(1)} all-to-all(bf16[8,16,512]{2,1,0:T(8,128)(2,1)S(1)} %join.1), channel_id=1, replica_groups=mesh['z'=16,'p'=8,'y'=4] {'p'}, dimensions={0} | all-to-all | bytes 262144 | tf_op jit(solution)/shard_map/all_to_all | solution.py:427
  238.2 0.6 finish.1
  (30 shorter events, 0.4 us)
Async XLA Ops:
  7.2 0.8 copy-start.3
  8.0 0.7 copy-start.4
  9.5 9.8 %all-to-all-start = ((bf16[4,2,8,1024]{3,2,1,0:T(8,128)(2,1)}), bf16[4,2,8,1024]{3,2,1,0:T(8,128)(2,1)S(1)}, u32[]{:S(2)}, u32[]{:S(2)}) async-start(bf16[4,2,8,1024]{3,2,1,0:T(8,128)(2,1)} %norm_pack.1), calls=%async_computation | async-start | bytes 262144 | tf_op jit(solution)/shard_map/all_to_all | solution.py:378
  20.8 72.9 %all-to-all-start.1 = ((bf16[128,4,1024]{2,1,0:T(4,128)(2,1)}), bf16[128,4,1024]{2,1,0:T(4,128)(2,1)S(1)}, u32[]{:S(2)}, u32[]{:S(2)}) async-start(bf16[128,4,1024]{2,1,0:T(4,128)(2,1)} %dispatch.1), calls=%async_computation.1 | async-start | bytes 2097152 | tf_op jit(solution)/shard_map/all_to_all | solution.py:397
  41.8 121.2 %all-gather.3.cloned.1.call-start = ((), (), s32[]{:S(2)}) async-start(), calls=%async_computation.6 | async-start | bytes 3342336 | tf_op jit(solution)/shard_map/all_gather | solution.py:375
  41.8 21.5 %collective-permute-start = (bf16[384,1024]{1,0:T(8,128)(2,1)}, bf16[384,1024]{1,0:T(8,128)(2,1)S(1)}, u32[]{:S(2)}, u32[]{:S(2)}) collective-permute-start(bf16[384,1024]{1,0:T(8,128)(2,1)} %get-tuple-element.26), channel_id=1, source_target_pairs={{0,1},{1,2},{2,3},{3,0},{4,5},{5,6},{6,7},{7,4},{8,9},{9,10},{10,1... | collective-permute-start | bytes 2359304 | tf_op jit(solution)/shard_map/ppermute | solution.py:24
  44.1 36.3 %collective-permute-start.1 = (bf16[384,1024]{1,0:T(8,128)(2,1)}, bf16[384,1024]{1,0:T(8,128)(2,1)}, u32[]{:S(2)}, u32[]{:S(2)}) collective-permute-start(bf16[384,1024]{1,0:T(8,128)(2,1)} %get-tuple-element.27), channel_id=1, source_target_pairs={{0,2},{1,3},{2,0},{3,1},{4,6},{5,7},{6,4},{7,5},{8,10},{9,11},{10,... | collective-permute-start | bytes 2359304 | tf_op jit(solution)/shard_map/ppermute | solution.py:24
  48.4 35.7 %collective-permute-start.2 = (bf16[384,1024]{1,0:T(8,128)(2,1)}, bf16[384,1024]{1,0:T(8,128)(2,1)}, u32[]{:S(2)}, u32[]{:S(2)}) collective-permute-start(bf16[384,1024]{1,0:T(8,128)(2,1)} %get-tuple-element.28), channel_id=1, source_target_pairs={{0,3},{1,0},{2,1},{3,2},{4,7},{5,4},{6,5},{7,6},{8,11},{9,8},{10,9... | collective-permute-start | bytes 2359304 | tf_op jit(solution)/shard_map/ppermute | solution.py:24
  53.8 44.2 %collective-permute-start.3 = (bf16[192,1024]{1,0:T(8,128)(2,1)}, bf16[192,1024]{1,0:T(8,128)(2,1)S(1)}, u32[]{:S(2)}, u32[]{:S(2)}) collective-permute-start(bf16[192,1024]{1,0:T(8,128)(2,1)} %get-tuple-element.29), channel_id=1, source_target_pairs={{0,1},{1,2},{2,3},{3,0},{4,5},{5,6},{6,7},{7,4},{8,9},{9,10},{10,1... | collective-permute-start | bytes 1179656 | tf_op jit(solution)/shard_map/ppermute | solution.py:24
  56.0 42.0 %collective-permute-start.4 = (bf16[192,1024]{1,0:T(8,128)(2,1)}, bf16[192,1024]{1,0:T(8,128)(2,1)S(1)}, u32[]{:S(2)}, u32[]{:S(2)}) collective-permute-start(bf16[192,1024]{1,0:T(8,128)(2,1)} %get-tuple-element.30), channel_id=1, source_target_pairs={{0,2},{1,3},{2,0},{3,1},{4,6},{5,7},{6,4},{7,5},{8,10},{9,11},{10,... | collective-permute-start | bytes 1179656 | tf_op jit(solution)/shard_map/ppermute | solution.py:24
  63.3 0.9 copy-start.6
  64.2 35.6 %collective-permute-start.5 = (bf16[192,1024]{1,0:T(8,128)(2,1)}, bf16[192,1024]{1,0:T(8,128)(2,1)S(1)}, u32[]{:S(2)}, u32[]{:S(2)}) collective-permute-start(bf16[192,1024]{1,0:T(8,128)(2,1)} %get-tuple-element.31), channel_id=1, source_target_pairs={{0,3},{1,0},{2,1},{3,2},{4,7},{5,4},{6,5},{7,6},{8,11},{9,8},{10,9... | collective-permute-start | bytes 1179656 | tf_op jit(solution)/shard_map/ppermute | solution.py:24
  68.7 25.0 %copy-start.2 = (bf16[384,1024]{1,0:T(8,128)(2,1)S(1)}, bf16[384,1024]{1,0:T(8,128)(2,1)}, u32[]{:S(2)}) copy-start(bf16[384,1024]{1,0:T(8,128)(2,1)} %gate_up_own.1.refs_0_) | copy-start | bytes 2359300
  93.6 1.1 copy-start.7
  124.0 11.9 %copy-start.1 = (bf16[192,1024]{1,0:T(8,128)(2,1)S(1)}, bf16[192,1024]{1,0:T(8,128)(2,1)}, u32[]{:S(2)}) copy-start(bf16[192,1024]{1,0:T(8,128)(2,1)} %down_own.1.refs_0_) | copy-start | bytes 1179652
  138.2 20.5 %copy-start.5 = (s32[4]{0:T(128)S(1)}, s32[4]{0:T(128)}, u32[]{:S(2)}) copy-start(s32[4]{0:T(128)} %node_ref.1) | copy-start | bytes 52
  138.2 24.4 %copy-start.8 = (f32[32,8]{0,1:T(8,128)S(1)}, f32[32,8]{0,1:T(8,128)}, u32[]{:S(2)}) copy-start(f32[32,8]{0,1:T(8,128)} %param.14) | copy-start | bytes 3076
  138.2 72.3 %all-to-all-start.3 = ((bf16[128,4,1024]{2,1,0:T(4,128)(2,1)}), bf16[128,4,1024]{2,1,0:T(4,128)(2,1)S(1)}, u32[]{:S(2)}, u32[]{:S(2)}) async-start(bf16[128,4,1024]{2,1,0:T(4,128)(2,1)} %down.1), calls=%async_computation.3 | async-start | bytes 2097152 | tf_op jit(solution)/shard_map/all_to_all | solution.py:409
  227.4 1.9 copy-start
Sparse Core Ops, SparseCore 0:
  66.7 85.9 all-gather.2

commit v5 on v4

v5 whole, which is shorter than its diff:
```python
import functools

import jax
import jax.numpy as jnp
from jax import lax
from jax.experimental import pallas as pl
from jax.experimental.pallas import tpu as pltpu
from jax.sharding import Mesh
from jax.sharding import PartitionSpec as P

EPSILON = 1e-06
Z_SIZE = 16
P_SIZE = 8
CAP = 4
EXPERT = ("z", "p")
LINE = 128
F32 = jnp.float32
BF16 = jnp.bfloat16
PARAMS = pltpu.CompilerParams(vmem_limit_bytes=40 * 1024 * 1024)
VMEM = pl.BlockSpec(memory_space=pltpu.VMEM)
SMEM = pl.BlockSpec(memory_space=pltpu.SMEM)


def shift_y(array, groups, shift):
    return lax.ppermute(array, "y", [(j, (j + shift) % groups) for j in range(groups)])


def cost(flops, moved):
    return pl.CostEstimate(flops=flops, bytes_accessed=moved, transcendentals=0)


def prepare_kernel(g_ref, layer_ref, gain_ref, ids_ref, logits_ref, out_ref, table_ref):
    dests, rows, step = out_ref.shape
    part = step - 2 * LINE
    groups = layer_ref.shape[1] // part
    top, block = ids_ref.shape
    widened = layer_ref[...].astype(F32)
    inverse = lax.rsqrt(jnp.mean(widened * widened, axis=-1, keepdims=True) + EPSILON)
    gain = gain_ref[...].reshape(1, -1).astype(F32)
    normed = (widened * inverse * gain).astype(BF16)

    exponent = jnp.exp(logits_ref[...])
    share = exponent / jnp.sum(exponent, axis=0, keepdims=True)
    expert = lax.broadcasted_iota(jnp.int32, (LINE, block), 0)
    named = jnp.zeros((LINE, block), F32)
    weight = jnp.zeros((LINE, block), F32)
    for k in range(top):
        same = expert == ids_ref[k : k + 1, :]
        named = jnp.where(same, 1.0, named)
        weight = jnp.where(same, share[k : k + 1, :], weight)
    first = lax.broadcasted_iota(jnp.int32, (block, block), 0)
    second = lax.broadcasted_iota(jnp.int32, (block, block), 1)
    earlier = jnp.where(first < second, 1.0, 0.0).astype(BF16)
    before = jnp.dot(named.astype(BF16), earlier, preferred_element_type=F32)
    ranked = jnp.where(named > 0.0, before + 1.0, 0.0).astype(BF16)
    square = (LINE, LINE)
    unit = lax.broadcasted_iota(jnp.int32, square, 0) == lax.broadcasted_iota(jnp.int32, square, 1)
    unit = jnp.where(unit, 1.0, 0.0).astype(BF16)
    table_ref[:, :LINE] = dot_tn(ranked, unit)
    table_ref[:, LINE:] = dot_tn(weight.astype(BF16), unit)
    own = table_ref[pl.ds(pl.multiple_of(g_ref[0] * rows, rows), rows), :].astype(BF16)
    for d in range(dests):
        j = d % groups
        out_ref[d, :, :part] = normed[:, j * part : (j + 1) * part]
        out_ref[d, :, part:] = own


def prepare(g, layer_in, norm_gain, ids, logits, groups):
    rows, width = layer_in.shape
    shape = (P_SIZE * groups, rows, width // groups + 2 * LINE)
    return pl.pallas_call(
        prepare_kernel,
        out_shape=jax.ShapeDtypeStruct(shape, BF16),
        in_specs=[SMEM] + [VMEM] * 4,
        out_specs=VMEM,
        scratch_shapes=[pltpu.VMEM((ids.shape[1], 2 * LINE), F32)],
        compiler_params=PARAMS,
        cost_estimate=cost(rows * width * 6, 2 << 20),
        name="prepare",
    )(g, layer_in, norm_gain, ids, logits)


def slice_kernel(shifts, groups, g_ref, *refs):
    count = len(refs) - 1 - len(shifts)
    sources, outs, sems = refs[:count], refs[count:-1], refs[-1]
    _, units, width = sources[0].shape
    part = width // groups
    copies = []
    for i, s in enumerate(shifts):
        lane = pl.multiple_of(lax.rem(g_ref[0] + s, groups) * part, part)
        for k, source in enumerate(sources):
            copies.append(
                pltpu.make_async_copy(
                    source.at[0, :, pl.ds(lane, part)],
                    outs[i].at[pl.ds(k * units, units), :],
                    sems.at[i, k],
                )
            )
    for copy in copies:
        copy.start()
    for copy in copies:
        copy.wait()


def weight_slices(g, sources, shifts, groups, name):
    _, units, width = sources[0].shape
    count = len(sources)
    shape = jax.ShapeDtypeStruct((count * units, width // groups), BF16)
    moved = 2 * len(shifts) * count * units * width // groups * 2
    return pl.pallas_call(
        functools.partial(slice_kernel, shifts, groups),
        out_shape=[shape] * len(shifts),
        in_specs=[SMEM] + [pl.BlockSpec(memory_space=pltpu.HBM)] * count,
        out_specs=[VMEM] * len(shifts),
        scratch_shapes=[pltpu.SemaphoreType.DMA((len(shifts), count))],
        compiler_params=pltpu.CompilerParams(vmem_limit_bytes=60 * 1024 * 1024),
        cost_estimate=cost(0, moved),
        name=name,
    )(g, *sources)


def dispatch_kernel(p_ref, tokens_ref, out_ref, combine_ref):
    z_size, per_z, part = out_ref.shape
    amount, slots = combine_ref.shape
    tokens = tokens_ref[...].reshape(amount, -1)
    block = amount // P_SIZE
    expert = lax.broadcasted_iota(jnp.int32, (LINE, slots), 0)
    column = lax.broadcasted_iota(jnp.int32, (LINE, slots), 1)
    chosen = expert == lax.div(column, per_z) * P_SIZE + p_ref[0]
    chosen = jnp.where(chosen, 1.0, 0.0).astype(BF16)
    rank = jnp.dot(tokens[:, part : part + LINE], chosen, preferred_element_type=F32)
    weight = jnp.dot(tokens[:, part + LINE :], chosen, preferred_element_type=F32)
    token = lax.broadcasted_iota(jnp.int32, (amount, slots), 0)
    column = lax.broadcasted_iota(jnp.int32, (amount, slots), 1)
    wanted = lax.rem(column, CAP) + 1
    match = (rank == wanted.astype(F32)) & (
        lax.div(token, block) == lax.rem(lax.div(column, CAP), P_SIZE)
    )
    combine_ref[...] = jnp.where(match, weight, 0.0).astype(BF16)
    onehot = jnp.where(match, 1.0, 0.0).astype(BF16)
    out_ref[...] = dot_tn(onehot, tokens[:, :part]).astype(BF16).reshape(out_ref.shape)


def dispatch_rows(p, tokens):
    sources, rows, step = tokens.shape
    part = step - 2 * LINE
    per_z = P_SIZE * CAP
    slots = Z_SIZE * per_z
    return pl.pallas_call(
        dispatch_kernel,
        out_shape=[
            jax.ShapeDtypeStruct((Z_SIZE, per_z, part), BF16),
            jax.ShapeDtypeStruct((sources * rows, slots), BF16),
        ],
        in_specs=[SMEM, VMEM],
        out_specs=[VMEM] * 2,
        compiler_params=PARAMS,
        cost_estimate=cost(2 * slots * sources * rows * part, 2 * slots * part),
        name="dispatch",
    )(p, tokens)


def dot_nt(a, b):
    return lax.dot_general(a, b, (((1,), (1,)), ((), ())), preferred_element_type=F32)


def dot_tn(a, b):
    return lax.dot_general(a, b, (((0,), (0,)), ((), ())), preferred_element_type=F32)


def gate_up_kernel(groups, g_ref, rows_ref, *refs):
    pieces, out_ref = refs[:-1], refs[-1]
    rows = rows_ref[...].reshape(-1, rows_ref.shape[2])
    for s in range(groups):
        home = lax.rem(g_ref[0] + groups - s, groups)
        out_ref[home] = dot_nt(pieces[s][...], rows).astype(BF16)


def gate_up(g, rows, pieces):
    z_size, per_z, part = rows.shape
    slots = z_size * per_z
    groups = len(pieces)
    double = pieces[0].shape[0]
    return pl.pallas_call(
        functools.partial(gate_up_kernel, groups),
        out_shape=jax.ShapeDtypeStruct((groups, double, slots), BF16),
        grid_spec=pltpu.PrefetchScalarGridSpec(
            num_scalar_prefetch=1,
            grid=(1,),
            in_specs=[pl.BlockSpec(rows.shape, lambda i, g_ref: (0, 0, 0))]
            + [pl.BlockSpec((double, part), lambda i, g_ref: (0, 0))] * groups,
            out_specs=pl.BlockSpec((groups, double, slots), lambda i, g_ref: (0, 0, 0)),
        ),
        compiler_params=PARAMS,
        cost_estimate=cost(2 * slots * part * double * groups, 6 << 20),
        name="gate_up",
    )(g, rows, *pieces)


def silu_kernel(acts_ref, out_ref):
    units = out_ref.shape[0]
    gate = jnp.sum(acts_ref[:, :units].astype(F32), axis=0)
    up = jnp.sum(acts_ref[:, units:].astype(F32), axis=0)
    out_ref[...] = (gate / (1.0 + jnp.exp(-gate)) * up).astype(BF16)


def silu(acts):
    _, double, slots = acts.shape
    return pl.pallas_call(
        silu_kernel,
        out_shape=jax.ShapeDtypeStruct((double // 2, slots), BF16),
        in_specs=[VMEM],
        out_specs=VMEM,
        compiler_params=PARAMS,
        cost_estimate=cost(8 * double * slots, 2 << 20),
        name="silu_sum",
    )(acts)


def down_kernel(groups, g_ref, hidden_ref, *refs):
    pieces, out_ref = refs[:-1], refs[-1]
    units, part = pieces[0].shape
    z_size, per_z, _ = out_ref.shape
    g = g_ref[0]
    chunk = part // 4
    held = [
        hidden_ref[pl.ds(pl.multiple_of(lax.rem(g + groups - s, groups) * units, units), units), :]
        for s in range(groups)
    ]
    for n in range(4):
        columns = slice(n * chunk, (n + 1) * chunk)
        total = dot_tn(held[0], pieces[0][:, columns])
        for s in range(1, groups):
            total += dot_tn(held[s], pieces[s][:, columns])
        out_ref[:, :, columns] = total.astype(BF16).reshape(z_size, per_z, chunk)


def down(g, hidden, pieces):
    inner, slots = hidden.shape
    groups = len(pieces)
    units, part = inner // groups, pieces[0].shape[1]
    out = (Z_SIZE, slots // Z_SIZE, part)
    return pl.pallas_call(
        functools.partial(down_kernel, groups),
        out_shape=jax.ShapeDtypeStruct(out, BF16),
        grid_spec=pltpu.PrefetchScalarGridSpec(
            num_scalar_prefetch=1,
            grid=(1,),
            in_specs=[pl.BlockSpec((inner, slots), lambda i, g_ref: (0, 0))]
            + [pl.BlockSpec((units, part), lambda i, g_ref: (0, 0))] * groups,
            out_specs=pl.BlockSpec(out, lambda i, g_ref: (0, 0, 0)),
        ),
        compiler_params=PARAMS,
        cost_estimate=cost(2 * slots * inner * part, 4 << 20),
        name="down",
    )(g, hidden, *pieces)


def column_kernel(table_ref, returned_ref, out_ref):
    returned = returned_ref[...].reshape(-1, out_ref.shape[2])
    moe = jnp.dot(table_ref[...], returned, preferred_element_type=F32)
    out_ref[...] = moe.astype(BF16).reshape(out_ref.shape)


def column_sum(table, returned):
    amount, slots = table.shape
    part = returned.shape[2]
    return pl.pallas_call(
        column_kernel,
        out_shape=jax.ShapeDtypeStruct((P_SIZE, amount // P_SIZE, part), BF16),
        in_specs=[VMEM] * 2,
        out_specs=VMEM,
        compiler_params=PARAMS,
        cost_estimate=cost(2 * amount * slots * part, 2 << 20),
        name="column_sum",
    )(table, returned)


def combine_kernel(node_ref, parts_ref, known_ref, out_ref):
    dests, trees, _ = out_ref.shape
    _, block, part = parts_ref.shape
    groups = dests // P_SIZE
    tree = block // trees
    zs = LINE // 32
    result = jnp.sum(parts_ref[...].astype(F32), axis=0)
    place = lax.broadcasted_iota(jnp.int32, (tree, part), 0)
    chosen = []
    for t in range(trees):
        rows = result[t * tree : (t + 1) * tree]
        chosen.append(jnp.sum(jnp.where(place == node_ref[t], rows, 0.0), axis=0, keepdims=True))
    chosen = jnp.concatenate(chosen, axis=0)
    for p in range(P_SIZE):
        first = [(z * P_SIZE + p) * 32 for z in range(zs)]
        high = jnp.concatenate([chosen[:, f : f + 32] for f in first], axis=1).astype(BF16)
        lanes = slice(p * LINE, (p + 1) * LINE)
        for j in range(groups):
            d = p * groups + j
            out_ref[d, :, : 3 * LINE] = known_ref[p]
            out_ref[d, :, 3 * LINE : 4 * LINE] = high
            rows = result[j * tree : (j + 1) * tree, lanes]
            out_ref[d, :, 4 * LINE : 5 * LINE] = rows[:trees].astype(BF16)
            out_ref[d, :, 5 * LINE :] = rows[trees:].astype(BF16)


def combine(nodes, parts, known, dests):
    trees = nodes.shape[0]
    return pl.pallas_call(
        combine_kernel,
        out_shape=jax.ShapeDtypeStruct((dests, trees, 6 * LINE), BF16),
        in_specs=[SMEM] + [VMEM] * 2,
        out_specs=VMEM,
        compiler_params=PARAMS,
        cost_estimate=cost(parts.size * 2, 1 << 20),
        name="combine",
    )(nodes, parts, known)


def join_kernel(rows_ref, tiles_ref, weight_ref, out_ref):
    amount, trees, step = tiles_ref.shape
    quarter = weight_ref.shape[0] // trees

    def lanes_of(t, k):
        return slice(t * step + k * LINE, t * step + (k + 1) * LINE)

    high = jnp.concatenate([rows_ref[:, lanes_of(t, 3)] for t in range(trees)], axis=0)
    row = lax.broadcasted_iota(jnp.int32, (amount, amount * trees), 0)
    column = lax.broadcasted_iota(jnp.int32, (amount, amount * trees), 1)
    place = lax.rem(column, amount)
    same = (lax.div(column, amount) == lax.rem(row, trees)) & (
        lax.div(place, trees) == lax.div(row, trees)
    )
    total = None
    for q in range(trees):
        chosen = jnp.where(same & (lax.rem(place, trees) == q), 1.0, 0.0).astype(BF16)
        moe = jnp.dot(chosen, high, preferred_element_type=F32)
        parts = [
            rows_ref[:, lanes_of(q, 0)],
            rows_ref[:, lanes_of(q, 1)],
            (rows_ref[:, lanes_of(q, 2)].astype(F32) + moe).astype(BF16),
        ]
        for k, values in enumerate(parts):
            weight = weight_ref[q * quarter : (q + 1) * quarter, k].reshape(LINE, -1)
            product = jnp.dot(values, weight, preferred_element_type=F32)
            total = product if total is None else total + product
    half = total.shape[1] // 2
    for p in range(P_SIZE):
        rows = slice(p * trees, (p + 1) * trees)
        pair = jnp.concatenate([total[rows, :half], total[rows, half:]], axis=0)
        out_ref[p, 0 : 2 * trees] = pair.astype(BF16)
        for j in range(trees):
            for h in range(2):
                out_ref[p, (2 + h) * trees : (3 + h) * trees, j * LINE : (j + 1) * LINE] = (
                    tiles_ref[p * trees + j, :, (4 + h) * LINE : (5 + h) * LINE]
                )


def join(tiles, weight):
    amount, trees, step = tiles.shape
    peers = amount // trees
    width = weight.shape[-1]
    return pl.pallas_call(
        join_kernel,
        out_shape=jax.ShapeDtypeStruct((peers, 4 * trees, width // 2), BF16),
        in_specs=[VMEM] * 3,
        out_specs=VMEM,
        compiler_params=PARAMS,
        cost_estimate=cost(2 * amount * weight.size, 4 << 20),
        name="join",
    )(tiles.reshape(amount, trees * step), tiles, weight)


def finish_kernel(back_ref, layer_in_ref, layer_ref, joined_ref):
    peers, rows, half = back_ref.shape
    trees = rows // 4
    summed = jnp.sum(back_ref[:, 0 : 2 * trees].astype(F32), axis=0)
    joined_ref[:, :half] = summed[:trees].astype(BF16)
    joined_ref[:, half:] = summed[trees:].astype(BF16)
    for p in range(peers):
        for j in range(trees):
            lane = j * 2 * half + p * LINE
            moe = back_ref[p, 2 * trees : 4 * trees, j * LINE : (j + 1) * LINE].astype(F32)
            own = layer_in_ref[:, lane : lane + LINE].astype(F32)
            layer_ref[:, lane : lane + LINE] = (own + moe).astype(BF16)


def finish(back, layer_in, joined_shape):
    return pl.pallas_call(
        finish_kernel,
        out_shape=[
            jax.ShapeDtypeStruct(layer_in.shape, BF16),
            jax.ShapeDtypeStruct(joined_shape, BF16),
        ],
        in_specs=[VMEM] * 2,
        out_specs=[VMEM] * 2,
        compiler_params=PARAMS,
        cost_estimate=cost(back.size, back.size * 4),
        name="finish",
    )(back, layer_in)


def on_device(
    layer_in,
    norm_gain,
    route_ids,
    route_logits,
    gate_proj,
    up_proj,
    down_proj,
    low_feature,
    mid_feature,
    accepted_node,
    join_weight,
):
    groups = lax.axis_size("y")
    g = lax.axis_index("y").astype(jnp.int32)
    g_one = g.reshape(1)
    p_one = lax.axis_index("p").astype(jnp.int32).reshape(1)
    width = layer_in.shape[1]
    part = width // groups
    trees = accepted_node.shape[0]

    join_all = lax.all_gather(join_weight, "z", axis=0, tiled=False)

    tokens = prepare(g_one, layer_in, norm_gain, route_ids.T, route_logits.T, groups)
    tokens = lax.all_to_all(tokens, ("p", "y"), 0, 0, tiled=True)
    outgoing, table = dispatch_rows(p_one, tokens)

    others = tuple(range(1, groups))
    both_in = [gate_proj, up_proj]
    cut = weight_slices(g_one, both_in, others, groups, "gate_up_slices")
    outgoing, *cut = lax.optimization_barrier((outgoing, *cut))
    gate_up_pieces = [shift_y(piece, groups, s) for s, piece in zip(others, cut)]
    cut = weight_slices(g_one, [down_proj], others, groups, "down_slices")
    down_pieces = [shift_y(piece, groups, s) for s, piece in zip(others, cut)]
    gate_up_pieces = [*weight_slices(g_one, both_in, (0,), groups, "gate_up_own"), *gate_up_pieces]
    down_pieces = [*weight_slices(g_one, [down_proj], (0,), groups, "down_own"), *down_pieces]
    received = lax.all_to_all(outgoing, "z", 0, 0, tiled=True)

    acts = gate_up(g_one, received, gate_up_pieces)
    acts, *down_pieces = lax.optimization_barrier((acts, *down_pieces))
    acts = lax.all_to_all(acts, "y", 0, 0, tiled=True)
    hidden = silu(acts)
    hidden_all = lax.all_gather(hidden, "y", axis=0, tiled=True)
    expert_out = down(g_one, hidden_all, down_pieces)
    returned = lax.all_to_all(expert_out, "z", 0, 0, tiled=True)

    own_node = lax.dynamic_slice_in_dim(accepted_node, g, 1, 0)[0]
    feat = width // (Z_SIZE * P_SIZE)
    z_part = Z_SIZE // groups

    def known(feature):
        row = lax.dynamic_index_in_dim(feature, own_node, 0, keepdims=False)
        row = row.reshape(groups, z_part, P_SIZE, feat).transpose(2, 0, 1, 3)
        return row.reshape(P_SIZE, groups, z_part * feat)

    early = jnp.concatenate([known(f) for f in (low_feature, mid_feature, layer_in)], axis=-1)
    early, table, join_all, returned = lax.optimization_barrier((early, table, join_all, returned))
    parts = lax.all_to_all(column_sum(table, returned), "p", 0, 0, tiled=True)

    sent = combine(accepted_node, parts, early, P_SIZE * groups)
    spread = lax.all_to_all(sent, ("p", "y"), 0, 0, tiled=True)

    back = lax.all_to_all(join(spread, join_all), "p", 0, 0, tiled=True)
    return tuple(finish(back, layer_in, (trees, part)))


def solution(mesh):
    split = Mesh(mesh.devices.reshape(Z_SIZE, P_SIZE, -1), ("z", "p", "y"))
    every = ("z", "p", "y")
    placed = (
        P(every, None),
        P(),
        P(EXPERT, None),
        P(EXPERT, None),
        P(EXPERT, "y", None),
        P(EXPERT, "y", None),
        P(EXPERT, "y", None),
        P(every, None),
        P(every, None),
        P(EXPERT),
        P(None, EXPERT, "y"),
    )
    return jax.shard_map(
        on_device,
        mesh=split,
        in_specs=placed,
        out_specs=(P(every, None), P(EXPERT, "y")),
        check_vma=False,
    )
```

time: 247 us -> 251 us (1.016)
  blocking collectives: 59.9 us -> 74.4 us
  starting transfers between devices: 63.5 us -> 52.3 us
    all_to_all x0 -> x1, blocking collectives: none -> 17.8 us  [on_device(): parts = lax.all_to_all(column_sum(table, returned), 'p', 0, 0, tiled=True)]
    all_to_all x3, starting transfers between devices: 46.5 us -> 35.1 us  [the longest x1 13 us: on_device(): received = lax.all_to_all(outgoing, 'z', 0, 0, tiled=True)]
    all_to_all x1, blocking collectives: 15.9 us -> 12.6 us  [on_device(): spread = lax.all_to_all(sent, ('p', 'y'), 0, 0, tiled=True)]
    ppermute x6, waiting for transfers between devices: 19.9 us -> 22.5 us  [shift_y(): lax.ppermute(array, 'y', [(j, (j + shift) % groups) for j in range(groups)])]
    unnamed x20 -> x23, local copies, waits for them, and re-layouts: 6.22 us -> 5.02 us
  transfers between devices with their start and end apart: 10 -> 10, of which waited for: 7 -> 8; matrix products, arithmetic and copies ran while one was open for 2% -> 1% of each run, Pallas kernels for 6% -> 6%
where the time goes in v5:
time: 251 us; the launch traced here: 250 us
  waiting for transfers between devices  79.2 us (32%)
  blocking collectives  74.4 us (30%)
  starting transfers between devices  52.3 us (21%)
  Pallas kernels  20.6 us (8%)
  between operations  16.2 us (6%)
  local copies, waits for them, and re-layouts  7.23 us (3%)
    all_to_all x1, waiting for transfers between devices, on_device(): returned = lax.all_to_all(expert_out, 'z', 0, 0, tiled=True)  40.8 us
    all_to_all x1, blocking collectives, on_device(): acts = lax.all_to_all(acts, 'y', 0, 0, tiled=True)  24 us
    ppermute x6, waiting for transfers between devices, shift_y(): lax.ppermute(array, 'y', [(j, (j + shift) % groups) for j in range(groups)])  22.5 us
    all_to_all x1, blocking collectives, on_device(): parts = lax.all_to_all(column_sum(table, returned), 'p', 0, 0, tiled=True)  17.8 us
    ppermute x6, starting transfers between devices, shift_y(): lax.ppermute(array, 'y', [(j, (j + shift) % groups) for j in range(groups)])  17.1 us
    all_to_all x1, starting transfers between devices, on_device(): received = lax.all_to_all(outgoing, 'z', 0, 0, tiled=True)  13 us
    all_to_all x1, blocking collectives, on_device(): spread = lax.all_to_all(sent, ('p', 'y'), 0, 0, tiled=True)  12.6 us
    all_gather x1, blocking collectives, on_device(): hidden_all = lax.all_gather(hidden, 'y', axis=0, tiled=True)  11.8 us
  transfers between devices with their start and end apart: 10, of which 8 were waited for; matrix products, arithmetic and copies ran while one was open for 1% of the time, Pallas kernels for 6%

profile of v5, /device:TPU:1, one launch (start us, length us, event | category | flops | bytes accessed | tf_op | source)
XLA Modules:
  0.0 250.0 jit_solution(5973812748149423367)
XLA Ops:
  7.2 0.8 copy-done.3
  8.0 0.7 copy-done.5
  8.7 0.7 copy-done.6
  9.4 0.7 copy-done.7
  10.1 1.2 prepare.1
  11.3 10.4 %all-to-all-start = ((bf16[32,8,1280]{2,1,0:T(8,128)(2,1)}), bf16[32,8,1280]{2,1,0:T(8,128)(2,1)S(1)}, u32[]{:S(2)}, u32[]{:S(2)}) async-start(bf16[32,8,1280]{2,1,0:T(8,128)(2,1)} %prepare.1), calls=%async_computation | async-start | bytes 1310720 | tf_op jit(solution)/shard_map/all_to_all | solution.py:425
  21.8 3.1 %gate_up_slices.1 = (bf16[384,1024]{1,0:T(8,128)(2,1)}, bf16[384,1024]{1,0:T(8,128)(2,1)}, bf16[384,1024]{1,0:T(8,128)(2,1)}) custom-call(s32[1]{0:T(128)} %bitcast.5.g_ref, bf16[1,192,4096]{2,1,0:T(8,128)(2,1)} %refs_0_.5, bf16[1,192,4096]{2,1,0:T(8,128)(2,1)} %refs_1_.3), custom_call_target="tpu_custom_call" | custom-call | bytes 4718592 | tf_op jit(solution)/shard_map/gate_up_slices/pallas_call | solution.py:110
  24.9 9.2 %all-to-all-done.tokens_ref = bf16[32,8,1280]{2,1,0:T(8,128)(2,1)S(1)} async-done(((bf16[32,8,1280]{2,1,0:T(8,128)(2,1)}), bf16[32,8,1280]{2,1,0:T(8,128)(2,1)S(1)}, u32[]{:S(2)}, u32[]{:S(2)}) %all-to-all-start) | async-done | bytes 655392 | tf_op jit(solution)/shard_map/all_to_all | solution.py:425
  34.1 1.7 dispatch.1
  35.8 13.0 %all-to-all-start.1 = ((bf16[16,32,1024]{2,1,0:T(8,128)(2,1)}), bf16[16,32,1024]{2,1,0:T(8,128)(2,1)S(1)}, u32[]{:S(2)}, u32[]{:S(2)}) async-start(bf16[16,32,1024]{2,1,0:T(8,128)(2,1)} %get-tuple-element.28), calls=%async_computation.1 | async-start | bytes 2097152 | tf_op jit(solution)/shard_map/all_to_all | solution.py:437
  48.8 2.5 collective-permute-start
  51.3 3.7 %collective-permute-start.1 = (bf16[384,1024]{1,0:T(8,128)(2,1)}, bf16[384,1024]{1,0:T(8,128)(2,1)}, u32[]{:S(2)}, u32[]{:S(2)}) collective-permute-start(bf16[384,1024]{1,0:T(8,128)(2,1)} %get-tuple-element.30), channel_id=1, source_target_pairs={{0,2},{1,3},{2,0},{3,1},{4,6},{5,7},{6,4},{7,5},{8,10},{9,11},{10,... | collective-permute-start | bytes 2359304 | tf_op jit(solution)/shard_map/ppermute | solution.py:25
  55.0 2.8 %collective-permute-start.2 = (bf16[384,1024]{1,0:T(8,128)(2,1)}, bf16[384,1024]{1,0:T(8,128)(2,1)}, u32[]{:S(2)}, u32[]{:S(2)}) collective-permute-start(bf16[384,1024]{1,0:T(8,128)(2,1)} %get-tuple-element.31), channel_id=1, source_target_pairs={{0,3},{1,0},{2,1},{3,2},{4,7},{5,4},{6,5},{7,6},{8,11},{9,8},{10,9... | collective-permute-start | bytes 2359304 | tf_op jit(solution)/shard_map/ppermute | solution.py:25
  57.8 2.3 down_slices.1
  60.1 2.5 collective-permute-start.3
  62.6 3.1 %collective-permute-start.4 = (bf16[192,1024]{1,0:T(8,128)(2,1)}, bf16[192,1024]{1,0:T(8,128)(2,1)S(1)}, u32[]{:S(2)}, u32[]{:S(2)}) collective-permute-start(bf16[192,1024]{1,0:T(8,128)(2,1)} %get-tuple-element.33), channel_id=1, source_target_pairs={{0,2},{1,3},{2,0},{3,1},{4,6},{5,7},{6,4},{7,5},{8,10},{9,11},{10,... | collective-permute-start | bytes 1179656 | tf_op jit(solution)/shard_map/ppermute | solution.py:25
  65.7 4.0 %collective-permute-done.refs_1_ = bf16[384,1024]{1,0:T(8,128)(2,1)S(1)} collective-permute-done((bf16[384,1024]{1,0:T(8,128)(2,1)}, bf16[384,1024]{1,0:T(8,128)(2,1)S(1)}, u32[]{:S(2)}, u32[]{:S(2)}) %collective-permute-start) | collective-permute-done | bytes 786464 | tf_op jit(solution)/shard_map/ppermute | solution.py:25
  69.7 0.9 copy-done.9
  70.7 2.5 %collective-permute-start.5 = (bf16[192,1024]{1,0:T(8,128)(2,1)}, bf16[192,1024]{1,0:T(8,128)(2,1)S(1)}, u32[]{:S(2)}, u32[]{:S(2)}) collective-permute-start(bf16[192,1024]{1,0:T(8,128)(2,1)} %get-tuple-element.34), channel_id=1, source_target_pairs={{0,3},{1,0},{2,1},{3,2},{4,7},{5,4},{6,5},{7,6},{8,11},{9,8},{10,9... | collective-permute-start | bytes 1179656 | tf_op jit(solution)/shard_map/ppermute | solution.py:25
  73.2 2.1 gate_up_own.1.refs_0_
  75.3 1.9 down_own.1.refs_0_
  77.1 9.8 %collective-permute-done.1.refs_2_ = bf16[384,1024]{1,0:T(8,128)(2,1)} collective-permute-done((bf16[384,1024]{1,0:T(8,128)(2,1)}, bf16[384,1024]{1,0:T(8,128)(2,1)}, u32[]{:S(2)}, u32[]{:S(2)}) %collective-permute-start.1) | collective-permute-done | bytes 786464 | tf_op jit(solution)/shard_map/ppermute | solution.py:25
  87.0 4.6 %collective-permute-done.2.refs_3_ = bf16[384,1024]{1,0:T(8,128)(2,1)} collective-permute-done((bf16[384,1024]{1,0:T(8,128)(2,1)}, bf16[384,1024]{1,0:T(8,128)(2,1)}, u32[]{:S(2)}, u32[]{:S(2)}) %collective-permute-start.2) | collective-permute-done | bytes 786464 | tf_op jit(solution)/shard_map/ppermute | solution.py:25
  91.5 6.7 %all-to-all-done.1.rows_ref = bf16[16,32,1024]{2,1,0:T(8,128)(2,1)S(1)} async-done(((bf16[16,32,1024]{2,1,0:T(8,128)(2,1)}), bf16[16,32,1024]{2,1,0:T(8,128)(2,1)S(1)}, u32[]{:S(2)}, u32[]{:S(2)}) %all-to-all-start.1) | async-done | bytes 1048608 | tf_op jit(solution)/shard_map/all_to_all | solution.py:437
  98.3 1.1 copy-done.10
  99.4 3.2 %gate_up.1 = bf16[4,384,512]{2,1,0:T(8,128)(2,1)S(1)} custom-call(s32[1]{0:T(128)} %bitcast.5.g_ref, bf16[16,32,1024]{2,1,0:T(8,128)(2,1)S(1)} %all-to-all-done.1.rows_ref, bf16[384,1024]{1,0:T(8,128)(2,1)S(1)} %copy-done.2, bf16[384,1024]{1,0:T(8,128)(2,1)S(1)} %copy-done.10, bf16[384,1024]{1,0:T(8,128)(2,1)} %collective-permute-done.1.refs_2_, ...), custom_call_target="tpu_custom_call" | custom-call | flops 1610612736 | bytes 6291456 | tf_op jit(solution)/shard_map/gate_up/pallas_call | solution.py:184
  102.6 1.1 collective-permute-done.4.refs_2_
  103.8 3.0 %collective-permute-done.5.refs_3_ = bf16[192,1024]{1,0:T(8,128)(2,1)S(1)} collective-permute-done((bf16[192,1024]{1,0:T(8,128)(2,1)}, bf16[192,1024]{1,0:T(8,128)(2,1)S(1)}, u32[]{:S(2)}, u32[]{:S(2)}) %collective-permute-start.5) | collective-permute-done | bytes 393248 | tf_op jit(solution)/shard_map/ppermute | solution.py:25
  106.7 24.0 %all_to_all.35.acts_ref = bf16[4,384,512]{2,1,0:T(8,128)(2,1)S(1)} all-to-all(bf16[4,384,512]{2,1,0:T(8,128)(2,1)S(1)} %gate_up.1), channel_id=1, replica_groups=mesh['z'=16,'p'=8,'y'=4] {'y'}, dimensions={0} | all-to-all | bytes 3145728 | tf_op jit(solution)/shard_map/all_to_all | solution.py:441
  130.8 0.3 silu_sum.1
  131.0 11.8 %all_gather.11.hidden_ref = bf16[768,512]{1,0:T(8,128)(2,1)S(1)} all-gather(bf16[192,512]{1,0:T(8,128)(2,1)S(1)} %silu_sum.1), channel_id=1, replica_groups=mesh['z'=16,'p'=8,'y'=4] {'y'}, dimensions={0}, use_global_device_ids=true | all-gather | bytes 983040 | tf_op jit(solution)/shard_map/all_gather | solution.py:443
  142.9 2.3 down.1
  145.1 11.7 %all-to-all-start.3 = ((bf16[16,32,1024]{2,1,0:T(8,128)(2,1)}), bf16[16,32,1024]{2,1,0:T(8,128)(2,1)S(1)}, u32[]{:S(2)}, u32[]{:S(2)}) async-start(bf16[16,32,1024]{2,1,0:T(8,128)(2,1)} %down.1), calls=%async_computation.3 | async-start | bytes 2097152 | tf_op jit(solution)/shard_map/all_to_all | solution.py:445
  156.9 0.6 dynamic_slice.13
  159.4 1.0 dynamic-slice_reduce_fusion.1
  160.4 0.1 reshape.34
  160.5 0.1 reshape.35
  160.7 0.1 reshape.37
  160.8 0.1 reshape.38
  161.0 0.1 reshape.39
  161.1 40.8 %all-to-all-done.3.returned_ref = bf16[16,32,1024]{2,1,0:T(8,128)(2,1)S(1)} async-done(((bf16[16,32,1024]{2,1,0:T(8,128)(2,1)}), bf16[16,32,1024]{2,1,0:T(8,128)(2,1)S(1)}, u32[]{:S(2)}, u32[]{:S(2)}) %all-to-all-start.3) | async-done | bytes 1048608 | tf_op jit(solution)/shard_map/all_to_all | solution.py:445
  201.9 0.4 column_sum.1
  202.3 17.8 %all_to_all.36.parts_ref = bf16[8,32,1024]{2,1,0:T(8,128)(2,1)S(1)} all-to-all(bf16[8,32,1024]{2,1,0:T(8,128)(2,1)S(1)} %column_sum.1), channel_id=1, replica_groups=mesh['z'=16,'p'=8,'y'=4] {'p'}, dimensions={0} | all-to-all | bytes 1048576 | tf_op jit(solution)/shard_map/all_to_all | solution.py:458
  220.1 0.7 combine.1
  220.8 12.6 %all_to_all.37.tiles_ref = bf16[32,4,768]{2,1,0:T(4,128)(2,1)S(1)} all-to-all(bf16[32,4,768]{2,1,0:T(4,128)(2,1)S(1)} %combine.1), channel_id=1, replica_groups=mesh['z'=16,'p'=8,'y'=4] {'p','y'}, dimensions={0} | all-to-all | bytes 393216 | tf_op jit(solution)/shard_map/all_to_all | solution.py:461
  233.5 0.8 join.1
  234.3 8.2 %all_to_all.38.back_ref = bf16[8,16,512]{2,1,0:T(8,128)(2,1)S(1)} all-to-all(bf16[8,16,512]{2,1,0:T(8,128)(2,1)S(1)} %join.1), channel_id=1, replica_groups=mesh['z'=16,'p'=8,'y'=4] {'p'}, dimensions={0} | all-to-all | bytes 262144 | tf_op jit(solution)/shard_map/all_to_all | solution.py:463
  242.5 0.7 finish.1
  (27 shorter events, 0.3 us)
Async XLA Ops:
  7.2 0.8 copy-start.3
  8.0 0.7 copy-start.5
  8.7 0.7 copy-start.6
  9.4 0.7 copy-start.7
  11.3 22.8 %all-to-all-start = ((bf16[32,8,1280]{2,1,0:T(8,128)(2,1)}), bf16[32,8,1280]{2,1,0:T(8,128)(2,1)S(1)}, u32[]{:S(2)}, u32[]{:S(2)}) async-start(bf16[32,8,1280]{2,1,0:T(8,128)(2,1)} %prepare.1), calls=%async_computation | async-start | bytes 1310720 | tf_op jit(solution)/shard_map/all_to_all | solution.py:425
  35.8 62.5 %all-to-all-start.1 = ((bf16[16,32,1024]{2,1,0:T(8,128)(2,1)}), bf16[16,32,1024]{2,1,0:T(8,128)(2,1)S(1)}, u32[]{:S(2)}, u32[]{:S(2)}) async-start(bf16[16,32,1024]{2,1,0:T(8,128)(2,1)} %get-tuple-element.28), calls=%async_computation.1 | async-start | bytes 2097152 | tf_op jit(solution)/shard_map/all_to_all | solution.py:437
  48.7 112.4 %all-gather.3.cloned.1.call-start = ((), (), s32[]{:S(2)}) async-start(), calls=%async_computation.7 | async-start | bytes 3342336 | tf_op jit(solution)/shard_map/all_gather | solution.py:422
  48.8 21.0 %collective-permute-start = (bf16[384,1024]{1,0:T(8,128)(2,1)}, bf16[384,1024]{1,0:T(8,128)(2,1)S(1)}, u32[]{:S(2)}, u32[]{:S(2)}) collective-permute-start(bf16[384,1024]{1,0:T(8,128)(2,1)} %get-tuple-element.29), channel_id=1, source_target_pairs={{0,1},{1,2},{2,3},{3,0},{4,5},{5,6},{6,7},{7,4},{8,9},{9,10},{10,1... | collective-permute-start | bytes 2359304 | tf_op jit(solution)/shard_map/ppermute | solution.py:25
  51.3 35.7 %collective-permute-start.1 = (bf16[384,1024]{1,0:T(8,128)(2,1)}, bf16[384,1024]{1,0:T(8,128)(2,1)}, u32[]{:S(2)}, u32[]{:S(2)}) collective-permute-start(bf16[384,1024]{1,0:T(8,128)(2,1)} %get-tuple-element.30), channel_id=1, source_target_pairs={{0,2},{1,3},{2,0},{3,1},{4,6},{5,7},{6,4},{7,5},{8,10},{9,11},{10,... | collective-permute-start | bytes 2359304 | tf_op jit(solution)/shard_map/ppermute | solution.py:25
  55.0 36.5 %collective-permute-start.2 = (bf16[384,1024]{1,0:T(8,128)(2,1)}, bf16[384,1024]{1,0:T(8,128)(2,1)}, u32[]{:S(2)}, u32[]{:S(2)}) collective-permute-start(bf16[384,1024]{1,0:T(8,128)(2,1)} %get-tuple-element.31), channel_id=1, source_target_pairs={{0,3},{1,0},{2,1},{3,2},{4,7},{5,4},{6,5},{7,6},{8,11},{9,8},{10,9... | collective-permute-start | bytes 2359304 | tf_op jit(solution)/shard_map/ppermute | solution.py:25
  60.1 42.5 %collective-permute-start.3 = (bf16[192,1024]{1,0:T(8,128)(2,1)}, bf16[192,1024]{1,0:T(8,128)(2,1)S(1)}, u32[]{:S(2)}, u32[]{:S(2)}) collective-permute-start(bf16[192,1024]{1,0:T(8,128)(2,1)} %get-tuple-element.32), channel_id=1, source_target_pairs={{0,1},{1,2},{2,3},{3,0},{4,5},{5,6},{6,7},{7,4},{8,9},{9,10},{10,1... | collective-permute-start | bytes 1179656 | tf_op jit(solution)/shard_map/ppermute | solution.py:25
  62.6 41.1 %collective-permute-start.4 = (bf16[192,1024]{1,0:T(8,128)(2,1)}, bf16[192,1024]{1,0:T(8,128)(2,1)S(1)}, u32[]{:S(2)}, u32[]{:S(2)}) collective-permute-start(bf16[192,1024]{1,0:T(8,128)(2,1)} %get-tuple-element.33), channel_id=1, source_target_pairs={{0,2},{1,3},{2,0},{3,1},{4,6},{5,7},{6,4},{7,5},{8,10},{9,11},{10,... | collective-permute-start | bytes 1179656 | tf_op jit(solution)/shard_map/ppermute | solution.py:25
  69.7 0.9 copy-start.9
  70.7 36.1 %collective-permute-start.5 = (bf16[192,1024]{1,0:T(8,128)(2,1)}, bf16[192,1024]{1,0:T(8,128)(2,1)S(1)}, u32[]{:S(2)}, u32[]{:S(2)}) collective-permute-start(bf16[192,1024]{1,0:T(8,128)(2,1)} %get-tuple-element.34), channel_id=1, source_target_pairs={{0,3},{1,0},{2,1},{3,2},{4,7},{5,4},{6,5},{7,6},{8,11},{9,8},{10,9... | collective-permute-start | bytes 1179656 | tf_op jit(solution)/shard_map/ppermute | solution.py:25
  75.3 23.0 %copy-start.2 = (bf16[384,1024]{1,0:T(8,128)(2,1)S(1)}, bf16[384,1024]{1,0:T(8,128)(2,1)}, u32[]{:S(2)}) copy-start(bf16[384,1024]{1,0:T(8,128)(2,1)} %gate_up_own.1.refs_0_) | copy-start | bytes 2359300
  98.3 1.1 copy-start.10
  130.8 12.1 %copy-start.1 = (bf16[192,1024]{1,0:T(8,128)(2,1)S(1)}, bf16[192,1024]{1,0:T(8,128)(2,1)}, u32[]{:S(2)}) copy-start(bf16[192,1024]{1,0:T(8,128)(2,1)} %down_own.1.refs_0_) | copy-start | bytes 1179652
  145.1 11.7 %copy-start.8 = (s32[4]{0:T(128)S(1)}, s32[4]{0:T(128)}, u32[]{:S(2)}) copy-start(s32[4]{0:T(128)} %node_ref.1) | copy-start | bytes 52
  145.1 15.6 %copy-start.4 = (bf16[8,4096]{1,0:T(8,128)(2,1)S(1)}, bf16[8,4096]{1,0:T(8,128)(2,1)}, u32[]{:S(2)}) copy-start(bf16[8,4096]{1,0:T(8,128)(2,1)} %layer_in_ref.1) | copy-start | bytes 196612
  145.1 56.7 %all-to-all-start.3 = ((bf16[16,32,1024]{2,1,0:T(8,128)(2,1)}), bf16[16,32,1024]{2,1,0:T(8,128)(2,1)S(1)}, u32[]{:S(2)}, u32[]{:S(2)}) async-start(bf16[16,32,1024]{2,1,0:T(8,128)(2,1)} %down.1), calls=%async_computation.3 | async-start | bytes 2097152 | tf_op jit(solution)/shard_map/all_to_all | solution.py:445
  201.9 31.6 %copy-start = (bf16[48,32,1024]{2,1,0:T(8,128)(2,1)S(1)}, bf16[48,32,1024]{2,1,0:T(8,128)(2,1)}, u32[]{:S(2)}) copy-start(bf16[48,32,1024]{2,1,0:T(8,128)(2,1)} %all-gather.3.cloned.1.call-done) | copy-start | bytes 9437188
Sparse Core Ops, SparseCore 0:
  57.9 85.4 all-gather.2

commit v6 on v4

--- a/solution.py
+++ b/solution.py
@@ -12,7 +12,10 @@
 Z_SIZE = 16
 P_SIZE = 8
 CAP = 4
-EXPERT = ("z", "p")
+LINE = 128
+EXPERT = ("zh", "zl", "p")
+NEAR = ("zl", "p")
+NEAR_SIZE = 2 * P_SIZE
 F32 = jnp.float32
 BF16 = jnp.bfloat16
 PARAMS = pltpu.CompilerParams(vmem_limit_bytes=40 * 1024 * 1024)
@@ -208,13 +211,10 @@
     )(g, hidden, *pieces)
 
 
-def combine_kernel(node_ref, table_ref, returned_ref, block_ref, known_ref, out_ref):
-    dests, trees, _ = out_ref.shape
+def combine_kernel(scalar_ref, table_ref, returned_ref, block_ref, known_ref, out_ref):
+    _, trees, _ = out_ref.shape
     block, part = block_ref.shape
-    peers = part // 128
-    groups = dests // peers
     tree = block // trees
-    zs = known_ref.shape[2] // 2 // 32
     returned = returned_ref[...].reshape(-1, part)
     moe = jnp.dot(table_ref[...], returned, preferred_element_type=F32)
     result = (block_ref[...].astype(F32) + moe).astype(BF16).astype(F32)
@@ -222,43 +222,50 @@
     chosen = []
     for t in range(trees):
         rows = result[t * tree : (t + 1) * tree]
-        chosen.append(jnp.sum(jnp.where(place == node_ref[t], rows, 0.0), axis=0, keepdims=True))
+        same = place == scalar_ref[1 + t]
+        chosen.append(jnp.sum(jnp.where(same, rows, 0.0), axis=0, keepdims=True))
     chosen = jnp.concatenate(chosen, axis=0)
-    for p in range(peers):
-        parts = [chosen[:, z * peers * 32 + p * 32 : z * peers * 32 + p * 32 + 32] for z in range(zs)]
-        high = jnp.concatenate(parts, axis=1).astype(BF16)
-        lanes = slice(p * 128, p * 128 + 128)
-        for j in range(groups):
-            d = p * groups + j
-            out_ref[d, :, 0:256] = known_ref[p]
-            out_ref[d, :, 256:384] = high
-            rows = result[j * tree : (j + 1) * tree, lanes]
-            out_ref[d, :, 384:512] = rows[:trees].astype(BF16)
-            out_ref[d, :, 512:640] = rows[trees:].astype(BF16)
-
-
-def combine(nodes, table, returned, block_in, known, dests):
+    lane = lax.broadcasted_iota(jnp.int32, (trees, LINE), 1)
+    kept = lax.div(lane, LINE // 2) == lax.rem(scalar_ref[0], 2)
+    for q in range(NEAR_SIZE):
+        parity, p = divmod(q, P_SIZE)
+        first = [(z * P_SIZE + p) * 32 for z in (parity, parity + 2)] * 2
+        high = jnp.concatenate([chosen[:, f : f + 32] for f in first], axis=1)
+        high = jnp.where(kept, high, 0.0).astype(BF16)
+        for j in range(trees):
+            d = q * trees + j
+            out_ref[d, :, :LINE] = known_ref[q]
+            out_ref[d, :, LINE : 2 * LINE] = high
+            row = result[j * tree + p : j * tree + p + 1]
+            at = parity * part // 2
+            lines = [row[:, at + r * LINE : at + (r + 1) * LINE] for r in range(trees)]
+            out_ref[d, :, 2 * LINE :] = jnp.concatenate(lines, axis=0).astype(BF16)
+
+
+def combine(scalars, table, returned, block_in, known):
     block, part = block_in.shape
-    trees = nodes.shape[0]
+    trees = known.shape[1]
     return pl.pallas_call(
         combine_kernel,
-        out_shape=jax.ShapeDtypeStruct((dests, trees, 640), BF16),
+        out_shape=jax.ShapeDtypeStruct((NEAR_SIZE * trees, trees, 3 * LINE), BF16),
         in_specs=[SMEM] + [VMEM] * 4,
         out_specs=VMEM,
         compiler_params=PARAMS,
         cost_estimate=cost(2 * block * table.shape[1] * part, 2 << 20),
         name="combine",
-    )(nodes, table, returned, block_in, known)
-
-
-def join_kernel(rows_ref, tiles_ref, weight_ref, out_ref):
-    amount, trees, step = tiles_ref.shape
-    peers = out_ref.shape[0]
-    line = 128
-    quarter = weight_ref.shape[0] // trees
-    high = jnp.concatenate(
-        [rows_ref[:, t * step + 2 * line : t * step + 3 * line] for t in range(trees)], axis=0
-    )
+    )(scalars, table, returned, block_in, known)
+
+
+def join_kernel(rows_ref, weight_ref, out_ref):
+    amount = rows_ref.shape[0]
+    trees = amount // NEAR_SIZE
+    step = rows_ref.shape[1] // trees
+    half = weight_ref.shape[0] // 2
+
+    def line(row, k):
+        return rows_ref[:, row * step + k * LINE : row * step + (k + 1) * LINE]
+
+    high = jnp.concatenate([line(t, 1) for t in range(trees)], axis=0)
     row = lax.broadcasted_iota(jnp.int32, (amount, amount * trees), 0)
     column = lax.broadcasted_iota(jnp.int32, (amount, amount * trees), 1)
     place = lax.rem(column, amount)
@@ -266,57 +273,55 @@
         lax.div(place, trees) == lax.div(row, trees)
     )
     total = None
-    for q in range(trees):
-        chosen = jnp.where(same & (lax.rem(place, trees) == q), 1.0, 0.0).astype(BF16)
+    for h in range(2):
+        wanted = same & (lax.div(lax.rem(place, trees), 2) == h)
+        wanted = jnp.where(wanted, 1.0, 0.0).astype(BF16)
         parts = [
-            rows_ref[:, q * step : q * step + line],
-            rows_ref[:, q * step + line : q * step + 2 * line],
-            jnp.dot(chosen, high, preferred_element_type=F32).astype(BF16),
+            line(h, 0),
+            line(2 + h, 0),
+            jnp.dot(wanted, high, preferred_element_type=F32).astype(BF16),
         ]
         for k, values in enumerate(parts):
-            weight = weight_ref[q * quarter : (q + 1) * quarter, k].reshape(line, -1)
+            weight = weight_ref[h * half : (h + 1) * half, k].reshape(LINE, -1)
             product = jnp.dot(values, weight, preferred_element_type=F32)
             total = product if total is None else total + product
-    half = total.shape[1] // 2
-    for p in range(peers):
-        rows = slice(p * trees, (p + 1) * trees)
-        pair = jnp.concatenate([total[rows, :half], total[rows, half:]], axis=0)
-        out_ref[p, 0 : 2 * trees] = pair.astype(BF16)
-        for j in range(trees):
-            for h in range(2):
-                lanes = slice((3 + h) * line, (4 + h) * line)
-                out_ref[p, (2 + h) * trees : (3 + h) * trees, j * line : (j + 1) * line] = (
-                    tiles_ref[p * trees + j, :, lanes]
-                )
+    home = jnp.concatenate([line(r, 2) for r in range(trees)], axis=1).astype(F32)
+    wide, narrow = total.shape[1] // 2, home.shape[1] // 2
+    for q in range(NEAR_SIZE):
+        rows = slice(q * trees, (q + 1) * trees)
+        pair = jnp.concatenate([total[rows, :wide], total[rows, wide:]], axis=0)
+        out_ref[q, :, :wide] = pair.astype(BF16)
+        pair = jnp.concatenate([home[rows, :narrow], home[rows, narrow:]], axis=0)
+        out_ref[q, :, wide:] = pair.astype(BF16)
 
 
 def join(tiles, weight):
     amount, trees, step = tiles.shape
-    peers = amount // trees
     width = weight.shape[-1]
+    shape = (NEAR_SIZE, 2 * trees, width // 2 + trees * LINE // 2)
     return pl.pallas_call(
         join_kernel,
-        out_shape=jax.ShapeDtypeStruct((peers, 4 * trees, width // 2), BF16),
-        in_specs=[VMEM] * 3,
+        out_shape=jax.ShapeDtypeStruct(shape, BF16),
+        in_specs=[VMEM] * 2,
         out_specs=VMEM,
         compiler_params=PARAMS,
         cost_estimate=cost(2 * amount * weight.size, 4 << 20),
         name="join",
-    )(tiles.reshape(amount, trees * step), tiles, weight)
+    )(tiles.reshape(amount, trees * step), weight)
 
 
 def finish_kernel(back_ref, layer_ref, joined_ref):
-    peers, rows, half = back_ref.shape
-    trees = rows // 4
-    summed = jnp.sum(back_ref[:, 0 : 2 * trees].astype(F32), axis=0)
+    _, rows, step = back_ref.shape
+    trees, half = joined_ref.shape[0], joined_ref.shape[1] // 2
+    narrow = step - half
+    summed = jnp.sum(back_ref[:, :, :half].astype(F32), axis=0)
     joined_ref[:, :half] = summed[:trees].astype(BF16)
     joined_ref[:, half:] = summed[trees:].astype(BF16)
-    for p in range(peers):
-        for j in range(trees):
-            lane = j * 2 * half + p * 128
-            layer_ref[:, lane : lane + 128] = back_ref[
-                p, 2 * trees : 4 * trees, j * 128 : (j + 1) * 128
-            ]
+    for parity in range(2):
+        home = back_ref[parity * P_SIZE : (parity + 1) * P_SIZE, :, half:].astype(F32)
+        for r in range(rows):
+            lane = (r % trees) * 2 * half + parity * half + (r // trees) * narrow
+            layer_ref[:, lane : lane + narrow] = home[:, r, :].astype(BF16)
 
 
 def finish(back, layer_shape, joined_shape):
@@ -372,7 +377,7 @@
     slots = experts * CAP
     trees = accepted_node.shape[0]
 
-    join_all = lax.all_gather(join_weight, "z", axis=0, tiled=False)
+    join_all = lax.all_gather(join_weight, "zh", axis=0, tiled=False)
 
     both = normed_and_raw(layer_in, norm_gain, groups)
     both = lax.all_to_all(both, "y", 0, 0, tiled=True)
@@ -406,31 +411,32 @@
     hidden = silu(acts)
     hidden_all = lax.all_gather(hidden, "y", axis=0, tiled=True)
     expert_out = down(g_one, hidden_all, down_pieces)
+    expert_out, join_all = lax.optimization_barrier((expert_out, join_all))
     returned = lax.all_to_all(expert_out, EXPERT, 0, 0, tiled=True)
 
     own_node = lax.dynamic_slice_in_dim(accepted_node, g, 1, 0)[0]
     feat = width // experts
-    z_part = Z_SIZE // groups
 
     def known(feature):
         row = lax.dynamic_index_in_dim(feature, own_node, 0, keepdims=False)
-        row = row.reshape(groups, z_part, P_SIZE, feat).transpose(2, 0, 1, 3)
-        return row.reshape(P_SIZE, groups, z_part * feat)
-
-    early = jnp.concatenate([known(low_feature), known(mid_feature)], axis=-1)
-    early, combine_table, block_in, join_all, returned = lax.optimization_barrier(
-        (early, combine_table, block_in, join_all, returned)
+        row = row.reshape(2, Z_SIZE // 4, 2, P_SIZE, feat).transpose(2, 3, 0, 1, 4)
+        return row.reshape(NEAR_SIZE, 2, LINE)
+
+    early = jnp.concatenate([known(low_feature), known(mid_feature)], axis=1)
+    early, combine_table, block_in, returned = lax.optimization_barrier(
+        (early, combine_table, block_in, returned)
     )
-    sent = combine(accepted_node, combine_table, returned, block_in, early, P_SIZE * groups)
-    spread = lax.all_to_all(sent, ("p", "y"), 0, 0, tiled=True)
-
-    back = lax.all_to_all(join(spread, join_all), "p", 0, 0, tiled=True)
+    scalars = jnp.concatenate([g_one, accepted_node])
+    sent = combine(scalars, combine_table, returned, block_in, early)
+    spread = lax.all_to_all(sent, (*NEAR, "y"), 0, 0, tiled=True)
+
+    back = lax.all_to_all(join(spread, join_all), NEAR, 0, 0, tiled=True)
     return tuple(finish(back, (rows_dev, width), (trees, part)))
 
 
 def solution(mesh):
-    split = Mesh(mesh.devices.reshape(Z_SIZE, P_SIZE, -1), ("z", "p", "y"))
-    every = ("z", "p", "y")
+    every = ("zh", "zl", "p", "y")
+    split = Mesh(mesh.devices.reshape(Z_SIZE // 2, 2, P_SIZE, -1), every)
     placed = (
         P(every, None),
         P(),

time: 247 us -> 250 us (1.012)
  waiting for transfers between devices: 77.2 us -> 84.9 us
  blocking collectives: 59.9 us -> 56.8 us
    all_to_all x1, waiting for transfers between devices: 9.53 us -> 18.4 us  [on_device(): received = lax.all_to_all(outgoing, EXPERT, 0, 0, tiled=True)]
    all_to_all x1, blocking collectives: 24.2 us -> 18.3 us  [on_device(): acts = lax.all_to_all(acts, 'y', 0, 0, tiled=True)]
    all_to_all x2, blocking collectives: 24.1 us -> 27.4 us  [the longest x1 17.7 us: on_device(): spread = lax.all_to_all(sent, (*NEAR, 'y'), 0, 0, tiled=True)]
  transfers between devices with their start and end apart: 10 -> 10, of which waited for: 7 -> 6; matrix products, arithmetic and copies ran while one was open for 2% -> 2% of each run, Pallas kernels for 6% -> 6%
where the time goes in v6:
time: 250 us; the launch traced here: 249 us
  waiting for transfers between devices  84.9 us (34%)
  starting transfers between devices  64.3 us (26%)
  blocking collectives  56.8 us (23%)
  Pallas kernels  19.4 us (8%)
  between operations  16.2 us (6%)
  local copies, waits for them, and re-layouts  6.56 us (3%)
    all_to_all x1, waiting for transfers between devices, on_device(): returned = lax.all_to_all(expert_out, EXPERT, 0, 0, tiled=True)  47.4 us
    all_to_all x1, starting transfers between devices, on_device(): returned = lax.all_to_all(expert_out, EXPERT, 0, 0, tiled=True)  21.2 us
    all_to_all x1, starting transfers between devices, on_device(): received = lax.all_to_all(outgoing, EXPERT, 0, 0, tiled=True)  21 us
    all_to_all x1, waiting for transfers between devices, on_device(): received = lax.all_to_all(outgoing, EXPERT, 0, 0, tiled=True)  18.4 us
    all_to_all x1, blocking collectives, on_device(): acts = lax.all_to_all(acts, 'y', 0, 0, tiled=True)  18.3 us
    ppermute x6, waiting for transfers between devices, shift_y(): lax.ppermute(array, 'y', [(j, (j + shift) % groups) for j in range(groups)])  18.1 us
    all_to_all x1, blocking collectives, on_device(): spread = lax.all_to_all(sent, (*NEAR, 'y'), 0, 0, tiled=True)  17.7 us
    ppermute x6, starting transfers between devices, shift_y(): lax.ppermute(array, 'y', [(j, (j + shift) % groups) for j in range(groups)])  17 us
  transfers between devices with their start and end apart: 10, of which 6 were waited for; matrix products, arithmetic and copies ran while one was open for 2% of the time, Pallas kernels for 6%

profile of v6, /device:TPU:1, one launch (start us, length us, event | category | flops | bytes accessed | tf_op | source)
XLA Modules:
  0.0 249.0 jit_solution(16668665407747419804)
XLA Ops:
  7.2 0.8 copy-done.3
  8.0 0.7 copy-done.4
  8.7 0.8 norm_pack.1
  9.5 5.0 %all-to-all-start = ((bf16[4,2,8,1024]{3,2,1,0:T(8,128)(2,1)}), bf16[4,2,8,1024]{3,2,1,0:T(8,128)(2,1)S(1)}, u32[]{:S(2)}, u32[]{:S(2)}) async-start(bf16[4,2,8,1024]{3,2,1,0:T(8,128)(2,1)} %norm_pack.1), calls=%async_computation | async-start | bytes 262144 | tf_op jit(solution)/shard_map/all_to_all | solution.py:383
  14.5 0.8 copy.27
  15.3 0.1 eq.29
  15.3 0.2 fusion
  15.6 0.1 convert_element_type.25
  15.7 0.2 fusion.1
  15.9 3.1 %gate_up_slices.1 = (bf16[384,1024]{1,0:T(8,128)(2,1)}, bf16[384,1024]{1,0:T(8,128)(2,1)}, bf16[384,1024]{1,0:T(8,128)(2,1)}) custom-call(s32[1]{0:T(128)} %bitcast.g_ref, bf16[1,192,4096]{2,1,0:T(8,128)(2,1)} %refs_0_.5, bf16[1,192,4096]{2,1,0:T(8,128)(2,1)} %refs_1_.3), custom_call_target="tpu_custom_call" | custom-call | bytes 4718592 | tf_op jit(solution)/shard_map/gate_up_slices/pallas_call | solution.py:85
  19.0 0.3 all-to-all-done.both_ref
  19.3 1.4 dispatch.1
  20.7 21.0 %all-to-all-start.1 = ((bf16[128,4,1024]{2,1,0:T(4,128)(2,1)}), bf16[128,4,1024]{2,1,0:T(4,128)(2,1)S(1)}, u32[]{:S(2)}, u32[]{:S(2)}) async-start(bf16[128,4,1024]{2,1,0:T(4,128)(2,1)} %dispatch.1), calls=%async_computation.1 | async-start | bytes 2097152 | tf_op jit(solution)/shard_map/all_to_all | solution.py:402
  41.8 0.7 all-gather.3.cloned.1.call-update
  42.5 2.2 collective-permute-start
  44.7 4.3 %collective-permute-start.1 = (bf16[384,1024]{1,0:T(8,128)(2,1)}, bf16[384,1024]{1,0:T(8,128)(2,1)}, u32[]{:S(2)}, u32[]{:S(2)}) collective-permute-start(bf16[384,1024]{1,0:T(8,128)(2,1)} %get-tuple-element.28), channel_id=1, source_target_pairs={{0,2},{1,3},{2,0},{3,1},{4,6},{5,7},{6,4},{7,5},{8,10},{9,11},{10,... | collective-permute-start | bytes 2359304 | tf_op jit(solution)/shard_map/ppermute | solution.py:27
  49.0 3.1 %collective-permute-start.2 = (bf16[384,1024]{1,0:T(8,128)(2,1)}, bf16[384,1024]{1,0:T(8,128)(2,1)}, u32[]{:S(2)}, u32[]{:S(2)}) collective-permute-start(bf16[384,1024]{1,0:T(8,128)(2,1)} %get-tuple-element.29), channel_id=1, source_target_pairs={{0,3},{1,0},{2,1},{3,2},{4,7},{5,4},{6,5},{7,6},{8,11},{9,8},{10,9... | collective-permute-start | bytes 2359304 | tf_op jit(solution)/shard_map/ppermute | solution.py:27
  52.1 2.3 down_slices.1
  54.5 2.2 collective-permute-start.3
  56.7 2.8 %collective-permute-start.4 = (bf16[192,1024]{1,0:T(8,128)(2,1)}, bf16[192,1024]{1,0:T(8,128)(2,1)S(1)}, u32[]{:S(2)}, u32[]{:S(2)}) collective-permute-start(bf16[192,1024]{1,0:T(8,128)(2,1)} %get-tuple-element.31), channel_id=1, source_target_pairs={{0,2},{1,3},{2,0},{3,1},{4,6},{5,7},{6,4},{7,5},{8,10},{9,11},{10,... | collective-permute-start | bytes 1179656 | tf_op jit(solution)/shard_map/ppermute | solution.py:27
  59.5 4.4 %collective-permute-done.refs_1_ = bf16[384,1024]{1,0:T(8,128)(2,1)S(1)} collective-permute-done((bf16[384,1024]{1,0:T(8,128)(2,1)}, bf16[384,1024]{1,0:T(8,128)(2,1)S(1)}, u32[]{:S(2)}, u32[]{:S(2)}) %collective-permute-start) | collective-permute-done | bytes 786464 | tf_op jit(solution)/shard_map/ppermute | solution.py:27
  64.0 0.9 copy-done.5
  64.8 2.3 collective-permute-start.5
  67.2 2.0 gate_up_own.1.refs_0_
  69.2 1.9 down_own.1.refs_0_
  71.1 9.9 %collective-permute-done.1.refs_2_ = bf16[384,1024]{1,0:T(8,128)(2,1)} collective-permute-done((bf16[384,1024]{1,0:T(8,128)(2,1)}, bf16[384,1024]{1,0:T(8,128)(2,1)}, u32[]{:S(2)}, u32[]{:S(2)}) %collective-permute-start.1) | collective-permute-done | bytes 786464 | tf_op jit(solution)/shard_map/ppermute | solution.py:27
  81.0 3.7 %collective-permute-done.2.refs_3_ = bf16[384,1024]{1,0:T(8,128)(2,1)} collective-permute-done((bf16[384,1024]{1,0:T(8,128)(2,1)}, bf16[384,1024]{1,0:T(8,128)(2,1)}, u32[]{:S(2)}, u32[]{:S(2)}) %collective-permute-start.2) | collective-permute-done | bytes 786464 | tf_op jit(solution)/shard_map/ppermute | solution.py:27
  84.8 18.4 %all-to-all-done.1.rows_ref = bf16[128,4,1024]{2,1,0:T(4,128)(2,1)S(1)} async-done(((bf16[128,4,1024]{2,1,0:T(4,128)(2,1)}), bf16[128,4,1024]{2,1,0:T(4,128)(2,1)S(1)}, u32[]{:S(2)}, u32[]{:S(2)}) %all-to-all-start.1) | async-done | bytes 1048608 | tf_op jit(solution)/shard_map/all_to_all | solution.py:402
  103.2 1.1 copy-done.6
  104.3 3.2 %gate_up.1 = bf16[4,384,512]{2,1,0:T(8,128)(2,1)S(1)} custom-call(s32[1]{0:T(128)} %bitcast.g_ref, bf16[128,4,1024]{2,1,0:T(4,128)(2,1)S(1)} %all-to-all-done.1.rows_ref, bf16[384,1024]{1,0:T(8,128)(2,1)S(1)} %copy-done.2, bf16[384,1024]{1,0:T(8,128)(2,1)S(1)} %copy-done.6, bf16[384,1024]{1,0:T(8,128)(2,1)} %collective-permute-done.1.refs_2_, ...), custom_call_target="tpu_custom_call" | custom-call | flops 1610612736 | bytes 6291456 | tf_op jit(solution)/shard_map/gate_up/pallas_call | solution.py:139
  107.5 18.3 %all_to_all.30.acts_ref = bf16[4,384,512]{2,1,0:T(8,128)(2,1)S(1)} all-to-all(bf16[4,384,512]{2,1,0:T(8,128)(2,1)S(1)} %gate_up.1), channel_id=1, replica_groups=mesh['zh'=8,'zl'=2,'p'=8,'y'=4] {'y'}, dimensions={0} | all-to-all | bytes 3145728 | tf_op jit(solution)/shard_map/all_to_all | solution.py:410
  125.8 0.3 silu_sum.1
  126.1 11.1 %all_gather.9.hidden_ref = bf16[768,512]{1,0:T(8,128)(2,1)S(1)} all-gather(bf16[192,512]{1,0:T(8,128)(2,1)S(1)} %silu_sum.1), channel_id=1, replica_groups=mesh['zh'=8,'zl'=2,'p'=8,'y'=4] {'y'}, dimensions={0}, use_global_device_ids=true | all-gather | bytes 983040 | tf_op jit(solution)/shard_map/all_gather | solution.py:412
  137.2 2.3 down.1
  139.5 21.2 %all-to-all-start.3 = ((bf16[128,4,1024]{2,1,0:T(4,128)(2,1)}), bf16[128,4,1024]{2,1,0:T(4,128)(2,1)S(1)}, u32[]{:S(2)}, u32[]{:S(2)}) async-start(bf16[128,4,1024]{2,1,0:T(4,128)(2,1)} %down.1), calls=%async_computation.3 | async-start | bytes 2097152 | tf_op jit(solution)/shard_map/all_to_all | solution.py:415
  160.7 0.6 dynamic_slice.10
  163.3 1.0 dynamic-slice_reduce_fusion
  164.3 0.1 reshape.50
  164.4 0.1 reshape.51
  164.5 0.1 reshape.48
  164.6 0.1 reshape.49
  164.9 0.2 select_reduce_fusion.table_ref
  165.1 47.4 %all-to-all-done.3.returned_ref = bf16[128,4,1024]{2,1,0:T(4,128)(2,1)S(1)} async-done(((bf16[128,4,1024]{2,1,0:T(4,128)(2,1)}), bf16[128,4,1024]{2,1,0:T(4,128)(2,1)S(1)}, u32[]{:S(2)}, u32[]{:S(2)}) %all-to-all-start.3) | async-done | bytes 1048608 | tf_op jit(solution)/shard_map/all_to_all | solution.py:415
  212.6 1.0 combine.1
  213.5 17.7 %all_to_all.31 = bf16[64,4,384]{2,1,0:T(4,128)(2,1)S(1)} all-to-all(bf16[64,4,384]{2,1,0:T(4,128)(2,1)S(1)} %combine.1), channel_id=1, replica_groups=mesh['zh'=8,'zl'=2,'p'=8,'y'=4] {'zl','p','y'}, dimensions={0} | all-to-all | bytes 393216 | tf_op jit(solution)/shard_map/all_to_all | solution.py:431
  231.3 0.5 join.1
  231.8 9.7 %all_to_all.32.back_ref = bf16[16,8,768]{2,1,0:T(8,128)(2,1)S(1)} all-to-all(bf16[16,8,768]{2,1,0:T(8,128)(2,1)S(1)} %join.1), channel_id=1, replica_groups=mesh['zh'=8,'zl'=2,'p'=8,'y'=4] {'zl','p'}, dimensions={0} | all-to-all | bytes 393216 | tf_op jit(solution)/shard_map/all_to_all | solution.py:433
  241.5 0.7 finish.1
  (31 shorter events, 0.4 us)
Async XLA Ops:
  7.2 0.8 copy-start.3
  8.0 0.7 copy-start.4
  9.5 9.8 %all-to-all-start = ((bf16[4,2,8,1024]{3,2,1,0:T(8,128)(2,1)}), bf16[4,2,8,1024]{3,2,1,0:T(8,128)(2,1)S(1)}, u32[]{:S(2)}, u32[]{:S(2)}) async-start(bf16[4,2,8,1024]{3,2,1,0:T(8,128)(2,1)} %norm_pack.1), calls=%async_computation | async-start | bytes 262144 | tf_op jit(solution)/shard_map/all_to_all | solution.py:383
  20.7 82.4 %all-to-all-start.1 = ((bf16[128,4,1024]{2,1,0:T(4,128)(2,1)}), bf16[128,4,1024]{2,1,0:T(4,128)(2,1)S(1)}, u32[]{:S(2)}, u32[]{:S(2)}) async-start(bf16[128,4,1024]{2,1,0:T(4,128)(2,1)} %dispatch.1), calls=%async_computation.1 | async-start | bytes 2097152 | tf_op jit(solution)/shard_map/all_to_all | solution.py:402
  41.7 97.7 %all-gather.3.cloned.1.call-start = ((), (), s32[]{:S(2)}) async-start(), calls=%async_computation.6 | async-start | bytes 1769472 | tf_op jit(solution)/shard_map/all_gather | solution.py:380
  42.5 21.5 %collective-permute-start = (bf16[384,1024]{1,0:T(8,128)(2,1)}, bf16[384,1024]{1,0:T(8,128)(2,1)S(1)}, u32[]{:S(2)}, u32[]{:S(2)}) collective-permute-start(bf16[384,1024]{1,0:T(8,128)(2,1)} %get-tuple-element.27), channel_id=1, source_target_pairs={{0,1},{1,2},{2,3},{3,0},{4,5},{5,6},{6,7},{7,4},{8,9},{9,10},{10,1... | collective-permute-start | bytes 2359304 | tf_op jit(solution)/shard_map/ppermute | solution.py:27
  44.7 36.3 %collective-permute-start.1 = (bf16[384,1024]{1,0:T(8,128)(2,1)}, bf16[384,1024]{1,0:T(8,128)(2,1)}, u32[]{:S(2)}, u32[]{:S(2)}) collective-permute-start(bf16[384,1024]{1,0:T(8,128)(2,1)} %get-tuple-element.28), channel_id=1, source_target_pairs={{0,2},{1,3},{2,0},{3,1},{4,6},{5,7},{6,4},{7,5},{8,10},{9,11},{10,... | collective-permute-start | bytes 2359304 | tf_op jit(solution)/shard_map/ppermute | solution.py:27
  49.0 35.7 %collective-permute-start.2 = (bf16[384,1024]{1,0:T(8,128)(2,1)}, bf16[384,1024]{1,0:T(8,128)(2,1)}, u32[]{:S(2)}, u32[]{:S(2)}) collective-permute-start(bf16[384,1024]{1,0:T(8,128)(2,1)} %get-tuple-element.29), channel_id=1, source_target_pairs={{0,3},{1,0},{2,1},{3,2},{4,7},{5,4},{6,5},{7,6},{8,11},{9,8},{10,9... | collective-permute-start | bytes 2359304 | tf_op jit(solution)/shard_map/ppermute | solution.py:27
  54.5 53.0 %collective-permute-start.3 = (bf16[192,1024]{1,0:T(8,128)(2,1)}, bf16[192,1024]{1,0:T(8,128)(2,1)S(1)}, u32[]{:S(2)}, u32[]{:S(2)}) collective-permute-start(bf16[192,1024]{1,0:T(8,128)(2,1)} %get-tuple-element.30), channel_id=1, source_target_pairs={{0,1},{1,2},{2,3},{3,0},{4,5},{5,6},{6,7},{7,4},{8,9},{9,10},{10,1... | collective-permute-start | bytes 1179656 | tf_op jit(solution)/shard_map/ppermute | solution.py:27
  56.7 50.8 %collective-permute-start.4 = (bf16[192,1024]{1,0:T(8,128)(2,1)}, bf16[192,1024]{1,0:T(8,128)(2,1)S(1)}, u32[]{:S(2)}, u32[]{:S(2)}) collective-permute-start(bf16[192,1024]{1,0:T(8,128)(2,1)} %get-tuple-element.31), channel_id=1, source_target_pairs={{0,2},{1,3},{2,0},{3,1},{4,6},{5,7},{6,4},{7,5},{8,10},{9,11},{10,... | collective-permute-start | bytes 1179656 | tf_op jit(solution)/shard_map/ppermute | solution.py:27
  64.0 0.9 copy-start.5
  64.8 42.7 %collective-permute-start.5 = (bf16[192,1024]{1,0:T(8,128)(2,1)}, bf16[192,1024]{1,0:T(8,128)(2,1)S(1)}, u32[]{:S(2)}, u32[]{:S(2)}) collective-permute-start(bf16[192,1024]{1,0:T(8,128)(2,1)} %get-tuple-element.32), channel_id=1, source_target_pairs={{0,3},{1,0},{2,1},{3,2},{4,7},{5,4},{6,5},{7,6},{8,11},{9,8},{10,9... | collective-permute-start | bytes 1179656 | tf_op jit(solution)/shard_map/ppermute | solution.py:27
  69.2 33.9 %copy-start.2 = (bf16[384,1024]{1,0:T(8,128)(2,1)S(1)}, bf16[384,1024]{1,0:T(8,128)(2,1)}, u32[]{:S(2)}) copy-start(bf16[384,1024]{1,0:T(8,128)(2,1)} %gate_up_own.1.refs_0_) | copy-start | bytes 2359300
  103.2 1.1 copy-start.6
  125.8 11.4 %copy-start.1 = (bf16[192,1024]{1,0:T(8,128)(2,1)S(1)}, bf16[192,1024]{1,0:T(8,128)(2,1)}, u32[]{:S(2)}) copy-start(bf16[192,1024]{1,0:T(8,128)(2,1)} %down_own.1.refs_0_) | copy-start | bytes 1179652
  139.5 21.3 %copy-start.8 = (s32[4]{0:T(128)S(1)}, s32[4]{0:T(128)}, u32[]{:S(2)}) copy-start(s32[4]{0:T(128)} %param.20) | copy-start | bytes 52
  139.5 25.2 %copy-start.7 = (f32[32,8]{0,1:T(8,128)S(1)}, f32[32,8]{0,1:T(8,128)}, u32[]{:S(2)}) copy-start(f32[32,8]{0,1:T(8,128)} %param.14) | copy-start | bytes 3076
  139.5 73.1 %all-to-all-start.3 = ((bf16[128,4,1024]{2,1,0:T(4,128)(2,1)}), bf16[128,4,1024]{2,1,0:T(4,128)(2,1)S(1)}, u32[]{:S(2)}, u32[]{:S(2)}) async-start(bf16[128,4,1024]{2,1,0:T(4,128)(2,1)} %down.1), calls=%async_computation.3 | async-start | bytes 2097152 | tf_op jit(solution)/shard_map/all_to_all | solution.py:415
  160.7 70.6 %copy-start = (bf16[24,32,1024]{2,1,0:T(8,128)(2,1)S(1)}, bf16[24,32,1024]{2,1,0:T(8,128)(2,1)}, u32[]{:S(2)}) copy-start(bf16[24,32,1024]{2,1,0:T(8,128)(2,1)} %all-gather.3.cloned.1.call-done) | copy-start | bytes 4718596
Sparse Core Ops, SparseCore 0:
  44.7 80.3 all-gather.2

commit v7 on v4

--- a/solution.py
+++ b/solution.py
@@ -52,41 +52,39 @@
     )(layer_in, norm_gain)
 
 
-def slice_kernel(shifts, groups, g_ref, *refs):
-    count = len(refs) - 1 - len(shifts)
-    sources, outs, sems = refs[:count], refs[count:-1], refs[-1]
-    _, units, width = sources[0].shape
-    part = width // groups
+def slice_kernel(plan, groups, g_ref, *refs):
+    sources, outs, sems = refs[:3], refs[3:-1], refs[-1]
+    part = sources[0].shape[2] // groups
     copies = []
-    for i, s in enumerate(shifts):
-        lane = pl.multiple_of(lax.rem(g_ref[0] + s, groups) * part, part)
-        for k, source in enumerate(sources):
+    for i, (out, moves) in enumerate(zip(outs, plan)):
+        at = 0
+        for k, (source, first, amount, shift) in enumerate(moves):
+            lane = pl.multiple_of(lax.rem(g_ref[0] + shift, groups) * part, part)
             copies.append(
                 pltpu.make_async_copy(
-                    source.at[0, :, pl.ds(lane, part)],
-                    outs[i].at[pl.ds(k * units, units), :],
+                    sources[source].at[0, pl.ds(first, amount), pl.ds(lane, part)],
+                    out.at[pl.ds(at, amount), :],
                     sems.at[i, k],
                 )
             )
+            at += amount
     for copy in copies:
         copy.start()
     for copy in copies:
         copy.wait()
 
 
-def weight_slices(g, sources, shifts, groups, name):
-    _, units, width = sources[0].shape
-    count = len(sources)
-    shape = jax.ShapeDtypeStruct((count * units, width // groups), BF16)
-    moved = 2 * len(shifts) * count * units * width // groups * 2
-    return pl.pallas_call(
-        functools.partial(slice_kernel, shifts, groups),
-        out_shape=[shape] * len(shifts),
-        in_specs=[SMEM] + [pl.BlockSpec(memory_space=pltpu.HBM)] * count,
-        out_specs=[VMEM] * len(shifts),
-        scratch_shapes=[pltpu.SemaphoreType.DMA((len(shifts), count))],
+def weight_slices(g, sources, plan, groups, name):
+    part = sources[0].shape[2] // groups
+    rows = [sum(amount for _, _, amount, _ in moves) for moves in plan]
+    return pl.pallas_call(
+        functools.partial(slice_kernel, plan, groups),
+        out_shape=[jax.ShapeDtypeStruct((amount, part), BF16) for amount in rows],
+        in_specs=[SMEM] + [pl.BlockSpec(memory_space=pltpu.HBM)] * 3,
+        out_specs=[VMEM] * len(plan),
+        scratch_shapes=[pltpu.SemaphoreType.DMA((len(plan), max(len(m) for m in plan)))],
         compiler_params=pltpu.CompilerParams(vmem_limit_bytes=60 * 1024 * 1024),
-        cost_estimate=cost(0, moved),
+        cost_estimate=cost(0, 4 * sum(rows) * part),
         name=name,
     )(g, *sources)
 
@@ -132,7 +130,7 @@
     experts, cap, part = rows.shape
     slots = experts * cap
     groups = len(pieces)
-    double = pieces[0].shape[0]
+    double = pieces[1].shape[0]
     return pl.pallas_call(
         functools.partial(gate_up_kernel, groups),
         out_shape=jax.ShapeDtypeStruct((groups, double, slots), BF16),
@@ -199,7 +197,10 @@
             num_scalar_prefetch=1,
             grid=(1,),
             in_specs=[pl.BlockSpec((inner, slots), lambda i, g_ref: (0, 0))]
-            + [pl.BlockSpec((units, part), lambda i, g_ref: (0, 0))] * groups,
+            + [
+                pl.BlockSpec((units, part), lambda i, g_ref, k=piece.shape[0] // units - 1: (k, 0))
+                for piece in pieces
+            ],
             out_specs=pl.BlockSpec(out, lambda i, g_ref: (0, 0, 0)),
         ),
         compiler_params=PARAMS,
@@ -385,15 +386,22 @@
     dispatch = jnp.any(matches, axis=1).astype(BF16)
     outgoing = dispatch_rows(dispatch, both)
 
-    others = tuple(range(1, groups))
-    both_in = [gate_proj, up_proj]
-    cut = weight_slices(g_one, both_in, others, groups, "gate_up_slices")
+    units = gate_proj.shape[1]
+    sources = [gate_proj, up_proj, down_proj]
+
+    def plan(shift, kinds):
+        return [(kind, 0, units, shift) for kind in kinds]
+
+    cut = [plan(1, (0, 1)), plan(2, (0, 1, 2)), plan(3, (0, 1))]
+    cut = weight_slices(g_one, sources, cut, groups, "first_slices")
     outgoing, *cut = lax.optimization_barrier((outgoing, *cut))
-    gate_up_pieces = [shift_y(piece, groups, s) for s, piece in zip(others, cut)]
-    cut = weight_slices(g_one, [down_proj], others, groups, "down_slices")
-    down_pieces = [shift_y(piece, groups, s) for s, piece in zip(others, cut)]
-    gate_up_pieces = [*weight_slices(g_one, both_in, (0,), groups, "gate_up_own"), *gate_up_pieces]
-    down_pieces = [*weight_slices(g_one, [down_proj], (0,), groups, "down_own"), *down_pieces]
+    near = [shift_y(cut[0], groups, 1), shift_y(cut[2], groups, 3)]
+    far = shift_y(cut[1], groups, 2)
+    cut = weight_slices(g_one, sources, [plan(1, (2,)), plan(3, (2,))], groups, "down_slices")
+    near_down = [shift_y(cut[0], groups, 1), shift_y(cut[1], groups, 3)]
+    (own,) = weight_slices(g_one, sources, [plan(0, (0, 1, 2))], groups, "own_slices")
+    gate_up_pieces = [own, near[0], far, near[1]]
+    down_pieces = [own, near_down[0], far, near_down[1]]
     received = lax.all_to_all(outgoing, EXPERT, 0, 0, tiled=True)
 
     combine_table = jnp.sum(
@@ -401,7 +409,9 @@
     ).astype(BF16)
 
     acts = gate_up(g_one, received, gate_up_pieces)
-    acts, *down_pieces = lax.optimization_barrier((acts, *down_pieces))
+    acts, down_pieces[1], down_pieces[3] = lax.optimization_barrier(
+        (acts, down_pieces[1], down_pieces[3])
+    )
     acts = lax.all_to_all(acts, "y", 0, 0, tiled=True)
     hidden = silu(acts)
     hidden_all = lax.all_gather(hidden, "y", axis=0, tiled=True)

time: 247 us -> 246 us (level)
  blocking collectives: 59.9 us -> 55.9 us
    ppermute x6 -> x5, waiting for transfers between devices: 19.9 us -> 27.1 us  [shift_y(): lax.ppermute(array, 'y', [(j, (j + shift) % groups) for j in range(groups)])]
    all_to_all x1, waiting for transfers between devices: 9.53 us -> 4.68 us  [on_device(): received = lax.all_to_all(outgoing, EXPERT, 0, 0, tiled=True)]
    all_to_all x1, blocking collectives: 24.2 us -> 19.6 us  [on_device(): acts = lax.all_to_all(acts, 'y', 0, 0, tiled=True)]
    pallas_call x4 -> x3, Pallas kernels: 9.34 us -> 7.65 us  [weight_slices(): pl.pallas_call(functools.partial(slice_kernel, plan, groups), out_shape=[...]
    unnamed x20 -> x16, local copies, waits for them, and re-layouts: 6.22 us -> 5.48 us
    ppermute x6 -> x5, starting transfers between devices: 17 us -> 17 us  [shift_y(): lax.ppermute(array, 'y', [(j, (j + shift) % groups) for j in range(groups)])]
  transfers between devices with their start and end apart: 10 -> 9, of which waited for: 7 -> 3; matrix products, arithmetic and copies ran while one was open for 2% -> 2% of each run, Pallas kernels for 6% -> 6%
where the time goes in v7:
time: 246 us; the launch traced here: 244 us
  waiting for transfers between devices  79.4 us (32%)
  starting transfers between devices  65.8 us (27%)
  blocking collectives  55.9 us (23%)
  Pallas kernels  18.8 us (8%)
  between operations  16.2 us (7%)
  local copies, waits for them, and re-layouts  7.68 us (3%)
    all_to_all x1, waiting for transfers between devices, on_device(): returned = lax.all_to_all(expert_out, EXPERT, 0, 0, tiled=True)  47.5 us
    ppermute x5, waiting for transfers between devices, shift_y(): lax.ppermute(array, 'y', [(j, (j + shift) % groups) for j in range(groups)])  27.1 us
    all_to_all x1, starting transfers between devices, on_device(): returned = lax.all_to_all(expert_out, EXPERT, 0, 0, tiled=True)  22.8 us
    all_to_all x1, starting transfers between devices, on_device(): received = lax.all_to_all(outgoing, EXPERT, 0, 0, tiled=True)  21 us
    all_to_all x1, blocking collectives, on_device(): acts = lax.all_to_all(acts, 'y', 0, 0, tiled=True)  19.6 us
    ppermute x5, starting transfers between devices, shift_y(): lax.ppermute(array, 'y', [(j, (j + shift) % groups) for j in range(groups)])  17 us
    all_to_all x1, blocking collectives, on_device(): spread = lax.all_to_all(sent, ('p', 'y'), 0, 0, tiled=True)  16 us
    all_gather x1, blocking collectives, on_device(): hidden_all = lax.all_gather(hidden, 'y', axis=0, tiled=True)  12.1 us
  transfers between devices with their start and end apart: 9, of which 3 were waited for; matrix products, arithmetic and copies ran while one was open for 2% of the time, Pallas kernels for 6%

profile of v7, /device:TPU:1, one launch (start us, length us, event | category | flops | bytes accessed | tf_op | source)
XLA Modules:
  0.0 244.5 jit_solution(14487630537311416417)
XLA Ops:
  7.2 0.8 copy-done.3
  8.0 0.7 copy-done.4
  8.7 0.8 norm_pack.1
  9.5 5.0 %all-to-all-start = ((bf16[4,2,8,1024]{3,2,1,0:T(8,128)(2,1)}), bf16[4,2,8,1024]{3,2,1,0:T(8,128)(2,1)S(1)}, u32[]{:S(2)}, u32[]{:S(2)}) async-start(bf16[4,2,8,1024]{3,2,1,0:T(8,128)(2,1)} %norm_pack.1), calls=%async_computation | async-start | bytes 262144 | tf_op jit(solution)/shard_map/all_to_all | solution.py:379
  14.5 0.8 copy.27
  15.3 0.1 eq.29
  15.4 0.2 fusion
  15.6 0.1 convert_element_type.25
  15.7 0.2 fusion.1
  16.0 3.3 %first_slices.1 = (bf16[384,1024]{1,0:T(8,128)(2,1)}, bf16[576,1024]{1,0:T(8,128)(2,1)}, bf16[384,1024]{1,0:T(8,128)(2,1)}) custom-call(s32[1]{0:T(128)} %bitcast.5.g_ref, bf16[1,192,4096]{2,1,0:T(8,128)(2,1)} %refs_0_.5, bf16[1,192,4096]{2,1,0:T(8,128)(2,1)} %refs_1_.5, bf16[1,192,4096]{2,1,0:T(8,128)(2,1)} %refs_2_.5), custom_call_target="tpu_custom_call" | custom-call | bytes 5505024 | tf_op jit(solution)/shard_map/first_slices/pallas_call | solution.py:80
  19.3 0.0 all-to-all-done.both_ref
  19.3 1.5 dispatch.1
  20.8 21.0 %all-to-all-start.1 = ((bf16[128,4,1024]{2,1,0:T(4,128)(2,1)}), bf16[128,4,1024]{2,1,0:T(4,128)(2,1)S(1)}, u32[]{:S(2)}, u32[]{:S(2)}) async-start(bf16[128,4,1024]{2,1,0:T(4,128)(2,1)} %dispatch.1), calls=%async_computation.1 | async-start | bytes 2097152 | tf_op jit(solution)/shard_map/all_to_all | solution.py:405
  41.8 0.0 all-gather.3.cloned.1.call-start
  41.8 4.0 %collective-permute-start.1 = (bf16[576,1024]{1,0:T(8,128)(2,1)}, bf16[576,1024]{1,0:T(8,128)(2,1)S(1)}, u32[]{:S(2)}, u32[]{:S(2)}) collective-permute-start(bf16[576,1024]{1,0:T(8,128)(2,1)} %get-tuple-element.24), channel_id=1, source_target_pairs={{0,2},{1,3},{2,0},{3,1},{4,6},{5,7},{6,4},{7,5},{8,10},{9,11},{10,... | collective-permute-start | bytes 3538952 | tf_op jit(solution)/shard_map/ppermute | solution.py:24
  45.8 2.2 collective-permute-start
  48.0 4.3 %collective-permute-start.2 = (bf16[384,1024]{1,0:T(8,128)(2,1)}, bf16[384,1024]{1,0:T(8,128)(2,1)}, u32[]{:S(2)}, u32[]{:S(2)}) collective-permute-start(bf16[384,1024]{1,0:T(8,128)(2,1)} %get-tuple-element.25), channel_id=1, source_target_pairs={{0,3},{1,0},{2,1},{3,2},{4,7},{5,4},{6,5},{7,6},{8,11},{9,8},{10,9... | collective-permute-start | bytes 2359304 | tf_op jit(solution)/shard_map/ppermute | solution.py:24
  52.3 2.0 down_slices.1
  54.4 1.9 collective-permute-start.3
  56.3 4.6 %collective-permute-start.4 = (bf16[192,1024]{1,0:T(8,128)(2,1)}, bf16[192,1024]{1,0:T(8,128)(2,1)}, u32[]{:S(2)}, u32[]{:S(2)}) collective-permute-start(bf16[192,1024]{1,0:T(8,128)(2,1)} %get-tuple-element.27), channel_id=1, source_target_pairs={{0,3},{1,0},{2,1},{3,2},{4,7},{5,4},{6,5},{7,6},{8,11},{9,8},{10,9... | collective-permute-start | bytes 1179656 | tf_op jit(solution)/shard_map/ppermute | solution.py:24
  60.9 0.0 all-gather.3.cloned.1.call-update
  60.9 2.3 own_slices.1.refs_0_
  63.2 27.1 %collective-permute-done.refs_1_ = bf16[384,1024]{1,0:T(8,128)(2,1)S(1)} collective-permute-done((bf16[384,1024]{1,0:T(8,128)(2,1)}, bf16[384,1024]{1,0:T(8,128)(2,1)S(1)}, u32[]{:S(2)}, u32[]{:S(2)}) %collective-permute-start) | collective-permute-done | bytes 786464 | tf_op jit(solution)/shard_map/ppermute | solution.py:24
  90.3 0.0 collective-permute-done.2.refs_3_
  90.3 4.7 %all-to-all-done.1.rows_ref = bf16[128,4,1024]{2,1,0:T(4,128)(2,1)S(1)} async-done(((bf16[128,4,1024]{2,1,0:T(4,128)(2,1)}), bf16[128,4,1024]{2,1,0:T(4,128)(2,1)S(1)}, u32[]{:S(2)}, u32[]{:S(2)}) %all-to-all-start.1) | async-done | bytes 1048608 | tf_op jit(solution)/shard_map/all_to_all | solution.py:405
  95.0 1.3 copy-done
  96.3 3.0 %gate_up.1 = bf16[4,384,512]{2,1,0:T(8,128)(2,1)S(1)} custom-call(s32[1]{0:T(128)} %bitcast.5.g_ref, bf16[128,4,1024]{2,1,0:T(4,128)(2,1)S(1)} %all-to-all-done.1.rows_ref, bf16[576,1024]{1,0:T(8,128)(2,1)S(1)} %copy-done, bf16[384,1024]{1,0:T(8,128)(2,1)S(1)} %collective-permute-done.refs_1_, bf16[576,1024]{1,0:T(8,128)(2,1)S(1)} %collective-permute-done.1.refs_2_, ...), custom_call_target="tpu_custom_call" | custom-call | flops 1610612736 | bytes 6291456 | tf_op jit(solution)/shard_map/gate_up/pallas_call | solution.py:134
  99.2 19.6 %all_to_all.30.acts_ref = bf16[4,384,512]{2,1,0:T(8,128)(2,1)S(1)} all-to-all(bf16[4,384,512]{2,1,0:T(8,128)(2,1)S(1)} %gate_up.1), channel_id=1, replica_groups=mesh['z'=16,'p'=8,'y'=4] {'y'}, dimensions={0} | all-to-all | bytes 3145728 | tf_op jit(solution)/shard_map/all_to_all | solution.py:415
  118.8 0.3 silu_sum.1
  119.1 12.1 %all_gather.11.hidden_ref = bf16[768,512]{1,0:T(8,128)(2,1)S(1)} all-gather(bf16[192,512]{1,0:T(8,128)(2,1)S(1)} %silu_sum.1), channel_id=1, replica_groups=mesh['z'=16,'p'=8,'y'=4] {'y'}, dimensions={0}, use_global_device_ids=true | all-gather | bytes 983040 | tf_op jit(solution)/shard_map/all_gather | solution.py:417
  131.2 3.3 %down.1 = bf16[128,4,1024]{2,1,0:T(4,128)(2,1)} custom-call(s32[1]{0:T(128)} %bitcast.5.g_ref, bf16[768,512]{1,0:T(8,128)(2,1)S(1)} %all_gather.11.hidden_ref, bf16[576,1024]{1,0:T(8,128)(2,1)S(1)} %copy-done.1, bf16[192,1024]{1,0:T(8,128)(2,1)S(1)} %collective-permute-done.3.refs_1_, bf16[576,1024]{1,0:T(8,128)(2,1)S(1)} %collective-permute-done.1.refs_2_, ...), custom_call_target="tpu_custom_call" | custom-call | flops 805306368 | bytes 4194304 | tf_op jit(solution)/shard_map/down/pallas_call | solution.py:193
  134.5 22.8 %all-to-all-start.3 = ((bf16[128,4,1024]{2,1,0:T(4,128)(2,1)}), bf16[128,4,1024]{2,1,0:T(4,128)(2,1)S(1)}, u32[]{:S(2)}, u32[]{:S(2)}) async-start(bf16[128,4,1024]{2,1,0:T(4,128)(2,1)} %down.1), calls=%async_computation.3 | async-start | bytes 2097152 | tf_op jit(solution)/shard_map/all_to_all | solution.py:419
  157.3 0.6 dynamic_slice.10
  159.8 1.0 dynamic-slice_reduce_fusion
  160.8 0.1 reshape.47
  160.9 0.1 reshape.48
  161.0 0.1 reshape.49
  161.1 0.1 reshape.50
  161.2 0.1 copy.29
  161.3 0.2 select_reduce_fusion.table_ref
  161.6 0.0 all-gather.3.cloned.1.call-done
  161.6 47.5 %all-to-all-done.3.returned_ref = bf16[128,4,1024]{2,1,0:T(4,128)(2,1)S(1)} async-done(((bf16[128,4,1024]{2,1,0:T(4,128)(2,1)}), bf16[128,4,1024]{2,1,0:T(4,128)(2,1)S(1)}, u32[]{:S(2)}, u32[]{:S(2)}) %all-to-all-start.3) | async-done | bytes 1048608 | tf_op jit(solution)/shard_map/all_to_all | solution.py:419
  209.1 0.9 combine.1
  210.1 16.0 %all_to_all.31.tiles_ref = bf16[32,4,640]{2,1,0:T(4,128)(2,1)S(1)} all-to-all(bf16[32,4,640]{2,1,0:T(4,128)(2,1)S(1)} %combine.1), channel_id=1, replica_groups=mesh['z'=16,'p'=8,'y'=4] {'p','y'}, dimensions={0} | all-to-all | bytes 327680 | tf_op jit(solution)/shard_map/all_to_all | solution.py:435
  226.1 1.9 copy-done.2
  228.0 0.8 join.1
  228.8 8.2 %all_to_all.32.back_ref = bf16[8,16,512]{2,1,0:T(8,128)(2,1)S(1)} all-to-all(bf16[8,16,512]{2,1,0:T(8,128)(2,1)S(1)} %join.1), channel_id=1, replica_groups=mesh['z'=16,'p'=8,'y'=4] {'p'}, dimensions={0} | all-to-all | bytes 262144 | tf_op jit(solution)/shard_map/all_to_all | solution.py:437
  237.0 0.6 finish.1
  (23 shorter events, 0.1 us)
Async XLA Ops:
  7.2 0.8 copy-start.3
  8.0 0.7 copy-start.4
  9.5 9.8 %all-to-all-start = ((bf16[4,2,8,1024]{3,2,1,0:T(8,128)(2,1)}), bf16[4,2,8,1024]{3,2,1,0:T(8,128)(2,1)S(1)}, u32[]{:S(2)}, u32[]{:S(2)}) async-start(bf16[4,2,8,1024]{3,2,1,0:T(8,128)(2,1)} %norm_pack.1), calls=%async_computation | async-start | bytes 262144 | tf_op jit(solution)/shard_map/all_to_all | solution.py:379
  20.8 74.2 %all-to-all-start.1 = ((bf16[128,4,1024]{2,1,0:T(4,128)(2,1)}), bf16[128,4,1024]{2,1,0:T(4,128)(2,1)S(1)}, u32[]{:S(2)}, u32[]{:S(2)}) async-start(bf16[128,4,1024]{2,1,0:T(4,128)(2,1)} %dispatch.1), calls=%async_computation.1 | async-start | bytes 2097152 | tf_op jit(solution)/shard_map/all_to_all | solution.py:405
  41.8 119.8 %all-gather.3.cloned.1.call-start = ((), (), s32[]{:S(2)}) async-start(), calls=%async_computation.6 | async-start | bytes 3342336 | tf_op jit(solution)/shard_map/all_gather | solution.py:376
  41.8 48.5 %collective-permute-start.1 = (bf16[576,1024]{1,0:T(8,128)(2,1)}, bf16[576,1024]{1,0:T(8,128)(2,1)S(1)}, u32[]{:S(2)}, u32[]{:S(2)}) collective-permute-start(bf16[576,1024]{1,0:T(8,128)(2,1)} %get-tuple-element.24), channel_id=1, source_target_pairs={{0,2},{1,3},{2,0},{3,1},{4,6},{5,7},{6,4},{7,5},{8,10},{9,11},{10,... | collective-permute-start | bytes 3538952 | tf_op jit(solution)/shard_map/ppermute | solution.py:24
  45.8 44.5 %collective-permute-start = (bf16[384,1024]{1,0:T(8,128)(2,1)}, bf16[384,1024]{1,0:T(8,128)(2,1)S(1)}, u32[]{:S(2)}, u32[]{:S(2)}) collective-permute-start(bf16[384,1024]{1,0:T(8,128)(2,1)} %get-tuple-element.23), channel_id=1, source_target_pairs={{0,1},{1,2},{2,3},{3,0},{4,5},{5,6},{6,7},{7,4},{8,9},{9,10},{10,1... | collective-permute-start | bytes 2359304 | tf_op jit(solution)/shard_map/ppermute | solution.py:24
  48.0 42.3 %collective-permute-start.2 = (bf16[384,1024]{1,0:T(8,128)(2,1)}, bf16[384,1024]{1,0:T(8,128)(2,1)}, u32[]{:S(2)}, u32[]{:S(2)}) collective-permute-start(bf16[384,1024]{1,0:T(8,128)(2,1)} %get-tuple-element.25), channel_id=1, source_target_pairs={{0,3},{1,0},{2,1},{3,2},{4,7},{5,4},{6,5},{7,6},{8,11},{9,8},{10,9... | collective-permute-start | bytes 2359304 | tf_op jit(solution)/shard_map/ppermute | solution.py:24
  54.4 44.9 %collective-permute-start.3 = (bf16[192,1024]{1,0:T(8,128)(2,1)}, bf16[192,1024]{1,0:T(8,128)(2,1)S(1)}, u32[]{:S(2)}, u32[]{:S(2)}) collective-permute-start(bf16[192,1024]{1,0:T(8,128)(2,1)} %get-tuple-element.26), channel_id=1, source_target_pairs={{0,1},{1,2},{2,3},{3,0},{4,5},{5,6},{6,7},{7,4},{8,9},{9,10},{10,1... | collective-permute-start | bytes 1179656 | tf_op jit(solution)/shard_map/ppermute | solution.py:24
  56.3 42.9 %collective-permute-start.4 = (bf16[192,1024]{1,0:T(8,128)(2,1)}, bf16[192,1024]{1,0:T(8,128)(2,1)}, u32[]{:S(2)}, u32[]{:S(2)}) collective-permute-start(bf16[192,1024]{1,0:T(8,128)(2,1)} %get-tuple-element.27), channel_id=1, source_target_pairs={{0,3},{1,0},{2,1},{3,2},{4,7},{5,4},{6,5},{7,6},{8,11},{9,8},{10,9... | collective-permute-start | bytes 1179656 | tf_op jit(solution)/shard_map/ppermute | solution.py:24
  95.0 1.3 copy-start
  118.8 12.4 %copy-start.1 = (bf16[576,1024]{1,0:T(8,128)(2,1)S(1)}, bf16[576,1024]{1,0:T(8,128)(2,1)}, u32[]{:S(2)}) copy-start(bf16[576,1024]{1,0:T(8,128)(2,1)} %own_slices.1.refs_0_) | copy-start | bytes 3538948
  134.5 22.8 %copy-start.5 = (s32[4]{0:T(128)S(1)}, s32[4]{0:T(128)}, u32[]{:S(2)}) copy-start(s32[4]{0:T(128)} %node_ref.1) | copy-start | bytes 52
  134.5 26.7 %copy-start.6 = (f32[32,8]{0,1:T(8,128)S(1)}, f32[32,8]{0,1:T(8,128)}, u32[]{:S(2)}) copy-start(f32[32,8]{0,1:T(8,128)} %param.14) | copy-start | bytes 3076
  134.5 74.6 %all-to-all-start.3 = ((bf16[128,4,1024]{2,1,0:T(4,128)(2,1)}), bf16[128,4,1024]{2,1,0:T(4,128)(2,1)S(1)}, u32[]{:S(2)}, u32[]{:S(2)}) async-start(bf16[128,4,1024]{2,1,0:T(4,128)(2,1)} %down.1), calls=%async_computation.3 | async-start | bytes 2097152 | tf_op jit(solution)/shard_map/all_to_all | solution.py:419
  226.1 1.9 copy-start.2
Sparse Core Ops, SparseCore 0:
  61.0 76.3 all-gather.2

commit v8 on v7

--- a/solution.py
+++ b/solution.py
@@ -252,6 +252,22 @@
     )(nodes, table, returned, block_in, known)
 
 
+def held_kernel(weight_ref, out_ref):
+    out_ref[...] = weight_ref[...]
+
+
+def held(weight):
+    return pl.pallas_call(
+        held_kernel,
+        out_shape=jax.ShapeDtypeStruct(weight.shape, BF16),
+        in_specs=[VMEM],
+        out_specs=VMEM,
+        compiler_params=PARAMS,
+        cost_estimate=cost(0, 4 * weight.size),
+        name="held",
+    )(weight)
+
+
 def join_kernel(rows_ref, tiles_ref, weight_ref, out_ref):
     amount, trees, step = tiles_ref.shape
     peers = out_ref.shape[0]
@@ -428,6 +444,7 @@
         return row.reshape(P_SIZE, groups, z_part * feat)
 
     early = jnp.concatenate([known(low_feature), known(mid_feature)], axis=-1)
+    join_all = held(join_all)
     early, combine_table, block_in, join_all, returned = lax.optimization_barrier(
         (early, combine_table, block_in, join_all, returned)
     )

time: 246 us -> 244 us (level)
  waiting for transfers between devices: 79.4 us -> 76.9 us
where the time goes in v8:
time: 244 us; the launch traced here: 243 us
  waiting for transfers between devices  76.9 us (32%)
  starting transfers between devices  66.3 us (27%)
  blocking collectives  55.9 us (23%)
  Pallas kernels  19.7 us (8%)
  between operations  16.2 us (7%)
  local copies, waits for them, and re-layouts  7.68 us (3%)
    all_to_all x1, waiting for transfers between devices, on_device(): returned = lax.all_to_all(expert_out, EXPERT, 0, 0, tiled=True)  45.1 us
    ppermute x5, waiting for transfers between devices, shift_y(): lax.ppermute(array, 'y', [(j, (j + shift) % groups) for j in range(groups)])  27.1 us
    all_to_all x1, starting transfers between devices, on_device(): returned = lax.all_to_all(expert_out, EXPERT, 0, 0, tiled=True)  23.2 us
    all_to_all x1, starting transfers between devices, on_device(): received = lax.all_to_all(outgoing, EXPERT, 0, 0, tiled=True)  21 us
    all_to_all x1, blocking collectives, on_device(): acts = lax.all_to_all(acts, 'y', 0, 0, tiled=True)  19.6 us
    ppermute x5, starting transfers between devices, shift_y(): lax.ppermute(array, 'y', [(j, (j + shift) % groups) for j in range(groups)])  17 us
    all_to_all x1, blocking collectives, on_device(): spread = lax.all_to_all(sent, ('p', 'y'), 0, 0, tiled=True)  16 us
    all_gather x1, blocking collectives, on_device(): hidden_all = lax.all_gather(hidden, 'y', axis=0, tiled=True)  12.1 us
  transfers between devices with their start and end apart: 9, of which 3 were waited for; matrix products, arithmetic and copies ran while one was open for 2% of the time, Pallas kernels for 6%

profile of v8, /device:TPU:1, one launch (start us, length us, event | category | flops | bytes accessed | tf_op | source)
XLA Modules:
  0.0 243.4 jit_solution(10565663583148580366)
XLA Ops:
  7.2 0.8 copy-done.3
  8.0 0.7 copy-done.4
  8.7 0.8 norm_pack.1
  9.5 5.0 %all-to-all-start = ((bf16[4,2,8,1024]{3,2,1,0:T(8,128)(2,1)}), bf16[4,2,8,1024]{3,2,1,0:T(8,128)(2,1)S(1)}, u32[]{:S(2)}, u32[]{:S(2)}) async-start(bf16[4,2,8,1024]{3,2,1,0:T(8,128)(2,1)} %norm_pack.1), calls=%async_computation | async-start | bytes 262144 | tf_op jit(solution)/shard_map/all_to_all | solution.py:395
  14.5 0.8 copy.27
  15.3 0.1 eq.29
  15.4 0.2 fusion
  15.6 0.1 convert_element_type.25
  15.7 0.2 fusion.1
  16.0 3.3 %first_slices.1 = (bf16[384,1024]{1,0:T(8,128)(2,1)}, bf16[576,1024]{1,0:T(8,128)(2,1)}, bf16[384,1024]{1,0:T(8,128)(2,1)}) custom-call(s32[1]{0:T(128)} %bitcast.5.g_ref, bf16[1,192,4096]{2,1,0:T(8,128)(2,1)} %refs_0_.5, bf16[1,192,4096]{2,1,0:T(8,128)(2,1)} %refs_1_.5, bf16[1,192,4096]{2,1,0:T(8,128)(2,1)} %refs_2_.5), custom_call_target="tpu_custom_call" | custom-call | bytes 5505024 | tf_op jit(solution)/shard_map/first_slices/pallas_call | solution.py:80
  19.3 0.0 all-to-all-done.both_ref
  19.3 1.5 dispatch.1
  20.8 21.0 %all-to-all-start.1 = ((bf16[128,4,1024]{2,1,0:T(4,128)(2,1)}), bf16[128,4,1024]{2,1,0:T(4,128)(2,1)S(1)}, u32[]{:S(2)}, u32[]{:S(2)}) async-start(bf16[128,4,1024]{2,1,0:T(4,128)(2,1)} %dispatch.1), calls=%async_computation.1 | async-start | bytes 2097152 | tf_op jit(solution)/shard_map/all_to_all | solution.py:421
  41.8 0.0 all-gather.3.cloned.1.call-start
  41.8 4.0 %collective-permute-start.1 = (bf16[576,1024]{1,0:T(8,128)(2,1)}, bf16[576,1024]{1,0:T(8,128)(2,1)S(1)}, u32[]{:S(2)}, u32[]{:S(2)}) collective-permute-start(bf16[576,1024]{1,0:T(8,128)(2,1)} %get-tuple-element.24), channel_id=1, source_target_pairs={{0,2},{1,3},{2,0},{3,1},{4,6},{5,7},{6,4},{7,5},{8,10},{9,11},{10,... | collective-permute-start | bytes 3538952 | tf_op jit(solution)/shard_map/ppermute | solution.py:24
  45.8 2.2 collective-permute-start
  48.0 4.3 %collective-permute-start.2 = (bf16[384,1024]{1,0:T(8,128)(2,1)}, bf16[384,1024]{1,0:T(8,128)(2,1)}, u32[]{:S(2)}, u32[]{:S(2)}) collective-permute-start(bf16[384,1024]{1,0:T(8,128)(2,1)} %get-tuple-element.25), channel_id=1, source_target_pairs={{0,3},{1,0},{2,1},{3,2},{4,7},{5,4},{6,5},{7,6},{8,11},{9,8},{10,9... | collective-permute-start | bytes 2359304 | tf_op jit(solution)/shard_map/ppermute | solution.py:24
  52.3 2.0 down_slices.1
  54.4 1.9 collective-permute-start.3
  56.3 4.6 %collective-permute-start.4 = (bf16[192,1024]{1,0:T(8,128)(2,1)}, bf16[192,1024]{1,0:T(8,128)(2,1)}, u32[]{:S(2)}, u32[]{:S(2)}) collective-permute-start(bf16[192,1024]{1,0:T(8,128)(2,1)} %get-tuple-element.27), channel_id=1, source_target_pairs={{0,3},{1,0},{2,1},{3,2},{4,7},{5,4},{6,5},{7,6},{8,11},{9,8},{10,9... | collective-permute-start | bytes 1179656 | tf_op jit(solution)/shard_map/ppermute | solution.py:24
  60.9 0.0 all-gather.3.cloned.1.call-update
  60.9 2.3 own_slices.1.refs_0_
  63.2 27.1 %collective-permute-done.refs_1_ = bf16[384,1024]{1,0:T(8,128)(2,1)S(1)} collective-permute-done((bf16[384,1024]{1,0:T(8,128)(2,1)}, bf16[384,1024]{1,0:T(8,128)(2,1)S(1)}, u32[]{:S(2)}, u32[]{:S(2)}) %collective-permute-start) | collective-permute-done | bytes 786464 | tf_op jit(solution)/shard_map/ppermute | solution.py:24
  90.3 4.7 %all-to-all-done.1.rows_ref = bf16[128,4,1024]{2,1,0:T(4,128)(2,1)S(1)} async-done(((bf16[128,4,1024]{2,1,0:T(4,128)(2,1)}), bf16[128,4,1024]{2,1,0:T(4,128)(2,1)S(1)}, u32[]{:S(2)}, u32[]{:S(2)}) %all-to-all-start.1) | async-done | bytes 1048608 | tf_op jit(solution)/shard_map/all_to_all | solution.py:421
  95.0 1.3 copy-done
  96.3 3.0 %gate_up.1 = bf16[4,384,512]{2,1,0:T(8,128)(2,1)S(1)} custom-call(s32[1]{0:T(128)} %bitcast.5.g_ref, bf16[128,4,1024]{2,1,0:T(4,128)(2,1)S(1)} %all-to-all-done.1.rows_ref, bf16[576,1024]{1,0:T(8,128)(2,1)S(1)} %copy-done, bf16[384,1024]{1,0:T(8,128)(2,1)S(1)} %collective-permute-done.refs_1_, bf16[576,1024]{1,0:T(8,128)(2,1)S(1)} %collective-permute-done.1.refs_2_, ...), custom_call_target="tpu_custom_call" | custom-call | flops 1610612736 | bytes 6291456 | tf_op jit(solution)/shard_map/gate_up/pallas_call | solution.py:134
  99.2 19.6 %all_to_all.30.acts_ref = bf16[4,384,512]{2,1,0:T(8,128)(2,1)S(1)} all-to-all(bf16[4,384,512]{2,1,0:T(8,128)(2,1)S(1)} %gate_up.1), channel_id=1, replica_groups=mesh['z'=16,'p'=8,'y'=4] {'y'}, dimensions={0} | all-to-all | bytes 3145728 | tf_op jit(solution)/shard_map/all_to_all | solution.py:431
  118.8 0.3 silu_sum.1
  119.1 12.1 %all_gather.11.hidden_ref = bf16[768,512]{1,0:T(8,128)(2,1)S(1)} all-gather(bf16[192,512]{1,0:T(8,128)(2,1)S(1)} %silu_sum.1), channel_id=1, replica_groups=mesh['z'=16,'p'=8,'y'=4] {'y'}, dimensions={0}, use_global_device_ids=true | all-gather | bytes 983040 | tf_op jit(solution)/shard_map/all_gather | solution.py:433
  131.2 3.3 %down.1 = bf16[128,4,1024]{2,1,0:T(4,128)(2,1)} custom-call(s32[1]{0:T(128)} %bitcast.5.g_ref, bf16[768,512]{1,0:T(8,128)(2,1)S(1)} %all_gather.11.hidden_ref, bf16[576,1024]{1,0:T(8,128)(2,1)S(1)} %copy-done.1, bf16[192,1024]{1,0:T(8,128)(2,1)S(1)} %collective-permute-done.3.refs_1_, bf16[576,1024]{1,0:T(8,128)(2,1)S(1)} %collective-permute-done.1.refs_2_, ...), custom_call_target="tpu_custom_call" | custom-call | flops 805306368 | bytes 4194304 | tf_op jit(solution)/shard_map/down/pallas_call | solution.py:193
  134.5 23.2 %all-to-all-start.3 = ((bf16[128,4,1024]{2,1,0:T(4,128)(2,1)}), bf16[128,4,1024]{2,1,0:T(4,128)(2,1)}, u32[]{:S(2)}, u32[]{:S(2)}) async-start(bf16[128,4,1024]{2,1,0:T(4,128)(2,1)} %down.1), calls=%async_computation.3 | async-start | bytes 2097152 | tf_op jit(solution)/shard_map/all_to_all | solution.py:435
  157.7 0.6 dynamic_slice.10
  160.3 1.0 dynamic-slice_reduce_fusion
  161.3 0.1 reshape.47
  161.4 0.1 reshape.48
  161.5 0.1 reshape.49
  161.6 0.1 reshape.50
  161.7 0.1 copy.29
  161.8 0.2 select_reduce_fusion.table_ref
  162.0 0.0 all-gather.3.cloned.1.call-done
  162.1 1.9 copy-done.2
  164.0 0.2 held.1.weight_ref
  164.2 45.1 %all-to-all-done.3.returned_ref = bf16[128,4,1024]{2,1,0:T(4,128)(2,1)} async-done(((bf16[128,4,1024]{2,1,0:T(4,128)(2,1)}), bf16[128,4,1024]{2,1,0:T(4,128)(2,1)}, u32[]{:S(2)}, u32[]{:S(2)}) %all-to-all-start.3) | async-done | bytes 1048608 | tf_op jit(solution)/shard_map/all_to_all | solution.py:435
  209.2 1.6 combine.1
  210.9 16.0 %all_to_all.31.tiles_ref = bf16[32,4,640]{2,1,0:T(4,128)(2,1)S(1)} all-to-all(bf16[32,4,640]{2,1,0:T(4,128)(2,1)S(1)} %combine.1), channel_id=1, replica_groups=mesh['z'=16,'p'=8,'y'=4] {'p','y'}, dimensions={0} | all-to-all | bytes 327680 | tf_op jit(solution)/shard_map/all_to_all | solution.py:452
  226.9 0.8 join.1
  227.7 8.2 %all_to_all.32.back_ref = bf16[8,16,512]{2,1,0:T(8,128)(2,1)S(1)} all-to-all(bf16[8,16,512]{2,1,0:T(8,128)(2,1)S(1)} %join.1), channel_id=1, replica_groups=mesh['z'=16,'p'=8,'y'=4] {'p'}, dimensions={0} | all-to-all | bytes 262144 | tf_op jit(solution)/shard_map/all_to_all | solution.py:454
  235.9 0.6 finish.1
  (24 shorter events, 0.1 us)
Async XLA Ops:
  7.2 0.8 copy-start.3
  8.0 0.7 copy-start.4
  9.5 9.8 %all-to-all-start = ((bf16[4,2,8,1024]{3,2,1,0:T(8,128)(2,1)}), bf16[4,2,8,1024]{3,2,1,0:T(8,128)(2,1)S(1)}, u32[]{:S(2)}, u32[]{:S(2)}) async-start(bf16[4,2,8,1024]{3,2,1,0:T(8,128)(2,1)} %norm_pack.1), calls=%async_computation | async-start | bytes 262144 | tf_op jit(solution)/shard_map/all_to_all | solution.py:395
  20.8 74.2 %all-to-all-start.1 = ((bf16[128,4,1024]{2,1,0:T(4,128)(2,1)}), bf16[128,4,1024]{2,1,0:T(4,128)(2,1)S(1)}, u32[]{:S(2)}, u32[]{:S(2)}) async-start(bf16[128,4,1024]{2,1,0:T(4,128)(2,1)} %dispatch.1), calls=%async_computation.1 | async-start | bytes 2097152 | tf_op jit(solution)/shard_map/all_to_all | solution.py:421
  41.8 120.3 %all-gather.3.cloned.1.call-start = ((), (), s32[]{:S(2)}) async-start(), calls=%async_computation.6 | async-start | bytes 3342336 | tf_op jit(solution)/shard_map/all_gather | solution.py:392
  41.8 48.5 %collective-permute-start.1 = (bf16[576,1024]{1,0:T(8,128)(2,1)}, bf16[576,1024]{1,0:T(8,128)(2,1)S(1)}, u32[]{:S(2)}, u32[]{:S(2)}) collective-permute-start(bf16[576,1024]{1,0:T(8,128)(2,1)} %get-tuple-element.24), channel_id=1, source_target_pairs={{0,2},{1,3},{2,0},{3,1},{4,6},{5,7},{6,4},{7,5},{8,10},{9,11},{10,... | collective-permute-start | bytes 3538952 | tf_op jit(solution)/shard_map/ppermute | solution.py:24
  45.8 44.5 %collective-permute-start = (bf16[384,1024]{1,0:T(8,128)(2,1)}, bf16[384,1024]{1,0:T(8,128)(2,1)S(1)}, u32[]{:S(2)}, u32[]{:S(2)}) collective-permute-start(bf16[384,1024]{1,0:T(8,128)(2,1)} %get-tuple-element.23), channel_id=1, source_target_pairs={{0,1},{1,2},{2,3},{3,0},{4,5},{5,6},{6,7},{7,4},{8,9},{9,10},{10,1... | collective-permute-start | bytes 2359304 | tf_op jit(solution)/shard_map/ppermute | solution.py:24
  48.0 42.3 %collective-permute-start.2 = (bf16[384,1024]{1,0:T(8,128)(2,1)}, bf16[384,1024]{1,0:T(8,128)(2,1)}, u32[]{:S(2)}, u32[]{:S(2)}) collective-permute-start(bf16[384,1024]{1,0:T(8,128)(2,1)} %get-tuple-element.25), channel_id=1, source_target_pairs={{0,3},{1,0},{2,1},{3,2},{4,7},{5,4},{6,5},{7,6},{8,11},{9,8},{10,9... | collective-permute-start | bytes 2359304 | tf_op jit(solution)/shard_map/ppermute | solution.py:24
  54.4 44.9 %collective-permute-start.3 = (bf16[192,1024]{1,0:T(8,128)(2,1)}, bf16[192,1024]{1,0:T(8,128)(2,1)S(1)}, u32[]{:S(2)}, u32[]{:S(2)}) collective-permute-start(bf16[192,1024]{1,0:T(8,128)(2,1)} %get-tuple-element.26), channel_id=1, source_target_pairs={{0,1},{1,2},{2,3},{3,0},{4,5},{5,6},{6,7},{7,4},{8,9},{9,10},{10,1... | collective-permute-start | bytes 1179656 | tf_op jit(solution)/shard_map/ppermute | solution.py:24
  56.3 42.9 %collective-permute-start.4 = (bf16[192,1024]{1,0:T(8,128)(2,1)}, bf16[192,1024]{1,0:T(8,128)(2,1)}, u32[]{:S(2)}, u32[]{:S(2)}) collective-permute-start(bf16[192,1024]{1,0:T(8,128)(2,1)} %get-tuple-element.27), channel_id=1, source_target_pairs={{0,3},{1,0},{2,1},{3,2},{4,7},{5,4},{6,5},{7,6},{8,11},{9,8},{10,9... | collective-permute-start | bytes 1179656 | tf_op jit(solution)/shard_map/ppermute | solution.py:24
  95.0 1.3 copy-start
  118.8 12.4 %copy-start.1 = (bf16[576,1024]{1,0:T(8,128)(2,1)S(1)}, bf16[576,1024]{1,0:T(8,128)(2,1)}, u32[]{:S(2)}) copy-start(bf16[576,1024]{1,0:T(8,128)(2,1)} %own_slices.1.refs_0_) | copy-start | bytes 3538948
  134.5 23.3 %copy-start.5 = (s32[4]{0:T(128)S(1)}, s32[4]{0:T(128)}, u32[]{:S(2)}) copy-start(s32[4]{0:T(128)} %node_ref.1) | copy-start | bytes 52
  134.5 27.2 %copy-start.6 = (f32[32,8]{0,1:T(8,128)S(1)}, f32[32,8]{0,1:T(8,128)}, u32[]{:S(2)}) copy-start(f32[32,8]{0,1:T(8,128)} %param.14) | copy-start | bytes 3076
  134.5 74.8 %all-to-all-start.3 = ((bf16[128,4,1024]{2,1,0:T(4,128)(2,1)}), bf16[128,4,1024]{2,1,0:T(4,128)(2,1)}, u32[]{:S(2)}, u32[]{:S(2)}) async-start(bf16[128,4,1024]{2,1,0:T(4,128)(2,1)} %down.1), calls=%async_computation.3 | async-start | bytes 2097152 | tf_op jit(solution)/shard_map/all_to_all | solution.py:435
  162.1 1.9 copy-start.2
Sparse Core Ops, SparseCore 0:
  61.0 76.3 all-gather.2

commit v9 on v8

--- a/solution.py
+++ b/solution.py
@@ -74,7 +74,7 @@
         copy.wait()
 
 
-def weight_slices(g, sources, plan, groups, name):
+def weight_slices(g, sources, plan, groups, name, mib=60):
     part = sources[0].shape[2] // groups
     rows = [sum(amount for _, _, amount, _ in moves) for moves in plan]
     return pl.pallas_call(
@@ -83,7 +83,7 @@
         in_specs=[SMEM] + [pl.BlockSpec(memory_space=pltpu.HBM)] * 3,
         out_specs=[VMEM] * len(plan),
         scratch_shapes=[pltpu.SemaphoreType.DMA((len(plan), max(len(m) for m in plan)))],
-        compiler_params=pltpu.CompilerParams(vmem_limit_bytes=60 * 1024 * 1024),
+        compiler_params=pltpu.CompilerParams(vmem_limit_bytes=mib * 1024 * 1024),
         cost_estimate=cost(0, 4 * sum(rows) * part),
         name=name,
     )(g, *sources)
@@ -415,7 +415,7 @@
     far = shift_y(cut[1], groups, 2)
     cut = weight_slices(g_one, sources, [plan(1, (2,)), plan(3, (2,))], groups, "down_slices")
     near_down = [shift_y(cut[0], groups, 1), shift_y(cut[1], groups, 3)]
-    (own,) = weight_slices(g_one, sources, [plan(0, (0, 1, 2))], groups, "own_slices")
+    (own,) = weight_slices(g_one, sources, [plan(0, (0, 1, 2))], groups, "own_slices", 40)
     gate_up_pieces = [own, near[0], far, near[1]]
     down_pieces = [own, near_down[0], far, near_down[1]]
     received = lax.all_to_all(outgoing, EXPERT, 0, 0, tiled=True)

time: 244 us -> 246 us (level)
    unnamed x16 -> x24, local copies, waits for them, and re-layouts: 5.48 us -> 7.93 us
  transfers between devices with their start and end apart: 9 -> 9, of which waited for: 3 -> 3; matrix products, arithmetic and copies ran while one was open for 2% -> 2% of each run, Pallas kernels for 6% -> 5%
where the time goes in v9:
time: 246 us; the launch traced here: 244 us
  waiting for transfers between devices  76 us (31%)
  starting transfers between devices  66.4 us (27%)
  blocking collectives  56.1 us (23%)
  Pallas kernels  18.8 us (8%)
  between operations  16.3 us (7%)
  local copies, waits for them, and re-layouts  10.1 us (4%)
    all_to_all x1, waiting for transfers between devices, on_device(): returned = lax.all_to_all(expert_out, EXPERT, 0, 0, tiled=True)  45.1 us
    ppermute x5, waiting for transfers between devices, shift_y(): lax.ppermute(array, 'y', [(j, (j + shift) % groups) for j in range(groups)])  26.6 us
    all_to_all x1, starting transfers between devices, on_device(): returned = lax.all_to_all(expert_out, EXPERT, 0, 0, tiled=True)  22.6 us
    all_to_all x1, starting transfers between devices, on_device(): received = lax.all_to_all(outgoing, EXPERT, 0, 0, tiled=True)  21.4 us
    all_to_all x1, blocking collectives, on_device(): acts = lax.all_to_all(acts, 'y', 0, 0, tiled=True)  19.1 us
    ppermute x5, starting transfers between devices, shift_y(): lax.ppermute(array, 'y', [(j, (j + shift) % groups) for j in range(groups)])  17.3 us
    all_to_all x1, blocking collectives, on_device(): spread = lax.all_to_all(sent, ('p', 'y'), 0, 0, tiled=True)  16 us
    all_gather x1, blocking collectives, on_device(): hidden_all = lax.all_gather(hidden, 'y', axis=0, tiled=True)  12.8 us
  transfers between devices with their start and end apart: 9, of which 3 were waited for; matrix products, arithmetic and copies ran while one was open for 2% of the time, Pallas kernels for 5%

profile of v9, /device:TPU:1, one launch (start us, length us, event | category | flops | bytes accessed | tf_op | source)
XLA Modules:
  0.0 244.5 jit_solution(14672486734832367729)
XLA Ops:
  7.2 0.8 copy-done.7
  8.0 0.7 copy-done.8
  8.7 0.8 norm_pack.1
  9.5 5.0 %all-to-all-start = ((bf16[4,2,8,1024]{3,2,1,0:T(8,128)(2,1)}), bf16[4,2,8,1024]{3,2,1,0:T(8,128)(2,1)S(1)}, u32[]{:S(2)}, u32[]{:S(2)}) async-start(bf16[4,2,8,1024]{3,2,1,0:T(8,128)(2,1)} %norm_pack.1), calls=%async_computation | async-start | bytes 262144 | tf_op jit(solution)/shard_map/all_to_all | solution.py:395
  14.5 0.8 copy.27
  15.3 0.1 eq.29
  15.4 0.2 fusion
  15.6 0.1 convert_element_type.25
  15.7 0.2 fusion.1
  16.0 3.4 %first_slices.1 = (bf16[384,1024]{1,0:T(8,128)(2,1)}, bf16[576,1024]{1,0:T(8,128)(2,1)}, bf16[384,1024]{1,0:T(8,128)(2,1)}) custom-call(s32[1]{0:T(128)} %bitcast.5.g_ref, bf16[1,192,4096]{2,1,0:T(8,128)(2,1)} %refs_0_.5, bf16[1,192,4096]{2,1,0:T(8,128)(2,1)} %refs_1_.5, bf16[1,192,4096]{2,1,0:T(8,128)(2,1)} %refs_2_.5), custom_call_target="tpu_custom_call" | custom-call | bytes 5505024 | tf_op jit(solution)/shard_map/first_slices/pallas_call | solution.py:80
  19.4 1.5 dispatch.1
  20.9 21.4 %all-to-all-start.1 = ((bf16[128,4,1024]{2,1,0:T(4,128)(2,1)}), bf16[128,4,1024]{2,1,0:T(4,128)(2,1)}, u32[]{:S(2)}, u32[]{:S(2)}) async-start(bf16[128,4,1024]{2,1,0:T(4,128)(2,1)} %dispatch.1), calls=%async_computation.1 | async-start | bytes 2097152 | tf_op jit(solution)/shard_map/all_to_all | solution.py:421
  42.4 0.0 all-gather.3.cloned.1.call-start
  42.4 4.3 %collective-permute-start.1 = (bf16[576,1024]{1,0:T(8,128)(2,1)}, bf16[576,1024]{1,0:T(8,128)(2,1)}, u32[]{:S(2)}, u32[]{:S(2)}) collective-permute-start(bf16[576,1024]{1,0:T(8,128)(2,1)} %get-tuple-element.24), channel_id=1, source_target_pairs={{0,2},{1,3},{2,0},{3,1},{4,6},{5,7},{6,4},{7,5},{8,10},{9,11},{10,... | collective-permute-start | bytes 3538952 | tf_op jit(solution)/shard_map/ppermute | solution.py:24
  46.7 2.2 collective-permute-start
  48.9 4.3 %collective-permute-start.2 = (bf16[384,1024]{1,0:T(8,128)(2,1)}, bf16[384,1024]{1,0:T(8,128)(2,1)}, u32[]{:S(2)}, u32[]{:S(2)}) collective-permute-start(bf16[384,1024]{1,0:T(8,128)(2,1)} %get-tuple-element.25), channel_id=1, source_target_pairs={{0,3},{1,0},{2,1},{3,2},{4,7},{5,4},{6,5},{7,6},{8,11},{9,8},{10,9... | collective-permute-start | bytes 2359304 | tf_op jit(solution)/shard_map/ppermute | solution.py:24
  53.3 2.1 down_slices.1
  55.4 1.9 collective-permute-start.3
  57.3 4.6 %collective-permute-start.4 = (bf16[192,1024]{1,0:T(8,128)(2,1)}, bf16[192,1024]{1,0:T(8,128)(2,1)}, u32[]{:S(2)}, u32[]{:S(2)}) collective-permute-start(bf16[192,1024]{1,0:T(8,128)(2,1)} %get-tuple-element.27), channel_id=1, source_target_pairs={{0,3},{1,0},{2,1},{3,2},{4,7},{5,4},{6,5},{7,6},{8,11},{9,8},{10,9... | collective-permute-start | bytes 1179656 | tf_op jit(solution)/shard_map/ppermute | solution.py:24
  61.9 1.4 copy-done.2
  63.3 0.1 own_slices.1.refs_0_
  63.5 1.0 copy-done.3
  64.5 26.6 %collective-permute-done.refs_1_ = bf16[384,1024]{1,0:T(8,128)(2,1)} collective-permute-done((bf16[384,1024]{1,0:T(8,128)(2,1)}, bf16[384,1024]{1,0:T(8,128)(2,1)}, u32[]{:S(2)}, u32[]{:S(2)}) %collective-permute-start) | collective-permute-done | bytes 786464 | tf_op jit(solution)/shard_map/ppermute | solution.py:24
  91.1 4.3 %all-to-all-done.1.rows_ref = bf16[128,4,1024]{2,1,0:T(4,128)(2,1)} async-done(((bf16[128,4,1024]{2,1,0:T(4,128)(2,1)}), bf16[128,4,1024]{2,1,0:T(4,128)(2,1)}, u32[]{:S(2)}, u32[]{:S(2)}) %all-to-all-start.1) | async-done | bytes 1048608 | tf_op jit(solution)/shard_map/all_to_all | solution.py:421
  95.4 1.3 copy-done.4
  96.7 3.8 %gate_up.1 = bf16[4,384,512]{2,1,0:T(8,128)(2,1)S(1)} custom-call(s32[1]{0:T(128)} %bitcast.5.g_ref, bf16[128,4,1024]{2,1,0:T(4,128)(2,1)} %all-to-all-done.1.rows_ref, bf16[576,1024]{1,0:T(8,128)(2,1)S(1)} %copy-done.4, bf16[384,1024]{1,0:T(8,128)(2,1)} %collective-permute-done.refs_1_, bf16[576,1024]{1,0:T(8,128)(2,1)} %collective-permute-done.1.refs_2_, ...), custom_call_target="tpu_custom_call" | custom-call | flops 1610612736 | bytes 6291456 | tf_op jit(solution)/shard_map/gate_up/pallas_call | solution.py:134
  100.5 19.1 %all_to_all.30.acts_ref = bf16[4,384,512]{2,1,0:T(8,128)(2,1)S(1)} all-to-all(bf16[4,384,512]{2,1,0:T(8,128)(2,1)S(1)} %gate_up.1), channel_id=1, replica_groups=mesh['z'=16,'p'=8,'y'=4] {'y'}, dimensions={0} | all-to-all | bytes 3145728 | tf_op jit(solution)/shard_map/all_to_all | solution.py:431
  119.6 0.3 silu_sum.1
  119.9 12.8 %all_gather.11.hidden_ref = bf16[768,512]{1,0:T(8,128)(2,1)S(1)} all-gather(bf16[192,512]{1,0:T(8,128)(2,1)S(1)} %silu_sum.1), channel_id=1, replica_groups=mesh['z'=16,'p'=8,'y'=4] {'y'}, dimensions={0}, use_global_device_ids=true | all-gather | bytes 983040 | tf_op jit(solution)/shard_map/all_gather | solution.py:433
  132.7 3.5 %down.1 = bf16[128,4,1024]{2,1,0:T(4,128)(2,1)} custom-call(s32[1]{0:T(128)} %bitcast.5.g_ref, bf16[768,512]{1,0:T(8,128)(2,1)S(1)} %all_gather.11.hidden_ref, bf16[576,1024]{1,0:T(8,128)(2,1)S(1)} %copy-done.5, bf16[192,1024]{1,0:T(8,128)(2,1)} %collective-permute-done.3.refs_1_, bf16[576,1024]{1,0:T(8,128)(2,1)} %collective-permute-done.1.refs_2_, ...), custom_call_target="tpu_custom_call" | custom-call | flops 805306368 | bytes 4194304 | tf_op jit(solution)/shard_map/down/pallas_call | solution.py:193
  136.2 22.6 %all-to-all-start.3 = ((bf16[128,4,1024]{2,1,0:T(4,128)(2,1)}), bf16[128,4,1024]{2,1,0:T(4,128)(2,1)}, u32[]{:S(2)}, u32[]{:S(2)}) async-start(bf16[128,4,1024]{2,1,0:T(4,128)(2,1)} %down.1), calls=%async_computation.3 | async-start | bytes 2097152 | tf_op jit(solution)/shard_map/all_to_all | solution.py:435
  158.8 0.6 dynamic_slice.10
  161.4 1.0 dynamic-slice_reduce_fusion
  162.3 0.1 reshape.47
  162.4 0.1 reshape.48
  162.5 0.1 reshape.49
  162.6 0.1 reshape.50
  162.8 0.1 copy.29
  162.9 0.2 select_reduce_fusion.table_ref
  163.1 0.0 all-gather.3.cloned.1.call-done
  163.2 1.9 copy-done.6
  165.0 0.2 held.1.weight_ref
  165.3 45.1 %all-to-all-done.3.returned_ref = bf16[128,4,1024]{2,1,0:T(4,128)(2,1)} async-done(((bf16[128,4,1024]{2,1,0:T(4,128)(2,1)}), bf16[128,4,1024]{2,1,0:T(4,128)(2,1)}, u32[]{:S(2)}, u32[]{:S(2)}) %all-to-all-start.3) | async-done | bytes 1048608 | tf_op jit(solution)/shard_map/all_to_all | solution.py:435
  210.3 1.6 combine.1
  211.9 16.0 %all_to_all.31.tiles_ref = bf16[32,4,640]{2,1,0:T(4,128)(2,1)S(1)} all-to-all(bf16[32,4,640]{2,1,0:T(4,128)(2,1)S(1)} %combine.1), channel_id=1, replica_groups=mesh['z'=16,'p'=8,'y'=4] {'p','y'}, dimensions={0} | all-to-all | bytes 327680 | tf_op jit(solution)/shard_map/all_to_all | solution.py:452
  228.0 0.8 join.1
  228.8 8.2 %all_to_all.32.back_ref = bf16[8,16,512]{2,1,0:T(8,128)(2,1)S(1)} all-to-all(bf16[8,16,512]{2,1,0:T(8,128)(2,1)S(1)} %join.1), channel_id=1, replica_groups=mesh['z'=16,'p'=8,'y'=4] {'p'}, dimensions={0} | all-to-all | bytes 262144 | tf_op jit(solution)/shard_map/all_to_all | solution.py:454
  237.0 0.6 finish.1
  (32 shorter events, 0.2 us)
Async XLA Ops:
  7.2 0.8 copy-start.7
  8.0 0.7 copy-start.8
  9.5 9.9 %all-to-all-start = ((bf16[4,2,8,1024]{3,2,1,0:T(8,128)(2,1)}), bf16[4,2,8,1024]{3,2,1,0:T(8,128)(2,1)S(1)}, u32[]{:S(2)}, u32[]{:S(2)}) async-start(bf16[4,2,8,1024]{3,2,1,0:T(8,128)(2,1)} %norm_pack.1), calls=%async_computation | async-start | bytes 262144 | tf_op jit(solution)/shard_map/all_to_all | solution.py:395
  20.9 74.5 %all-to-all-start.1 = ((bf16[128,4,1024]{2,1,0:T(4,128)(2,1)}), bf16[128,4,1024]{2,1,0:T(4,128)(2,1)}, u32[]{:S(2)}, u32[]{:S(2)}) async-start(bf16[128,4,1024]{2,1,0:T(4,128)(2,1)} %dispatch.1), calls=%async_computation.1 | async-start | bytes 2097152 | tf_op jit(solution)/shard_map/all_to_all | solution.py:421
  42.3 19.6 %copy-start = (bf16[1,192,4096]{2,1,0:T(8,128)(2,1)S(1)}, bf16[1,192,4096]{2,1,0:T(8,128)(2,1)}, u32[]{:S(2)}) copy-start(bf16[1,192,4096]{2,1,0:T(8,128)(2,1)} %refs_0_.5) | copy-start | bytes 4718596
  42.4 19.6 %copy-start.1 = (bf16[1,192,4096]{2,1,0:T(8,128)(2,1)S(1)}, bf16[1,192,4096]{2,1,0:T(8,128)(2,1)}, u32[]{:S(2)}) copy-start(bf16[1,192,4096]{2,1,0:T(8,128)(2,1)} %refs_1_.5) | copy-start | bytes 4718596
  42.4 120.8 %all-gather.3.cloned.1.call-start = ((), (), s32[]{:S(2)}) async-start(), calls=%async_computation.6 | async-start | bytes 3342336 | tf_op jit(solution)/shard_map/all_gather | solution.py:392
  42.4 48.7 %collective-permute-start.1 = (bf16[576,1024]{1,0:T(8,128)(2,1)}, bf16[576,1024]{1,0:T(8,128)(2,1)}, u32[]{:S(2)}, u32[]{:S(2)}) collective-permute-start(bf16[576,1024]{1,0:T(8,128)(2,1)} %get-tuple-element.24), channel_id=1, source_target_pairs={{0,2},{1,3},{2,0},{3,1},{4,6},{5,7},{6,4},{7,5},{8,10},{9,11},{10,... | collective-permute-start | bytes 3538952 | tf_op jit(solution)/shard_map/ppermute | solution.py:24
  46.7 44.4 %collective-permute-start = (bf16[384,1024]{1,0:T(8,128)(2,1)}, bf16[384,1024]{1,0:T(8,128)(2,1)}, u32[]{:S(2)}, u32[]{:S(2)}) collective-permute-start(bf16[384,1024]{1,0:T(8,128)(2,1)} %get-tuple-element.23), channel_id=1, source_target_pairs={{0,1},{1,2},{2,3},{3,0},{4,5},{5,6},{6,7},{7,4},{8,9},{9,10},{10,1... | collective-permute-start | bytes 2359304 | tf_op jit(solution)/shard_map/ppermute | solution.py:24
  48.9 42.2 %collective-permute-start.2 = (bf16[384,1024]{1,0:T(8,128)(2,1)}, bf16[384,1024]{1,0:T(8,128)(2,1)}, u32[]{:S(2)}, u32[]{:S(2)}) collective-permute-start(bf16[384,1024]{1,0:T(8,128)(2,1)} %get-tuple-element.25), channel_id=1, source_target_pairs={{0,3},{1,0},{2,1},{3,2},{4,7},{5,4},{6,5},{7,6},{8,11},{9,8},{10,9... | collective-permute-start | bytes 2359304 | tf_op jit(solution)/shard_map/ppermute | solution.py:24
  55.4 45.1 %collective-permute-start.3 = (bf16[192,1024]{1,0:T(8,128)(2,1)}, bf16[192,1024]{1,0:T(8,128)(2,1)}, u32[]{:S(2)}, u32[]{:S(2)}) collective-permute-start(bf16[192,1024]{1,0:T(8,128)(2,1)} %get-tuple-element.26), channel_id=1, source_target_pairs={{0,1},{1,2},{2,3},{3,0},{4,5},{5,6},{6,7},{7,4},{8,9},{9,10},{10,1... | collective-permute-start | bytes 1179656 | tf_op jit(solution)/shard_map/ppermute | solution.py:24
  57.3 43.2 %collective-permute-start.4 = (bf16[192,1024]{1,0:T(8,128)(2,1)}, bf16[192,1024]{1,0:T(8,128)(2,1)}, u32[]{:S(2)}, u32[]{:S(2)}) collective-permute-start(bf16[192,1024]{1,0:T(8,128)(2,1)} %get-tuple-element.27), channel_id=1, source_target_pairs={{0,3},{1,0},{2,1},{3,2},{4,7},{5,4},{6,5},{7,6},{8,11},{9,8},{10,9... | collective-permute-start | bytes 1179656 | tf_op jit(solution)/shard_map/ppermute | solution.py:24
  61.9 1.4 copy-start.2
  63.5 1.0 copy-start.3
  95.4 1.3 copy-start.4
  119.6 13.1 %copy-start.5 = (bf16[576,1024]{1,0:T(8,128)(2,1)S(1)}, bf16[576,1024]{1,0:T(8,128)(2,1)}, u32[]{:S(2)}) copy-start(bf16[576,1024]{1,0:T(8,128)(2,1)} %copy-done.3) | copy-start | bytes 3538948
  136.2 22.6 %copy-start.9 = (s32[4]{0:T(128)S(1)}, s32[4]{0:T(128)}, u32[]{:S(2)}) copy-start(s32[4]{0:T(128)} %node_ref.1) | copy-start | bytes 52
  136.2 26.5 %copy-start.10 = (f32[32,8]{0,1:T(8,128)S(1)}, f32[32,8]{0,1:T(8,128)}, u32[]{:S(2)}) copy-start(f32[32,8]{0,1:T(8,128)} %param.14) | copy-start | bytes 3076
  136.2 74.1 %all-to-all-start.3 = ((bf16[128,4,1024]{2,1,0:T(4,128)(2,1)}), bf16[128,4,1024]{2,1,0:T(4,128)(2,1)}, u32[]{:S(2)}, u32[]{:S(2)}) async-start(bf16[128,4,1024]{2,1,0:T(4,128)(2,1)} %down.1), calls=%async_computation.3 | async-start | bytes 2097152 | tf_op jit(solution)/shard_map/all_to_all | solution.py:435
  163.2 1.9 copy-start.6
Sparse Core Ops, SparseCore 0:
  62.0 75.7 all-gather.2
